TPU v7x, 32 devices: a whole 2x2x4 slice. The times are simulated.
32 devices in a mesh: ao: 8 (over y, x, core), aux: 4 (over z).
Axes of the slice: x: 2, y: 2, z: 4, core: 2. Of those that a mesh axis runs over, the one named last changes fastest.
Arguments:
- factors: bfloat16 [16, 32, 256, 512], P('ao', 'aux'), may hold values from -0.8984375 to 0.8984375
- pair_cols: int32 [16, 3], P('ao'), may hold values from 0 to 15, as said below
- pair_count: int32 [16], P('ao'), may hold values from 1 to 3, as said below
Outputs:
- ex_blocks: float32 [16, 3, 256, 256], P('ao', None, 'aux')
Inputs may be any that keep to these rules, and one draw needn't show every extreme that they name: pair_cols[a, s] = (a + t) mod 16 with 0 <= t < 7, the offsets t of one row all distinct; so every unordered pair of blocks stands at most once in the table. Slots at or beyond pair_count of a row are not live; some row is full.
All inputs are finite; a program needn't handle non-finite values.
Results may differ from a plain program's by a relative error of at most 0.0003.
Values may be sent and summed in bfloat16 or wider, within the bound.
No kernel may reach another device: no remote copies, remote signals or barrier semaphores. Data moves between devices by JAX's collectives and lax.ppermute only.
A program may use at most 320 MiB of HBM per device.

v0:
```python
import jax
import jax.numpy as jnp
from jax import lax
from jax.sharding import PartitionSpec as P


def from_behind(value, axis, steps):
    count = lax.axis_size(axis)
    pairs = [(source, (source + steps) % count) for source in range(count)]
    return lax.ppermute(value, axis, pairs)


def body(factors, pair_cols, pair_count):
    blocks_dev = factors.shape[0]
    slot_total = pair_cols.shape[1]
    devices = lax.axis_size("ao")

    def advance(carry, unused):
        arrived = from_behind(carry, "ao", -1)
        return (arrived, arrived)

    last_block, received = lax.scan(advance, factors, None, length=devices // 2 - 1)
    resident = jnp.concatenate([factors, received.reshape((-1,) + factors.shape[1:])], axis=0)
    offset = lax.axis_index("ao") * blocks_dev
    slot_index = jnp.mod(pair_cols - offset, devices * blocks_dev)
    columns = jnp.take(resident, slot_index.reshape(-1), axis=0)
    columns = columns.reshape((blocks_dev, slot_total) + factors.shape[1:])
    partial_value = jnp.einsum(
        "apri,aspci->asrc", factors, columns, preferred_element_type=jnp.float32
    )
    active = lax.broadcasted_iota(jnp.int32, (blocks_dev, slot_total), 1) < pair_count[:, None]
    partial_value = jnp.where(active[:, :, None, None], partial_value, 0.0)
    return lax.psum_scatter(partial_value, "aux", scatter_dimension=2, tiled=True)


def solution(mesh):
    return jax.shard_map(
        body,
        mesh=mesh,
        in_specs=(P("ao", "aux", None, None), P("ao", None), P("ao")),
        out_specs=P("ao", None, "aux", None),
        check_vma=False,
    )
```

profile of v0, /device:TPU:0, one launch (start us, length us, event | category | flops | bytes accessed | tf_op | source)
XLA Modules:
  0.0 314.7 jit_solution(9576830380725689063)
XLA Ops:
  6.5 0.0 all-reduce.3.cloned.1.call-start
  6.5 4.5 %copy.11 = bf16[2,8,256,512]{3,2,1,0:T(8,128)(2,1)} copy(bf16[2,8,256,512]{3,2,1,0:T(8,128)(2,1)} %param.5) | data formatting | bytes 8388608
  11.0 175.0 %while.12 = (s32[]{:T(128)}, bf16[2,8,256,512]{3,2,1,0:T(8,128)(2,1)}, bf16[3,2,8,256,512]{4,3,2,1,0:T(8,128)(2,1)}, s32[]{:T(128)}) while((s32[]{:T(128)}, bf16[2,8,256,512]{3,2,1,0:T(8,128)(2,1)}, bf16[3,2,8,256,512]{4,3,2,1,0:T(8,128)(2,1)}, s32[]{:T(128)}) %tuple.21), condition=%wide.region_1.2_spmd, body=%wide.region_0.1_spmd.sunk | while | flops 2 | bytes 33554536 | solution.py:22
  11.0 3.3 %collective-permute-start = (bf16[2,8,256,512]{3,2,1,0:T(8,128)(2,1)}, bf16[2,8,256,512]{3,2,1,0:T(8,128)(2,1)}, u32[]{:S(2)}, u32[]{:S(2)}) collective-permute-start(bf16[2,8,256,512]{3,2,1,0:T(8,128)(2,1)} %get-tuple-element.58), channel_id=1, source_target_pairs={{0,28},{4,0},{8,4},{12,8},{16,12},{20,16},{24,20},{28,24},{1,29},{... | collective-permute-start | bytes 12582920 | tf_op jit(solution)/shard_map/while/body/eval_jaxpr/ppermute | solution.py:10
  14.4 46.3 %collective-permute-done = bf16[2,8,256,512]{3,2,1,0:T(8,128)(2,1)} collective-permute-done((bf16[2,8,256,512]{3,2,1,0:T(8,128)(2,1)}, bf16[2,8,256,512]{3,2,1,0:T(8,128)(2,1)}, u32[]{:S(2)}, u32[]{:S(2)}) %collective-permute-start) | collective-permute-done | bytes 4194336 | tf_op jit(solution)/shard_map/while/body/eval_jaxpr/ppermute | solution.py:10
  60.7 4.5 %copy.17 = bf16[2,8,256,512]{3,2,1,0:T(8,128)(2,1)} copy(bf16[2,8,256,512]{3,2,1,0:T(8,128)(2,1)} %collective-permute-done) | data formatting | bytes 8388608 | tf_op jit(solution)/shard_map/while
  65.2 4.5 %bitcast_dynamic-update-slice_fusion.2 = bf16[3,2,8,256,512]{4,3,2,1,0:T(8,128)(2,1)} fusion(bf16[3,2,8,256,512]{4,3,2,1,0:T(8,128)(2,1)} %get-tuple-element.59, s32[]{:T(128)S(6)} %copy.13, bf16[2,8,256,512]{3,2,1,0:T(8,128)(2,1)} %collective-permute-done), kind=kLoop, calls=%fused_computation.2.clone.1 | loop fusion | bytes 8388612 | tf_op jit(solution)/shard_map/while/body/jit(dynamic_update_index_in_dim)/dynamic_update_slice | solution.py:22
  69.7 2.8 collective-permute-start
  72.5 46.3 %collective-permute-done = bf16[2,8,256,512]{3,2,1,0:T(8,128)(2,1)} collective-permute-done((bf16[2,8,256,512]{3,2,1,0:T(8,128)(2,1)}, bf16[2,8,256,512]{3,2,1,0:T(8,128)(2,1)}, u32[]{:S(2)}, u32[]{:S(2)}) %collective-permute-start) | collective-permute-done | bytes 4194336 | tf_op jit(solution)/shard_map/while/body/eval_jaxpr/ppermute | solution.py:10
  118.8 4.5 %copy.17 = bf16[2,8,256,512]{3,2,1,0:T(8,128)(2,1)} copy(bf16[2,8,256,512]{3,2,1,0:T(8,128)(2,1)} %collective-permute-done) | data formatting | bytes 8388608 | tf_op jit(solution)/shard_map/while
  123.3 4.5 %bitcast_dynamic-update-slice_fusion.2 = bf16[3,2,8,256,512]{4,3,2,1,0:T(8,128)(2,1)} fusion(bf16[3,2,8,256,512]{4,3,2,1,0:T(8,128)(2,1)} %get-tuple-element.59, s32[]{:T(128)S(6)} %copy.13, bf16[2,8,256,512]{3,2,1,0:T(8,128)(2,1)} %collective-permute-done), kind=kLoop, calls=%fused_computation.2.clone.1 | loop fusion | bytes 8388612 | tf_op jit(solution)/shard_map/while/body/jit(dynamic_update_index_in_dim)/dynamic_update_slice | solution.py:22
  127.9 2.8 collective-permute-start
  130.7 46.3 %collective-permute-done = bf16[2,8,256,512]{3,2,1,0:T(8,128)(2,1)} collective-permute-done((bf16[2,8,256,512]{3,2,1,0:T(8,128)(2,1)}, bf16[2,8,256,512]{3,2,1,0:T(8,128)(2,1)}, u32[]{:S(2)}, u32[]{:S(2)}) %collective-permute-start) | collective-permute-done | bytes 4194336 | tf_op jit(solution)/shard_map/while/body/eval_jaxpr/ppermute | solution.py:10
  177.0 4.5 %copy.17 = bf16[2,8,256,512]{3,2,1,0:T(8,128)(2,1)} copy(bf16[2,8,256,512]{3,2,1,0:T(8,128)(2,1)} %collective-permute-done) | data formatting | bytes 8388608 | tf_op jit(solution)/shard_map/while
  181.5 4.5 %bitcast_dynamic-update-slice_fusion.2 = bf16[3,2,8,256,512]{4,3,2,1,0:T(8,128)(2,1)} fusion(bf16[3,2,8,256,512]{4,3,2,1,0:T(8,128)(2,1)} %get-tuple-element.59, s32[]{:T(128)S(6)} %copy.13, bf16[2,8,256,512]{3,2,1,0:T(8,128)(2,1)} %collective-permute-done), kind=kLoop, calls=%fused_computation.2.clone.1 | loop fusion | bytes 8388612 | tf_op jit(solution)/shard_map/while/body/jit(dynamic_update_index_in_dim)/dynamic_update_slice | solution.py:22
  186.0 11.7 %fusion.3 = (bf16[8,8,256,256]{3,2,1,0:T(8,128)(2,1)}, bf16[8,8,256,256]{3,2,1,0:T(8,128)(2,1)}) fusion(bf16[2,8,256,512]{3,2,1,0:T(8,128)(2,1)} %param.5, bf16[6,8,256,512]{3,2,1,0:T(8,128)(2,1)} %bitcast.24), kind=kLoop, calls=%fused_computation.9 | loop fusion | flops 33554432 | bytes 33554432 | tf_op jit(solution)/shard_map/concatenate | solution.py:23
  197.8 0.0 copy-done.1
  197.8 0.0 copy-done.2
  197.8 0.1 compare_and_fusion
  197.9 0.1 reshape.63
  198.0 7.5 %gather_fusion.1 = bf16[6,8,256,256]{3,2,1,0:T(8,128)(2,1)} fusion(bf16[8,8,256,256]{3,2,1,0:T(8,128)(2,1)} %get-tuple-element.32, s32[1024]{0:T(1024)S(1)} %pad_clamp_fusion), kind=kCustom, calls=%fused_computation.1 | custom fusion | bytes 12582936 | tf_op jit(solution)/shard_map/jit(_take)/gather | solution.py:26
  205.5 7.5 %gather_fusion = bf16[6,8,256,256]{3,2,1,0:T(8,128)(2,1)} fusion(bf16[8,8,256,256]{3,2,1,0:T(8,128)(2,1)} %get-tuple-element.31, s32[1024]{0:T(1024)S(1)} %pad_clamp_fusion), kind=kCustom, calls=%fused_computation | custom fusion | bytes 12582936 | tf_op jit(solution)/shard_map/jit(_take)/gather | solution.py:26
  212.9 10.6 %pad_maximum_fusion = bf16[6,8,256,512]{3,2,1,0:T(8,128)(2,1)} fusion(bf16[6,8,256,256]{3,2,1,0:T(8,128)(2,1)} %gather_fusion.1, bf16[6,8,256,256]{3,2,1,0:T(8,128)(2,1)} %gather_fusion), kind=kLoop, calls=%fused_computation.5 | loop fusion | flops 25165824 | bytes 25165824
  223.5 0.0 copy-done
  223.5 7.8 %fusion.6 = f32[2,3,256,256]{2,3,1,0:T(8,128)} fusion(bf16[2,8,256,512]{3,2,1,0:T(8,128)(2,1)S(1)} %copy-done, bf16[2,3,8,256,512]{4,3,2,1,0:T(8,128)(2,1)} %bitcast.23, pred[2,3]{1,0:T(4,128)(4,1)S(1)} %get-tuple-element.29, pred[2,3]{1,0:T(4,128)(4,1)S(1)} %get-tuple-element.33), kind=kOutput, calls=%fused_computation.14 | convolution fusion | flops 3227910144 | bytes 18350092 | tf_op jit(solution)/shard_map/apri,aspci->asrc/dot_general | solution.py:28
  231.3 3.7 %copy.5 = f32[2,3,256,256]{3,0,1,2:T(2,128)} copy(f32[2,3,256,256]{2,3,1,0:T(8,128)} %fusion.6) | data formatting | bytes 3145728 | tf_op jit(solution)/shard_map/jit(_where)/select_n | solution.py:32
  235.1 0.0 all-reduce.3.cloned.1.call-update
  235.1 0.0 copy-done.3
  235.1 0.6 dynamic-slice
  236.3 69.7 %all-reduce.3.cloned.1.call-done = f32[2,3,256,256]{3,0,1,2:T(2,128)} async-done(((f32[2,3,256,256]{3,0,1,2:T(2,128)}), f32[2,3,256,256]{3,0,1,2:T(2,128)}) %all-reduce.3.cloned.1.call-update) | async-done | bytes 1572880
  306.0 1.1 constant_dynamic-slice_fusion
  307.1 0.8 copy.6
  (7 shorter events, 0.0 us)
Async XLA Ops:
  6.5 299.5 %all-reduce.3.cloned.1.call-start = ((), (), s32[]{:S(2)}) async-start(), calls=%async_computation | async-start | bytes 3145728
  11.0 49.7 %collective-permute-start = (bf16[2,8,256,512]{3,2,1,0:T(8,128)(2,1)}, bf16[2,8,256,512]{3,2,1,0:T(8,128)(2,1)}, u32[]{:S(2)}, u32[]{:S(2)}) collective-permute-start(bf16[2,8,256,512]{3,2,1,0:T(8,128)(2,1)} %get-tuple-element.58), channel_id=1, source_target_pairs={{0,28},{4,0},{8,4},{12,8},{16,12},{20,16},{24,20},{28,24},{1,29},{... | collective-permute-start | bytes 12582920 | tf_op jit(solution)/shard_map/while/body/eval_jaxpr/ppermute | solution.py:10
  69.7 49.1 %collective-permute-start = (bf16[2,8,256,512]{3,2,1,0:T(8,128)(2,1)}, bf16[2,8,256,512]{3,2,1,0:T(8,128)(2,1)}, u32[]{:S(2)}, u32[]{:S(2)}) collective-permute-start(bf16[2,8,256,512]{3,2,1,0:T(8,128)(2,1)} %get-tuple-element.58), channel_id=1, source_target_pairs={{0,28},{4,0},{8,4},{12,8},{16,12},{20,16},{24,20},{28,24},{1,29},{... | collective-permute-start | bytes 12582920 | tf_op jit(solution)/shard_map/while/body/eval_jaxpr/ppermute | solution.py:10
  127.9 49.1 %collective-permute-start = (bf16[2,8,256,512]{3,2,1,0:T(8,128)(2,1)}, bf16[2,8,256,512]{3,2,1,0:T(8,128)(2,1)}, u32[]{:S(2)}, u32[]{:S(2)}) collective-permute-start(bf16[2,8,256,512]{3,2,1,0:T(8,128)(2,1)} %get-tuple-element.58), channel_id=1, source_target_pairs={{0,28},{4,0},{8,4},{12,8},{16,12},{20,16},{24,20},{28,24},{1,29},{... | collective-permute-start | bytes 12582920 | tf_op jit(solution)/shard_map/while/body/eval_jaxpr/ppermute | solution.py:10
  186.0 11.8 %copy-start.1 = (s32[2,3]{1,0:T(2,128)S(1)}, s32[2,3]{1,0:T(2,128)}, u32[]{:S(2)}) copy-start(s32[2,3]{1,0:T(2,128)} %param.6) | copy-start | bytes 76
  186.0 11.8 %copy-start.2 = (s32[2]{0:T(128)S(1)}, s32[2]{0:T(128)}, u32[]{:S(2)}) copy-start(s32[2]{0:T(128)} %param.7) | copy-start | bytes 28
  212.9 10.6 %copy-start = (bf16[2,8,256,512]{3,2,1,0:T(8,128)(2,1)S(1)}, bf16[2,8,256,512]{3,2,1,0:T(8,128)(2,1)}, u32[]{:S(2)}) copy-start(bf16[2,8,256,512]{3,2,1,0:T(8,128)(2,1)} %param.5) | copy-start | bytes 12582916
  223.5 11.6 %copy-start.3 = (u32[32]{0:T(128)S(1)}, u32[32]{0:T(128)}, u32[]{:S(2)}) copy-start(u32[32]{0:T(128)} %constant.55) | copy-start | bytes 388
Sparse Core Ops, SparseCore 0:
  235.2 70.7 all-reduce.2
where the time goes:
time: 315 us
  waiting for transfers between devices  209 us (66%)
  local copies, waits for them, and re-layouts  52.7 us (17%)
  other arithmetic  22.4 us (7%)
  between operations  14.1 us (4%)
  starting transfers between devices  8.95 us (3%)
  matrix products  7.81 us (2%)
    ppermute x3, waiting for transfers between devices, from_behind(): return lax.ppermute(value, axis, pairs)  139 us
    unnamed x2, waiting for transfers between devices  69.7 us
    gather x2, local copies, waits for them, and re-layouts, body(): columns = jnp.take(resident, slot_index.reshape(-1), axis=0)  15 us
    dynamic_update_slice x3, local copies, waits for them, and re-layouts, body(): lax.scan(advance, factors, None, length=devices // 2 - 1)  13.5 us
    while x3, local copies, waits for them, and re-layouts  13.5 us
    concatenate x1, other arithmetic, body(): jnp.concatenate([factors, received.reshape((-1,) + factors.shape[1:])], a...  11.7 us
    unnamed x1, other arithmetic  10.6 us
    ppermute x3, starting transfers between devices, from_behind(): return lax.ppermute(value, axis, pairs)  8.95 us
  transfers between devices with their start and end apart: 4, of which 4 were waited for; matrix products, arithmetic and copies ran while one was open for 0% of the time, Pallas kernels for 0%

commit v1 on v0

--- a/solution.py
+++ b/solution.py
@@ -1,7 +1,236 @@
+import functools
+
 import jax
 import jax.numpy as jnp
 from jax import lax
+from jax.experimental import pallas as pl
+from jax.experimental.pallas import tpu as pltpu
 from jax.sharding import PartitionSpec as P
+
+LANES = 128
+PIECES = ((0, 96), (96, 96), (192, 64))
+GROUPS = 4
+KERNEL_BYTES = 14 << 20
+
+
+def pack_kernel(pieces, which, *refs):
+    sources, outs, sems = refs[: -len(pieces) - 1], refs[-len(pieces) - 1 : -1], refs[-1]
+    blocks = outs[0].shape[0]
+    copies = [(turn, block) for turn in range(len(pieces)) for block in range(blocks)]
+
+    def copy(source, turn, block):
+        first, wide = pieces[turn]
+        return pltpu.make_async_copy(
+            source.at[block, :, pl.ds(first, wide)], outs[turn].at[block], sems.at[turn, block]
+        )
+
+    for index, source in enumerate(sources):
+
+        @pl.when(which[0] == index)
+        def start(source=source):
+            for turn, block in copies:
+                copy(source, turn, block).start()
+
+    @pl.when(which[0] < len(sources))
+    def wait():
+        for turn, block in copies:
+            copy(sources[0], turn, block).wait()
+
+
+def in_hbm(value):
+    return pltpu.with_memory_space_constraint(value, pltpu.HBM)
+
+
+def pack(which, sources, pieces):
+    blocks, depth, _, inner = sources[0].shape
+    shapes = [jax.ShapeDtypeStruct((blocks, depth, wide, inner), sources[0].dtype) for _, wide in pieces]
+    return pl.pallas_call(
+        functools.partial(pack_kernel, pieces),
+        in_specs=[pl.BlockSpec(memory_space=pltpu.SMEM)] + [pl.BlockSpec(memory_space=pl.ANY)] * len(sources),
+        out_specs=[pl.BlockSpec(memory_space=pltpu.VMEM)] * len(pieces),
+        scratch_shapes=[pltpu.SemaphoreType.DMA((len(pieces), blocks))],
+        out_shape=shapes,
+        compiler_params=pltpu.CompilerParams(vmem_limit_bytes=KERNEL_BYTES),
+        cost_estimate=pl.CostEstimate(flops=0, bytes_accessed=1 << 20, transcendentals=0),
+        name="pack_ranges",
+    )(which, *sources)
+
+
+def pair_kernel(slots, first, wide, parts, places, unread, rows_hbm, *refs):
+    *refs, rows, held, total, row_sems, column_sems = refs
+    sources, outs = refs[:-parts], refs[-parts:]
+    blocks, depth, height, inner = rows.shape
+    count = blocks * slots
+    group = depth // GROUPS
+
+    def row_copy(g):
+        part = pl.ds(g * group, group)
+        return pltpu.make_async_copy(rows_hbm.at[:, part], rows.at[:, part], row_sems.at[g])
+
+    def column_copy(source, slot, g):
+        part = pl.ds(g * group, group)
+        start = first if source.shape[2] == height else 0
+        return pltpu.make_async_copy(
+            source.at[places[count + slot], part, pl.ds(start, wide)],
+            held.at[slot // slots, part, pl.ds(slot % slots * wide, wide)],
+            column_sems.at[slot, g],
+        )
+
+    for g in range(GROUPS):
+        row_copy(g).start()
+        for slot in range(count):
+            for index, source in enumerate(sources):
+
+                @pl.when(places[slot] == index)
+                def fetch(source=source, slot=slot, g=g):
+                    column_copy(source, slot, g).start()
+
+    for g in range(GROUPS):
+        row_copy(g).wait()
+        for slot in range(count):
+
+            @pl.when(places[slot] >= 0)
+            def arrived(slot=slot, g=g):
+                column_copy(sources[-1], slot, g).wait()
+
+        for row in range(blocks):
+            product = 0.0 if g == 0 else total[row]
+            for p in range(g * group, (g + 1) * group):
+                product += lax.dot_general(
+                    held[row, p],
+                    rows[row, p],
+                    (((1,), (1,)), ((), ())),
+                    preferred_element_type=jnp.float32,
+                )
+            total[row] = product
+
+    parts = len(outs)
+    lanes = outs[0].shape[2]
+    span = height // parts
+    fold = lanes // span
+    for slot in range(count):
+        start = slot % slots * wide
+        block = jnp.where(places[slot] >= 0, total[slot // slots, start : start + wide], 0.0)
+        left = slot % fold * span
+        for mine in range(parts):
+
+            @pl.when(places[2 * count] == mine)
+            def write(slot=slot, block=block, left=left, mine=mine):
+                for step, out in enumerate(outs):
+                    part = (mine + step) % parts
+                    out[slot // fold, :, left : left + span] = block[:, part * span : (part + 1) * span]
+
+
+def pair_products(places, begun, rows, columns, piece, parts, slots):
+    first, wide = piece
+    blocks, depth, height, inner = rows.shape
+    count = blocks * slots
+    fold = LANES * parts // height if count % (LANES * parts // height) == 0 else 1
+    shape = (count // fold, wide, height // parts * fold)
+    return pl.pallas_call(
+        functools.partial(pair_kernel, slots, first, wide, parts),
+        in_specs=[pl.BlockSpec(memory_space=pltpu.SMEM)] + [pl.BlockSpec(memory_space=pl.ANY)]
+        + [pl.BlockSpec(memory_space=pl.ANY)] * (1 + len(columns)),
+        out_specs=[pl.BlockSpec(memory_space=pltpu.VMEM)] * parts,
+        scratch_shapes=[
+            pltpu.VMEM(rows.shape, rows.dtype),
+            pltpu.VMEM((blocks, depth, slots * wide, inner), rows.dtype),
+            pltpu.VMEM((blocks, slots * wide, height), jnp.float32),
+            pltpu.SemaphoreType.DMA((GROUPS,)),
+            pltpu.SemaphoreType.DMA((count, GROUPS)),
+        ],
+        out_shape=[jax.ShapeDtypeStruct(shape, jnp.float32)] * parts,
+        compiler_params=pltpu.CompilerParams(vmem_limit_bytes=KERNEL_BYTES),
+        cost_estimate=pl.CostEstimate(flops=0, bytes_accessed=1 << 20, transcendentals=0),
+        name="pair_products",
+    )(places, begun, *(in_hbm(a) if a.shape == rows.shape else a for a in (rows, *columns)))
+
+
+def sum_kernel(parts, *refs):
+    *terms, out = refs
+    pairs, _, lanes = terms[0].shape
+    span = out.shape[1]
+    for pair in range(pairs):
+        sums = [sum(term[pair] for term in terms[k : k + parts]) for k in range(0, len(terms), parts)]
+        turned = jnp.concatenate(sums, axis=0).T
+        for side in range(lanes // span):
+            out[pair * (lanes // span) + side] = turned[side * span : (side + 1) * span]
+
+
+def mark_kernel(value, out):
+    out[...] = jnp.zeros_like(out)
+
+
+def mark(value):
+    return pl.pallas_call(
+        mark_kernel,
+        in_specs=[pl.BlockSpec(memory_space=pl.ANY)],
+        out_specs=pl.BlockSpec(memory_space=pltpu.VMEM),
+        out_shape=jax.ShapeDtypeStruct((8, LANES), jnp.float32),
+        compiler_params=pltpu.CompilerParams(vmem_limit_bytes=1 << 20),
+        cost_estimate=pl.CostEstimate(flops=10**12, bytes_accessed=10**9, transcendentals=0),
+        name="mark",
+    )(value)
+
+
+def squares(factors, pair_cols, pair_count):
+    blocks, _, height, _ = factors.shape
+    slots = pair_cols.shape[1]
+    devices = lax.axis_size("ao")
+    parts = lax.axis_size("aux")
+    chips = devices // 2
+    me = lax.axis_index("ao")
+    core = lax.rem(me, 2)
+    even = lax.rem(me, 4) < 2
+
+    swap = [(d, d ^ 1) for d in range(devices)]
+    to_core_1 = [(2 * c, 2 * c + 1) for c in range(chips)]
+    early, late = [], []
+    for c in range(0, chips, 2):
+        across = (c + 2) % chips
+        early += [(2 * across, 2 * c), (2 * c + 3, 2 * c + 1), (2 * across + 1, 2 * c + 3)]
+        late += [(2 * c, 2 * c + 2), (2 * c + 2, 2 * c), (2 * across + 3, 2 * c + 3)]
+
+    relative = jnp.mod(pair_cols - me * blocks, devices * blocks)
+    slab = relative // blocks
+    first_core = jnp.where(slab == 2, 4, jnp.where(slab == 3, 3, slab))
+    second_core = jnp.where(slab == 1, 5, jnp.where(slab == 2, 2, jnp.where(even, 3, 4)))
+    source = jnp.where((core == 0) | (slab == 0), first_core, second_core)
+    live = lax.broadcasted_iota(jnp.int32, (blocks, slots), 1) < pair_count[:, None]
+    places = jnp.concatenate([jnp.where(live, source, -1).reshape(-1), lax.rem(relative, blocks).reshape(-1)])
+    places = jnp.concatenate([places, lax.axis_index("aux").astype(jnp.int32).reshape(1)])
+    which = jnp.where(even, 3 * core, 1 + core).astype(jnp.int32).reshape(1)
+
+    one = lax.ppermute(factors, "ao", early)
+    mate = lax.ppermute(factors, "ao", swap)
+    one_mate = lax.ppermute(one, "ao", swap)
+    senders = [one, in_hbm(factors), mate]
+    sent = pack(which, senders, PIECES[:1])
+    sent += pack(after(which, places, *sent), senders, PIECES[1:])
+    twos, made, terms, marks = [], [], [], [mark(sent[-1])]
+    for turn, piece in enumerate(PIECES):
+        twos.append(lax.ppermute(after(sent[turn], *made[: max(turn - 1, 0)][-1:]), "ao", late))
+        earlier = terms[1 - parts :] if turn == 1 else []
+        two_mate = lax.ppermute(after(twos[turn], marks[turn], *earlier), "ao", to_core_1)
+        columns = [factors, mate, one, one_mate, twos[turn], two_mate]
+        products = pair_products(places, marks[turn], factors, columns, piece, parts, slots)
+        made.append(products[0])
+        if turn + 1 < len(PIECES):
+            marks.append(mark(products[0]))
+        terms.append(products[0])
+        for step in range(1, parts):
+            terms.append(lax.ppermute(products[step], "aux", [(z, (z + step) % parts) for z in range(parts)]))
+    out = pl.pallas_call(
+        functools.partial(sum_kernel, parts),
+        out_shape=jax.ShapeDtypeStruct((blocks * slots, height // parts, height), jnp.float32),
+        compiler_params=pltpu.CompilerParams(vmem_limit_bytes=KERNEL_BYTES),
+        name="sum_terms",
+    )(*terms)
+    return out.reshape(blocks, slots, height // parts, height)
+
+
+def after(value, *others):
+    return lax.optimization_barrier((value, *others))[0]
 
 
 def from_behind(value, axis, steps):
@@ -10,7 +239,7 @@
     return lax.ppermute(value, axis, pairs)
 
 
-def body(factors, pair_cols, pair_count):
+def ring(factors, pair_cols, pair_count):
     blocks_dev = factors.shape[0]
     slot_total = pair_cols.shape[1]
     devices = lax.axis_size("ao")
@@ -35,7 +264,7 @@
 
 def solution(mesh):
     return jax.shard_map(
-        body,
+        squares if mesh.shape["ao"] == 8 else ring,
         mesh=mesh,
         in_specs=(P("ao", "aux", None, None), P("ao", None), P("ao")),
         out_specs=P("ao", None, "aux", None),

time: 315 us -> 147 us (0.47)
  the two profiles are of different devices: /device:TPU:0 before, /device:TPU:11 now
where the time goes in v1:
time: 147 us; the launch traced here: 148 us
  waiting for transfers between devices  97.2 us (66%)
  starting transfers between devices  25.6 us (17%)
  Pallas kernels  23.7 us (16%)
    ppermute x1, waiting for transfers between devices, squares(): one = lax.ppermute(factors, 'ao', early)  43.3 us
    ppermute x3, waiting for transfers between devices, squares(): lax.ppermute(after(sent[turn], *made[:max(turn - 1, 0)][-1:]), 'ao', late)  29.7 us
    ppermute x9, waiting for transfers between devices, squares(): lax.ppermute(products[step], 'aux', [(z, (z + step) % parts) for z in ran...  17.2 us
    pallas_call x3, Pallas kernels, pair_products(): pl.pallas_call(functools.partial(pair_kernel, slots, first, wide, parts),...  15.9 us
    ppermute x3, starting transfers between devices, squares(): lax.ppermute(after(sent[turn], *made[:max(turn - 1, 0)][-1:]), 'ao', late)  9.85 us
    ppermute x9, starting transfers between devices, squares(): lax.ppermute(products[step], 'aux', [(z, (z + step) % parts) for z in ran...  8.97 us
    pallas_call x2, Pallas kernels, pack(): pl.pallas_call(functools.partial(pack_kernel, pieces), in_specs=[pl.Block...  5.79 us
    ppermute x1, waiting for transfers between devices, squares(): mate = lax.ppermute(factors, 'ao', swap)  3.93 us
  transfers between devices with their start and end apart: 18, of which 13 were waited for; matrix products, arithmetic and copies ran while one was open for 1% of the time, Pallas kernels for 13%

profile of v1, /device:TPU:11, one launch (start us, length us, event | category | flops | bytes accessed | tf_op | source)
XLA Modules:
  0.0 147.7 jit_solution(12204405196570567929)
XLA Ops:
  0.0 0.7 collective-permute-start.1
  0.7 2.2 %collective-permute-start = (bf16[2,8,256,512]{3,2,1,0:T(8,128)(2,1)}, bf16[2,8,256,512]{3,2,1,0:T(8,128)(2,1)}, u32[]{:S(2)}, u32[]{:S(2)}) collective-permute-start(bf16[2,8,256,512]{3,2,1,0:T(8,128)(2,1)} %refs_0_.5), channel_id=1, source_target_pairs={{16,0},{12,4},{20,12},{0,16},{28,20},{4,28},{17,1},{13,5},{21,13},... | collective-permute-start | bytes 12582920 | tf_op jit(solution)/shard_map/ppermute | solution.py:204
  2.9 0.8 compare_select_fusion.4
  3.9 3.9 %collective-permute-done.1.refs_2_.refs_1_ = bf16[2,8,256,512]{3,2,1,0:T(8,128)(2,1)} collective-permute-done((bf16[2,8,256,512]{3,2,1,0:T(8,128)(2,1)}, bf16[2,8,256,512]{3,2,1,0:T(8,128)(2,1)}, u32[]{:S(2)}, u32[]{:S(2)}) %collective-permute-start.1) | collective-permute-done | bytes 4194336 | tf_op jit(solution)/shard_map/ppermute | solution.py:205
  7.8 43.3 %collective-permute-done.refs_0_.refs_2_ = bf16[2,8,256,512]{3,2,1,0:T(8,128)(2,1)} collective-permute-done((bf16[2,8,256,512]{3,2,1,0:T(8,128)(2,1)}, bf16[2,8,256,512]{3,2,1,0:T(8,128)(2,1)}, u32[]{:S(2)}, u32[]{:S(2)}) %collective-permute-start) | collective-permute-done | bytes 4194336 | tf_op jit(solution)/shard_map/ppermute | solution.py:204
  51.1 2.5 %pack_ranges.2 = bf16[2,8,96,512]{3,2,1,0:T(8,128)(2,1)} custom-call(s32[1]{0:T(128)} %bitcast.1.which, bf16[2,8,256,512]{3,2,1,0:T(8,128)(2,1)} %collective-permute-done.refs_0_.refs_2_, bf16[2,8,256,512]{3,2,1,0:T(8,128)(2,1)} %refs_0_.5, bf16[2,8,256,512]{3,2,1,0:T(8,128)(2,1)} %collective-permute-done.1.refs_2_.refs_1_), custom_call_target="tpu_custom_call" | custom-call | bytes 1048576 | tf_op jit(solution)/shard_map/pack_ranges/pallas_call | solution.py:47
  53.7 3.1 %collective-permute-start.3 = (bf16[2,8,96,512]{3,2,1,0:T(8,128)(2,1)}, bf16[2,8,96,512]{3,2,1,0:T(8,128)(2,1)}, u32[]{:S(2)}, u32[]{:S(2)}) collective-permute-start(bf16[2,8,96,512]{3,2,1,0:T(8,128)(2,1)} %pack_ranges.2), channel_id=1, source_target_pairs={{0,8},{8,0},{28,12},{16,24},{24,16},{12,28},{1,9},{9,1},{29,13},{1... | collective-permute-start | bytes 4718600 | tf_op jit(solution)/shard_map/ppermute | solution.py:212
  56.9 3.3 %pack_ranges.3 = (bf16[2,8,96,512]{3,2,1,0:T(8,128)(2,1)}, bf16[2,8,64,512]{3,2,1,0:T(8,128)(2,1)}) custom-call(s32[1]{0:T(128)} %bitcast.1.which, bf16[2,8,256,512]{3,2,1,0:T(8,128)(2,1)} %collective-permute-done.refs_0_.refs_2_, bf16[2,8,256,512]{3,2,1,0:T(8,128)(2,1)} %refs_0_.5, bf16[2,8,256,512]{3,2,1,0:T(8,128)(2,1)} %collective-permute-done.1.refs_2_.refs_1_), custom_call_target="tpu_custom_call" | custom-call | bytes 1048576 | tf_op jit(solution)/shard_map/pack_ranges/pallas_call | solution.py:47
  60.2 15.0 %collective-permute-done.3.refs_4_ = bf16[2,8,96,512]{3,2,1,0:T(8,128)(2,1)} collective-permute-done((bf16[2,8,96,512]{3,2,1,0:T(8,128)(2,1)}, bf16[2,8,96,512]{3,2,1,0:T(8,128)(2,1)}, u32[]{:S(2)}, u32[]{:S(2)}) %collective-permute-start.3) | collective-permute-done | bytes 1572896 | tf_op jit(solution)/shard_map/ppermute | solution.py:212
  75.2 1.3 collective-permute-start.4
  76.4 3.1 %collective-permute-start.8 = (bf16[2,8,96,512]{3,2,1,0:T(8,128)(2,1)}, bf16[2,8,96,512]{3,2,1,0:T(8,128)(2,1)}, u32[]{:S(2)}, u32[]{:S(2)}) collective-permute-start(bf16[2,8,96,512]{3,2,1,0:T(8,128)(2,1)} %get-tuple-element.31), channel_id=1, source_target_pairs={{0,8},{8,0},{28,12},{16,24},{24,16},{12,28},{1,9},{9,1},{29,13},{1... | collective-permute-start | bytes 4718600 | tf_op jit(solution)/shard_map/ppermute | solution.py:212
  79.6 1.1 collective-permute-done.4.refs_5_
  80.7 6.0 %pair_products.3 = (f32[3,96,128]{2,1,0:T(8,128)S(1)}, f32[3,96,128]{2,1,0:T(8,128)}, f32[3,96,128]{2,1,0:T(8,128)}, f32[3,96,128]{2,1,0:T(8,128)}) custom-call(s32[13]{0:T(128)S(1)} %pad_add_fusion.places, f32[8,128]{1,0:T(8,128)S(1)} %mark.3.unread, bf16[2,8,256,512]{3,2,1,0:T(8,128)(2,1)} %refs_0_.5, bf16[2,8,256,512]{3,2,1,0:T(8,128)(2,1)} %refs_0_.5, ...), custom_call_target="tpu_custom_call" | custom-call | bytes 1048576 | tf_op jit(solution)/shard_map/pair_products/pallas_call | solution.py:130
  86.7 1.3 collective-permute-start.5
  88.0 1.1 collective-permute-start.6
  89.1 1.4 collective-permute-start.7
  90.5 7.7 %collective-permute-done.8.refs_4_ = bf16[2,8,96,512]{3,2,1,0:T(8,128)(2,1)} collective-permute-done((bf16[2,8,96,512]{3,2,1,0:T(8,128)(2,1)}, bf16[2,8,96,512]{3,2,1,0:T(8,128)(2,1)}, u32[]{:S(2)}, u32[]{:S(2)}) %collective-permute-start.8) | collective-permute-done | bytes 1572896 | tf_op jit(solution)/shard_map/ppermute | solution.py:212
  98.2 2.2 %collective-permute-done.6.refs_2_ = f32[3,96,128]{2,1,0:T(8,128)} collective-permute-done((f32[3,96,128]{2,1,0:T(8,128)}, f32[3,96,128]{2,1,0:T(8,128)}, u32[]{:S(2)}, u32[]{:S(2)}) %collective-permute-start.6) | collective-permute-done | bytes 147488 | tf_op jit(solution)/shard_map/ppermute | solution.py:222
  100.5 2.7 %collective-permute-done.7.refs_3_ = f32[3,96,128]{2,1,0:T(8,128)} collective-permute-done((f32[3,96,128]{2,1,0:T(8,128)}, f32[3,96,128]{2,1,0:T(8,128)}, u32[]{:S(2)}, u32[]{:S(2)}) %collective-permute-start.7) | collective-permute-done | bytes 147488 | tf_op jit(solution)/shard_map/ppermute | solution.py:222
  103.1 1.3 collective-permute-start.9
  104.4 3.6 %collective-permute-start.13 = (bf16[2,8,64,512]{3,2,1,0:T(8,128)(2,1)}, bf16[2,8,64,512]{3,2,1,0:T(8,128)(2,1)}, u32[]{:S(2)}, u32[]{:S(2)}) collective-permute-start(bf16[2,8,64,512]{3,2,1,0:T(8,128)(2,1)} %get-tuple-element.37.value), channel_id=1, source_target_pairs={{0,8},{8,0},{28,12},{16,24},{24,16},{12,28},{1,9},{9,1},{29,13},{1... | collective-permute-start | bytes 3145736 | tf_op jit(solution)/shard_map/ppermute | solution.py:212
  108.6 5.1 %pair_products.4 = (f32[3,96,128]{2,1,0:T(8,128)S(1)}, f32[3,96,128]{2,1,0:T(8,128)S(1)}, f32[3,96,128]{2,1,0:T(8,128)S(1)}, f32[3,96,128]{2,1,0:T(8,128)S(1)}) custom-call(s32[13]{0:T(128)S(1)} %pad_add_fusion.places, f32[8,128]{1,0:T(8,128)S(1)} %mark.4.unread, bf16[2,8,256,512]{3,2,1,0:T(8,128)(2,1)} %refs_0_.5, bf16[2,8,256,512]{3,2,1,0:T(8,128)(2,1)} %refs_0_.5, ...), custom_call_target="tpu_custom_call" | custom-call | bytes 1048576 | tf_op jit(solution)/shard_map/pair_products/pallas_call | solution.py:130
  113.8 7.0 %collective-permute-done.13.refs_4_ = bf16[2,8,64,512]{3,2,1,0:T(8,128)(2,1)} collective-permute-done((bf16[2,8,64,512]{3,2,1,0:T(8,128)(2,1)}, bf16[2,8,64,512]{3,2,1,0:T(8,128)(2,1)}, u32[]{:S(2)}, u32[]{:S(2)}) %collective-permute-start.13) | collective-permute-done | bytes 1048608 | tf_op jit(solution)/shard_map/ppermute | solution.py:212
  120.8 1.3 collective-permute-start.14
  122.1 1.4 collective-permute-start.11
  123.5 1.4 collective-permute-start.12
  124.9 1.4 collective-permute-done.14.refs_5_
  126.3 4.8 %pair_products.5 = (f32[3,64,128]{2,1,0:T(8,128)S(1)}, f32[3,64,128]{2,1,0:T(8,128)S(1)}, f32[3,64,128]{2,1,0:T(8,128)S(1)}, f32[3,64,128]{2,1,0:T(8,128)S(1)}) custom-call(s32[13]{0:T(128)S(1)} %pad_add_fusion.places, f32[8,128]{1,0:T(8,128)S(1)} %mark.5.unread, bf16[2,8,256,512]{3,2,1,0:T(8,128)(2,1)} %refs_0_.5, bf16[2,8,256,512]{3,2,1,0:T(8,128)(2,1)} %refs_0_.5, ...), custom_call_target="tpu_custom_call" | custom-call | bytes 1048576 | tf_op jit(solution)/shard_map/pair_products/pallas_call | solution.py:130
  131.2 1.6 %collective-permute-start.16 = (f32[3,64,128]{2,1,0:T(8,128)S(1)}, f32[3,64,128]{2,1,0:T(8,128)S(1)}, u32[]{:S(2)}, u32[]{:S(2)}) collective-permute-start(f32[3,64,128]{2,1,0:T(8,128)S(1)} %get-tuple-element.41), channel_id=1, source_target_pairs={{0,2},{1,3},{2,0},{3,1},{4,6},{5,7},{6,4},{7,5},{8,10},{9,11},{10,... | collective-permute-start | bytes 294920 | tf_op jit(solution)/shard_map/ppermute | solution.py:222
  133.4 8.0 %collective-permute-done.12.refs_7_ = f32[3,96,128]{2,1,0:T(8,128)S(1)} collective-permute-done((f32[3,96,128]{2,1,0:T(8,128)S(1)}, f32[3,96,128]{2,1,0:T(8,128)S(1)}, u32[]{:S(2)}, u32[]{:S(2)}) %collective-permute-start.12) | collective-permute-done | bytes 147488 | tf_op jit(solution)/shard_map/ppermute | solution.py:222
  141.8 3.8 %collective-permute-done.17.refs_11_ = f32[3,64,128]{2,1,0:T(8,128)S(1)} collective-permute-done((f32[3,64,128]{2,1,0:T(8,128)S(1)}, f32[3,64,128]{2,1,0:T(8,128)S(1)}, u32[]{:S(2)}, u32[]{:S(2)}) %collective-permute-start.17) | collective-permute-done | bytes 98336 | tf_op jit(solution)/shard_map/ppermute | solution.py:222
  145.7 2.0 %sum_terms.1 = f32[6,64,256]{2,1,0:T(8,128)} custom-call(f32[3,96,128]{2,1,0:T(8,128)S(1)} %get-tuple-element.27.value.refs_0_, f32[3,96,128]{2,1,0:T(8,128)} %collective-permute-done.5.refs_1_, f32[3,96,128]{2,1,0:T(8,128)} %collective-permute-done.6.refs_2_, f32[3,96,128]{2,1,0:T(8,128)} %collective-permute-done.7.refs_3_, ...), custom_call_target="tpu_custom_call" | custom-call | tf_op jit(solution)/shard_map/sum_terms/pallas_call | solution.py:223
  (18 shorter events, 2.1 us)
Async XLA Ops:
  0.0 7.8 %collective-permute-start.1 = (bf16[2,8,256,512]{3,2,1,0:T(8,128)(2,1)}, bf16[2,8,256,512]{3,2,1,0:T(8,128)(2,1)}, u32[]{:S(2)}, u32[]{:S(2)}) collective-permute-start(bf16[2,8,256,512]{3,2,1,0:T(8,128)(2,1)} %refs_0_.5), channel_id=1, source_target_pairs={{0,4},{4,0},{8,12},{12,8},{16,20},{20,16},{24,28},{28,24},{1,5},{5... | collective-permute-start | bytes 12582920 | tf_op jit(solution)/shard_map/ppermute | solution.py:205
  0.7 50.5 %collective-permute-start = (bf16[2,8,256,512]{3,2,1,0:T(8,128)(2,1)}, bf16[2,8,256,512]{3,2,1,0:T(8,128)(2,1)}, u32[]{:S(2)}, u32[]{:S(2)}) collective-permute-start(bf16[2,8,256,512]{3,2,1,0:T(8,128)(2,1)} %refs_0_.5), channel_id=1, source_target_pairs={{16,0},{12,4},{20,12},{0,16},{28,20},{4,28},{17,1},{13,5},{21,13},... | collective-permute-start | bytes 12582920 | tf_op jit(solution)/shard_map/ppermute | solution.py:204
  53.7 21.5 %collective-permute-start.3 = (bf16[2,8,96,512]{3,2,1,0:T(8,128)(2,1)}, bf16[2,8,96,512]{3,2,1,0:T(8,128)(2,1)}, u32[]{:S(2)}, u32[]{:S(2)}) collective-permute-start(bf16[2,8,96,512]{3,2,1,0:T(8,128)(2,1)} %pack_ranges.2), channel_id=1, source_target_pairs={{0,8},{8,0},{28,12},{16,24},{24,16},{12,28},{1,9},{9,1},{29,13},{1... | collective-permute-start | bytes 4718600 | tf_op jit(solution)/shard_map/ppermute | solution.py:212
  56.8 23.8 %collective-permute-start.2 = (bf16[2,8,256,512]{3,2,1,0:T(8,128)(2,1)}, bf16[2,8,256,512]{3,2,1,0:T(8,128)(2,1)}, u32[]{:S(2)}, u32[]{:S(2)}) collective-permute-start(bf16[2,8,256,512]{3,2,1,0:T(8,128)(2,1)} %collective-permute-done.refs_0_.refs_2_), channel_id=1, source_target_pairs={{0,4},{4,0},{8,12},{12,8},{16,20},{20,16},{24,28},{28,24},{1,5},{5... | collective-permute-start | bytes 12582920 | tf_op jit(solution)/shard_map/ppermute | solution.py:206
  75.2 5.5 %collective-permute-start.4 = (bf16[2,8,96,512]{3,2,1,0:T(8,128)(2,1)}, bf16[2,8,96,512]{3,2,1,0:T(8,128)(2,1)S(1)}, u32[]{:S(2)}, u32[]{:S(2)}) collective-permute-start(bf16[2,8,96,512]{3,2,1,0:T(8,128)(2,1)} %collective-permute-done.3.refs_4_), channel_id=1, source_target_pairs={{0,4},{8,12},{16,20},{24,28},{1,5},{9,13},{17,21},{25,29},{2,6},{1... | collective-permute-start | bytes 4718600 | tf_op jit(solution)/shard_map/ppermute | solution.py:214
  76.4 21.8 %collective-permute-start.8 = (bf16[2,8,96,512]{3,2,1,0:T(8,128)(2,1)}, bf16[2,8,96,512]{3,2,1,0:T(8,128)(2,1)}, u32[]{:S(2)}, u32[]{:S(2)}) collective-permute-start(bf16[2,8,96,512]{3,2,1,0:T(8,128)(2,1)} %get-tuple-element.31), channel_id=1, source_target_pairs={{0,8},{8,0},{28,12},{16,24},{24,16},{12,28},{1,9},{9,1},{29,13},{1... | collective-permute-start | bytes 4718600 | tf_op jit(solution)/shard_map/ppermute | solution.py:212
  86.7 11.6 %collective-permute-start.5 = (f32[3,96,128]{2,1,0:T(8,128)}, f32[3,96,128]{2,1,0:T(8,128)}, u32[]{:S(2)}, u32[]{:S(2)}) collective-permute-start(f32[3,96,128]{2,1,0:T(8,128)} %get-tuple-element.28), channel_id=1, source_target_pairs={{0,1},{1,2},{2,3},{3,0},{4,5},{5,6},{6,7},{7,4},{8,9},{9,10},{10,1... | collective-permute-start | bytes 442376 | tf_op jit(solution)/shard_map/ppermute | solution.py:222
  88.0 12.4 %collective-permute-start.6 = (f32[3,96,128]{2,1,0:T(8,128)}, f32[3,96,128]{2,1,0:T(8,128)}, u32[]{:S(2)}, u32[]{:S(2)}) collective-permute-start(f32[3,96,128]{2,1,0:T(8,128)} %get-tuple-element.29), channel_id=1, source_target_pairs={{0,2},{1,3},{2,0},{3,1},{4,6},{5,7},{6,4},{7,5},{8,10},{9,11},{10,... | collective-permute-start | bytes 442376 | tf_op jit(solution)/shard_map/ppermute | solution.py:222
  89.1 14.0 %collective-permute-start.7 = (f32[3,96,128]{2,1,0:T(8,128)}, f32[3,96,128]{2,1,0:T(8,128)}, u32[]{:S(2)}, u32[]{:S(2)}) collective-permute-start(f32[3,96,128]{2,1,0:T(8,128)} %get-tuple-element.30), channel_id=1, source_target_pairs={{0,3},{1,0},{2,1},{3,2},{4,7},{5,4},{6,5},{7,6},{8,11},{9,8},{10,9... | collective-permute-start | bytes 442376 | tf_op jit(solution)/shard_map/ppermute | solution.py:222
  103.1 5.5 %collective-permute-start.9 = (bf16[2,8,96,512]{3,2,1,0:T(8,128)(2,1)}, bf16[2,8,96,512]{3,2,1,0:T(8,128)(2,1)S(1)}, u32[]{:S(2)}, u32[]{:S(2)}) collective-permute-start(bf16[2,8,96,512]{3,2,1,0:T(8,128)(2,1)} %collective-permute-done.8.refs_4_), channel_id=1, source_target_pairs={{0,4},{8,12},{16,20},{24,28},{1,5},{9,13},{17,21},{25,29},{2,6},{1... | collective-permute-start | bytes 4718600 | tf_op jit(solution)/shard_map/ppermute | solution.py:214
  104.4 16.3 %collective-permute-start.13 = (bf16[2,8,64,512]{3,2,1,0:T(8,128)(2,1)}, bf16[2,8,64,512]{3,2,1,0:T(8,128)(2,1)}, u32[]{:S(2)}, u32[]{:S(2)}) collective-permute-start(bf16[2,8,64,512]{3,2,1,0:T(8,128)(2,1)} %get-tuple-element.37.value), channel_id=1, source_target_pairs={{0,8},{8,0},{28,12},{16,24},{24,16},{12,28},{1,9},{9,1},{29,13},{1... | collective-permute-start | bytes 3145736 | tf_op jit(solution)/shard_map/ppermute | solution.py:212
  120.8 5.5 %collective-permute-start.14 = (bf16[2,8,64,512]{3,2,1,0:T(8,128)(2,1)}, bf16[2,8,64,512]{3,2,1,0:T(8,128)(2,1)S(1)}, u32[]{:S(2)}, u32[]{:S(2)}) collective-permute-start(bf16[2,8,64,512]{3,2,1,0:T(8,128)(2,1)} %collective-permute-done.13.refs_4_), channel_id=1, source_target_pairs={{0,4},{8,12},{16,20},{24,28},{1,5},{9,13},{17,21},{25,29},{2,6},{1... | collective-permute-start | bytes 3145736 | tf_op jit(solution)/shard_map/ppermute | solution.py:214
  122.1 10.7 %collective-permute-start.10 = (f32[3,96,128]{2,1,0:T(8,128)S(1)}, f32[3,96,128]{2,1,0:T(8,128)S(1)}, u32[]{:S(2)}, u32[]{:S(2)}) collective-permute-start(f32[3,96,128]{2,1,0:T(8,128)S(1)} %get-tuple-element.34), channel_id=1, source_target_pairs={{0,1},{1,2},{2,3},{3,0},{4,5},{5,6},{6,7},{7,4},{8,9},{9,10},{10,1... | collective-permute-start | bytes 442376 | tf_op jit(solution)/shard_map/ppermute | solution.py:222
  122.1 11.3 %collective-permute-start.11 = (f32[3,96,128]{2,1,0:T(8,128)S(1)}, f32[3,96,128]{2,1,0:T(8,128)S(1)}, u32[]{:S(2)}, u32[]{:S(2)}) collective-permute-start(f32[3,96,128]{2,1,0:T(8,128)S(1)} %get-tuple-element.35), channel_id=1, source_target_pairs={{0,2},{1,3},{2,0},{3,1},{4,6},{5,7},{6,4},{7,5},{8,10},{9,11},{10,... | collective-permute-start | bytes 442376 | tf_op jit(solution)/shard_map/ppermute | solution.py:222
  123.5 17.9 %collective-permute-start.12 = (f32[3,96,128]{2,1,0:T(8,128)S(1)}, f32[3,96,128]{2,1,0:T(8,128)S(1)}, u32[]{:S(2)}, u32[]{:S(2)}) collective-permute-start(f32[3,96,128]{2,1,0:T(8,128)S(1)} %get-tuple-element.36), channel_id=1, source_target_pairs={{0,3},{1,0},{2,1},{3,2},{4,7},{5,4},{6,5},{7,6},{8,11},{9,8},{10,9... | collective-permute-start | bytes 442376 | tf_op jit(solution)/shard_map/ppermute | solution.py:222
  131.1 10.3 %collective-permute-start.15 = (f32[3,64,128]{2,1,0:T(8,128)S(1)}, f32[3,64,128]{2,1,0:T(8,128)S(1)}, u32[]{:S(2)}, u32[]{:S(2)}) collective-permute-start(f32[3,64,128]{2,1,0:T(8,128)S(1)} %get-tuple-element.40), channel_id=1, source_target_pairs={{0,1},{1,2},{2,3},{3,0},{4,5},{5,6},{6,7},{7,4},{8,9},{9,10},{10,1... | collective-permute-start | bytes 294920 | tf_op jit(solution)/shard_map/ppermute | solution.py:222
  131.2 10.6 %collective-permute-start.16 = (f32[3,64,128]{2,1,0:T(8,128)S(1)}, f32[3,64,128]{2,1,0:T(8,128)S(1)}, u32[]{:S(2)}, u32[]{:S(2)}) collective-permute-start(f32[3,64,128]{2,1,0:T(8,128)S(1)} %get-tuple-element.41), channel_id=1, source_target_pairs={{0,2},{1,3},{2,0},{3,1},{4,6},{5,7},{6,4},{7,5},{8,10},{9,11},{10,... | collective-permute-start | bytes 294920 | tf_op jit(solution)/shard_map/ppermute | solution.py:222
  132.8 12.9 %collective-permute-start.17 = (f32[3,64,128]{2,1,0:T(8,128)S(1)}, f32[3,64,128]{2,1,0:T(8,128)S(1)}, u32[]{:S(2)}, u32[]{:S(2)}) collective-permute-start(f32[3,64,128]{2,1,0:T(8,128)S(1)} %get-tuple-element.42), channel_id=1, source_target_pairs={{0,3},{1,0},{2,1},{3,2},{4,7},{5,4},{6,5},{7,6},{8,11},{9,8},{10,9... | collective-permute-start | bytes 294920 | tf_op jit(solution)/shard_map/ppermute | solution.py:222

commit v2 on v1

--- a/solution.py
+++ b/solution.py
@@ -8,33 +8,36 @@
 from jax.sharding import PartitionSpec as P
 
 LANES = 128
-PIECES = ((0, 96), (96, 96), (192, 64))
+PIECES = ((0, 48), (48, 96), (144, 112))
 GROUPS = 4
 KERNEL_BYTES = 14 << 20
+MARK_FLOPS = 10**6
 
 
 def pack_kernel(pieces, which, *refs):
     sources, outs, sems = refs[: -len(pieces) - 1], refs[-len(pieces) - 1 : -1], refs[-1]
-    blocks = outs[0].shape[0]
-    copies = [(turn, block) for turn in range(len(pieces)) for block in range(blocks)]
-
-    def copy(source, turn, block):
+    blocks, depth = outs[0].shape[:2]
+    group = depth // GROUPS
+    copies = [(turn, block, g) for turn in range(len(pieces)) for block in range(blocks) for g in range(GROUPS)]
+
+    def copy(source, turn, block, g):
         first, wide = pieces[turn]
+        part = pl.ds(g * group, group)
         return pltpu.make_async_copy(
-            source.at[block, :, pl.ds(first, wide)], outs[turn].at[block], sems.at[turn, block]
+            source.at[block, part, pl.ds(first, wide)], outs[turn].at[block, part], sems.at[turn, block, g]
         )
 
     for index, source in enumerate(sources):
 
         @pl.when(which[0] == index)
         def start(source=source):
-            for turn, block in copies:
-                copy(source, turn, block).start()
+            for which_part in copies:
+                copy(source, *which_part).start()
 
     @pl.when(which[0] < len(sources))
     def wait():
-        for turn, block in copies:
-            copy(sources[0], turn, block).wait()
+        for which_part in copies:
+            copy(sources[0], *which_part).wait()
 
 
 def in_hbm(value):
@@ -48,7 +51,7 @@
         functools.partial(pack_kernel, pieces),
         in_specs=[pl.BlockSpec(memory_space=pltpu.SMEM)] + [pl.BlockSpec(memory_space=pl.ANY)] * len(sources),
         out_specs=[pl.BlockSpec(memory_space=pltpu.VMEM)] * len(pieces),
-        scratch_shapes=[pltpu.SemaphoreType.DMA((len(pieces), blocks))],
+        scratch_shapes=[pltpu.SemaphoreType.DMA((len(pieces), blocks, GROUPS))],
         out_shape=shapes,
         compiler_params=pltpu.CompilerParams(vmem_limit_bytes=KERNEL_BYTES),
         cost_estimate=pl.CostEstimate(flops=0, bytes_accessed=1 << 20, transcendentals=0),
@@ -161,14 +164,14 @@
     out[...] = jnp.zeros_like(out)
 
 
-def mark(value):
+def mark(value, flops=MARK_FLOPS):
     return pl.pallas_call(
         mark_kernel,
         in_specs=[pl.BlockSpec(memory_space=pl.ANY)],
         out_specs=pl.BlockSpec(memory_space=pltpu.VMEM),
         out_shape=jax.ShapeDtypeStruct((8, LANES), jnp.float32),
         compiler_params=pltpu.CompilerParams(vmem_limit_bytes=1 << 20),
-        cost_estimate=pl.CostEstimate(flops=10**12, bytes_accessed=10**9, transcendentals=0),
+        cost_estimate=pl.CostEstimate(flops=flops, bytes_accessed=1024, transcendentals=0),
         name="mark",
     )(value)
 
@@ -183,7 +186,7 @@
     core = lax.rem(me, 2)
     even = lax.rem(me, 4) < 2
 
-    swap = [(d, d ^ 1) for d in range(devices)]
+    to_core_0 = [(2 * c + 1, 2 * c) for c in range(chips)]
     to_core_1 = [(2 * c, 2 * c + 1) for c in range(chips)]
     early, late = [], []
     for c in range(0, chips, 2):
@@ -202,15 +205,15 @@
     which = jnp.where(even, 3 * core, 1 + core).astype(jnp.int32).reshape(1)
 
     one = lax.ppermute(factors, "ao", early)
-    mate = lax.ppermute(factors, "ao", swap)
-    one_mate = lax.ppermute(one, "ao", swap)
+    mate = lax.ppermute(after(factors, places), "ao", to_core_0 + to_core_1[1::2])
+    one_mate = lax.ppermute(one, "ao", to_core_0 + to_core_1[::2])
     senders = [one, in_hbm(factors), mate]
     sent = pack(which, senders, PIECES[:1])
     sent += pack(after(which, places, *sent), senders, PIECES[1:])
-    twos, made, terms, marks = [], [], [], [mark(sent[-1])]
+    twos, made, terms, marks = [], [], [], [mark(sent[-1], 10**12)]
     for turn, piece in enumerate(PIECES):
         twos.append(lax.ppermute(after(sent[turn], *made[: max(turn - 1, 0)][-1:]), "ao", late))
-        earlier = terms[1 - parts :] if turn == 1 else []
+        earlier = terms[-parts // 2 : 1 - parts // 2] if turn else []
         two_mate = lax.ppermute(after(twos[turn], marks[turn], *earlier), "ao", to_core_1)
         columns = [factors, mate, one, one_mate, twos[turn], two_mate]
         products = pair_products(places, marks[turn], factors, columns, piece, parts, slots)
@@ -218,8 +221,9 @@
         if turn + 1 < len(PIECES):
             marks.append(mark(products[0]))
         terms.append(products[0])
+        others = [t for k, t in enumerate(terms) if k // parts == turn - 1 and k % parts]
         for step in range(1, parts):
-            terms.append(lax.ppermute(products[step], "aux", [(z, (z + step) % parts) for z in range(parts)]))
+            terms.append(lax.ppermute(after(products[step], *others), "aux", [(z, (z + step) % parts) for z in range(parts)]))
     out = pl.pallas_call(
         functools.partial(sum_kernel, parts),
         out_shape=jax.ShapeDtypeStruct((blocks * slots, height // parts, height), jnp.float32),

time: 147 us -> 139 us (0.946)
  the two profiles are of different devices: /device:TPU:11 before, /device:TPU:0 now
where the time goes in v2:
time: 139 us
  waiting for transfers between devices  79.5 us (57%)
  starting transfers between devices  37.3 us (27%)
  Pallas kernels  21.1 us (15%)
    ppermute x1, waiting for transfers between devices, squares(): one = lax.ppermute(factors, 'ao', early)  43.6 us
    ppermute x9, waiting for transfers between devices, squares(): lax.ppermute(after(products[step], *others), 'aux', [(z, (z + step) % par...  24.9 us
    ppermute x9, starting transfers between devices, squares(): lax.ppermute(after(products[step], *others), 'aux', [(z, (z + step) % par...  15.6 us
    pallas_call x3, Pallas kernels, pair_products(): pl.pallas_call(functools.partial(pair_kernel, slots, first, wide, parts),...  14.6 us
    ppermute x3, starting transfers between devices, squares(): lax.ppermute(after(sent[turn], *made[:max(turn - 1, 0)][-1:]), 'ao', late)  9.46 us
    pallas_call x2, Pallas kernels, pack(): pl.pallas_call(functools.partial(pack_kernel, pieces), in_specs=[pl.Block...  5.51 us
    ppermute x1, starting transfers between devices, squares(): one = lax.ppermute(factors, 'ao', early)  4.88 us
    ppermute x3, waiting for transfers between devices, squares(): lax.ppermute(after(sent[turn], *made[:max(turn - 1, 0)][-1:]), 'ao', late)  4.14 us
  transfers between devices with their start and end apart: 18, of which 10 were waited for; matrix products, arithmetic and copies ran while one was open for 0% of the time, Pallas kernels for 13%

profile of v2, /device:TPU:0, one launch (start us, length us, event | category | flops | bytes accessed | tf_op | source)
XLA Modules:
  0.0 139.1 jit_solution(7936783379916416374)
XLA Ops:
  0.0 0.8 compare_select_fusion.4
  1.0 1.3 collective-permute-start.1
  2.3 4.9 %collective-permute-start = (bf16[2,8,256,512]{3,2,1,0:T(8,128)(2,1)}, bf16[2,8,256,512]{3,2,1,0:T(8,128)(2,1)}, u32[]{:S(2)}, u32[]{:S(2)}) collective-permute-start(bf16[2,8,256,512]{3,2,1,0:T(8,128)(2,1)} %refs_0_.5), channel_id=1, source_target_pairs={{16,0},{12,4},{20,12},{0,16},{28,20},{4,28},{17,1},{13,5},{21,13},... | collective-permute-start | bytes 12582920 | tf_op jit(solution)/shard_map/ppermute | solution.py:207
  7.2 3.2 %collective-permute-done.1.refs_2_.refs_1_ = bf16[2,8,256,512]{3,2,1,0:T(8,128)(2,1)} collective-permute-done((bf16[2,8,256,512]{3,2,1,0:T(8,128)(2,1)}, bf16[2,8,256,512]{3,2,1,0:T(8,128)(2,1)}, u32[]{:S(2)}, u32[]{:S(2)}) %collective-permute-start.1) | collective-permute-done | bytes 4194336 | tf_op jit(solution)/shard_map/ppermute | solution.py:208
  10.4 43.6 %collective-permute-done.refs_0_.refs_2_ = bf16[2,8,256,512]{3,2,1,0:T(8,128)(2,1)} collective-permute-done((bf16[2,8,256,512]{3,2,1,0:T(8,128)(2,1)}, bf16[2,8,256,512]{3,2,1,0:T(8,128)(2,1)}, u32[]{:S(2)}, u32[]{:S(2)}) %collective-permute-start) | collective-permute-done | bytes 4194336 | tf_op jit(solution)/shard_map/ppermute | solution.py:207
  54.0 2.2 %pack_ranges.2 = bf16[2,8,48,512]{3,2,1,0:T(8,128)(2,1)} custom-call(s32[1]{0:T(128)} %bitcast.1.which, bf16[2,8,256,512]{3,2,1,0:T(8,128)(2,1)} %collective-permute-done.refs_0_.refs_2_, bf16[2,8,256,512]{3,2,1,0:T(8,128)(2,1)} %refs_0_.5, bf16[2,8,256,512]{3,2,1,0:T(8,128)(2,1)} %collective-permute-done.1.refs_2_.refs_1_), custom_call_target="tpu_custom_call" | custom-call | bytes 1048576 | tf_op jit(solution)/shard_map/pack_ranges/pallas_call | solution.py:50
  56.2 1.9 %collective-permute-start.3 = (bf16[2,8,48,512]{3,2,1,0:T(8,128)(2,1)}, bf16[2,8,48,512]{3,2,1,0:T(8,128)(2,1)}, u32[]{:S(2)}, u32[]{:S(2)}) collective-permute-start(bf16[2,8,48,512]{3,2,1,0:T(8,128)(2,1)} %pack_ranges.2), channel_id=1, source_target_pairs={{0,8},{8,0},{28,12},{16,24},{24,16},{12,28},{1,9},{9,1},{29,13},{1... | collective-permute-start | bytes 2359304 | tf_op jit(solution)/shard_map/ppermute | solution.py:215
  58.1 3.3 %pack_ranges.3 = (bf16[2,8,96,512]{3,2,1,0:T(8,128)(2,1)}, bf16[2,8,112,512]{3,2,1,0:T(8,128)(2,1)S(1)}) custom-call(s32[1]{0:T(128)} %bitcast.1.which, bf16[2,8,256,512]{3,2,1,0:T(8,128)(2,1)} %collective-permute-done.refs_0_.refs_2_, bf16[2,8,256,512]{3,2,1,0:T(8,128)(2,1)} %refs_0_.5, bf16[2,8,256,512]{3,2,1,0:T(8,128)(2,1)} %collective-permute-done.1.refs_2_.refs_1_), custom_call_target="tpu_custom_call" | custom-call | bytes 1048576 | tf_op jit(solution)/shard_map/pack_ranges/pallas_call | solution.py:50
  61.4 3.9 %collective-permute-start.8 = (bf16[2,8,96,512]{3,2,1,0:T(8,128)(2,1)}, bf16[2,8,96,512]{3,2,1,0:T(8,128)(2,1)}, u32[]{:S(2)}, u32[]{:S(2)}) collective-permute-start(bf16[2,8,96,512]{3,2,1,0:T(8,128)(2,1)} %get-tuple-element.39), channel_id=1, source_target_pairs={{0,8},{8,0},{28,12},{16,24},{24,16},{12,28},{1,9},{9,1},{29,13},{1... | collective-permute-start | bytes 4718600 | tf_op jit(solution)/shard_map/ppermute | solution.py:215
  65.4 1.9 %collective-permute-start.2 = (bf16[2,8,256,512]{3,2,1,0:T(8,128)(2,1)}, bf16[2,8,256,512]{3,2,1,0:T(8,128)(2,1)}, u32[]{:S(2)}, u32[]{:S(2)}) collective-permute-start(bf16[2,8,256,512]{3,2,1,0:T(8,128)(2,1)} %collective-permute-done.refs_0_.refs_2_), channel_id=1, source_target_pairs={{4,0},{12,8},{20,16},{28,24},{0,4},{16,20},{5,1},{13,9},{21,17},{2... | collective-permute-start | bytes 12582920 | tf_op jit(solution)/shard_map/ppermute | solution.py:209
  67.3 3.0 %collective-permute-done.3.refs_4_ = bf16[2,8,48,512]{3,2,1,0:T(8,128)(2,1)} collective-permute-done((bf16[2,8,48,512]{3,2,1,0:T(8,128)(2,1)}, bf16[2,8,48,512]{3,2,1,0:T(8,128)(2,1)}, u32[]{:S(2)}, u32[]{:S(2)}) %collective-permute-start.3) | collective-permute-done | bytes 786464 | tf_op jit(solution)/shard_map/ppermute | solution.py:215
  70.4 1.3 collective-permute-start.4
  71.7 3.7 %collective-permute-done.4.refs_5_ = bf16[2,8,48,512]{3,2,1,0:T(8,128)(2,1)S(1)} collective-permute-done((bf16[2,8,48,512]{3,2,1,0:T(8,128)(2,1)}, bf16[2,8,48,512]{3,2,1,0:T(8,128)(2,1)S(1)}, u32[]{:S(2)}, u32[]{:S(2)}) %collective-permute-start.4) | collective-permute-done | bytes 786464 | tf_op jit(solution)/shard_map/ppermute | solution.py:217
  75.4 4.4 %pair_products.3 = (f32[3,48,128]{2,1,0:T(8,128)S(1)}, f32[3,48,128]{2,1,0:T(8,128)S(1)}, f32[3,48,128]{2,1,0:T(8,128)S(1)}, f32[3,48,128]{2,1,0:T(8,128)S(1)}) custom-call(s32[13]{0:T(128)S(1)} %pad_add_fusion.places, f32[8,128]{1,0:T(8,128)S(1)} %mark.3.unread, bf16[2,8,256,512]{3,2,1,0:T(8,128)(2,1)} %refs_0_.5, bf16[2,8,256,512]{3,2,1,0:T(8,128)(2,1)} %refs_0_.5, ...), custom_call_target="tpu_custom_call" | custom-call | bytes 1048576 | tf_op jit(solution)/shard_map/pair_products/pallas_call | solution.py:133
  79.8 3.6 %collective-permute-start.13 = (bf16[2,8,112,512]{3,2,1,0:T(8,128)(2,1)S(1)}, bf16[2,8,112,512]{3,2,1,0:T(8,128)(2,1)S(1)}, u32[]{:S(2)}, u32[]{:S(2)}) collective-permute-start(bf16[2,8,112,512]{3,2,1,0:T(8,128)(2,1)S(1)} %get-tuple-element.48.value), channel_id=1, source_target_pairs={{0,8},{8,0},{28,12},{16,24},{24,16},{12,28},{1,9},{9,1},{29,13},{1... | collective-permute-start | bytes 5505032 | tf_op jit(solution)/shard_map/ppermute | solution.py:215
  83.4 2.7 %collective-permute-start.6 = (f32[3,48,128]{2,1,0:T(8,128)S(1)}, f32[3,48,128]{2,1,0:T(8,128)S(1)}, u32[]{:S(2)}, u32[]{:S(2)}) collective-permute-start(f32[3,48,128]{2,1,0:T(8,128)S(1)} %get-tuple-element.37), channel_id=1, source_target_pairs={{0,2},{1,3},{2,0},{3,1},{4,6},{5,7},{6,4},{7,5},{8,10},{9,11},{10,... | collective-permute-start | bytes 221192 | tf_op jit(solution)/shard_map/ppermute | solution.py:226
  86.1 1.1 collective-permute-done.8.refs_4_
  87.2 1.5 %collective-permute-done.6.refs_2_ = f32[3,48,128]{2,1,0:T(8,128)S(1)} collective-permute-done((f32[3,48,128]{2,1,0:T(8,128)S(1)}, f32[3,48,128]{2,1,0:T(8,128)S(1)}, u32[]{:S(2)}, u32[]{:S(2)}) %collective-permute-start.6) | collective-permute-done | bytes 73760 | tf_op jit(solution)/shard_map/ppermute | solution.py:226
  88.7 1.4 collective-permute-start.9
  90.1 1.7 %collective-permute-start.5 = (f32[3,48,128]{2,1,0:T(8,128)S(1)}, f32[3,48,128]{2,1,0:T(8,128)S(1)}, u32[]{:S(2)}, u32[]{:S(2)}) collective-permute-start(f32[3,48,128]{2,1,0:T(8,128)S(1)} %get-tuple-element.36), channel_id=1, source_target_pairs={{0,1},{1,2},{2,3},{3,0},{4,5},{5,6},{6,7},{7,4},{8,9},{9,10},{10,1... | collective-permute-start | bytes 221192 | tf_op jit(solution)/shard_map/ppermute | solution.py:226
  91.8 2.8 %collective-permute-start.7 = (f32[3,48,128]{2,1,0:T(8,128)S(1)}, f32[3,48,128]{2,1,0:T(8,128)S(1)}, u32[]{:S(2)}, u32[]{:S(2)}) collective-permute-start(f32[3,48,128]{2,1,0:T(8,128)S(1)} %get-tuple-element.38), channel_id=1, source_target_pairs={{0,3},{1,0},{2,1},{3,2},{4,7},{5,4},{6,5},{7,6},{8,11},{9,8},{10,9... | collective-permute-start | bytes 221192 | tf_op jit(solution)/shard_map/ppermute | solution.py:226
  94.6 5.0 %pair_products.4 = (f32[3,96,128]{2,1,0:T(8,128)S(1)}, f32[3,96,128]{2,1,0:T(8,128)S(1)}, f32[3,96,128]{2,1,0:T(8,128)S(1)}, f32[3,96,128]{2,1,0:T(8,128)S(1)}) custom-call(s32[13]{0:T(128)S(1)} %pad_add_fusion.places, f32[8,128]{1,0:T(8,128)S(1)} %mark.4.unread, bf16[2,8,256,512]{3,2,1,0:T(8,128)(2,1)} %refs_0_.5, bf16[2,8,256,512]{3,2,1,0:T(8,128)(2,1)} %refs_0_.5, ...), custom_call_target="tpu_custom_call" | custom-call | bytes 1048576 | tf_op jit(solution)/shard_map/pair_products/pallas_call | solution.py:133
  99.6 1.5 %collective-permute-start.11 = (f32[3,96,128]{2,1,0:T(8,128)S(1)}, f32[3,96,128]{2,1,0:T(8,128)S(1)}, u32[]{:S(2)}, u32[]{:S(2)}) collective-permute-start(f32[3,96,128]{2,1,0:T(8,128)S(1)} %get-tuple-element.45), channel_id=1, source_target_pairs={{0,2},{1,3},{2,0},{3,1},{4,6},{5,7},{6,4},{7,5},{8,10},{9,11},{10,... | collective-permute-start | bytes 442376 | tf_op jit(solution)/shard_map/ppermute | solution.py:226
  101.1 7.3 %collective-permute-done.11.refs_6_ = f32[3,96,128]{2,1,0:T(8,128)S(1)} collective-permute-done((f32[3,96,128]{2,1,0:T(8,128)S(1)}, f32[3,96,128]{2,1,0:T(8,128)S(1)}, u32[]{:S(2)}, u32[]{:S(2)}) %collective-permute-start.11) | collective-permute-done | bytes 147488 | tf_op jit(solution)/shard_map/ppermute | solution.py:226
  108.4 1.4 %collective-permute-start.14 = (bf16[2,8,112,512]{3,2,1,0:T(8,128)(2,1)S(1)}, bf16[2,8,112,512]{3,2,1,0:T(8,128)(2,1)S(1)}, u32[]{:S(2)}, u32[]{:S(2)}) collective-permute-start(bf16[2,8,112,512]{3,2,1,0:T(8,128)(2,1)S(1)} %collective-permute-done.13.refs_4_), channel_id=1, source_target_pairs={{0,4},{8,12},{16,20},{24,28},{1,5},{9,13},{17,21},{25,29},{2,6},{1... | collective-permute-start | bytes 5505032 | tf_op jit(solution)/shard_map/ppermute | solution.py:217
  109.8 4.2 %collective-permute-start.12 = (f32[3,96,128]{2,1,0:T(8,128)S(1)}, f32[3,96,128]{2,1,0:T(8,128)S(1)}, u32[]{:S(2)}, u32[]{:S(2)}) collective-permute-start(f32[3,96,128]{2,1,0:T(8,128)S(1)} %get-tuple-element.47), channel_id=1, source_target_pairs={{0,3},{1,0},{2,1},{3,2},{4,7},{5,4},{6,5},{7,6},{8,11},{9,8},{10,9... | collective-permute-start | bytes 442376 | tf_op jit(solution)/shard_map/ppermute | solution.py:226
  114.0 5.2 %pair_products.5 = (f32[3,112,128]{2,1,0:T(8,128)S(1)}, f32[3,112,128]{2,1,0:T(8,128)S(1)}, f32[3,112,128]{2,1,0:T(8,128)S(1)}, f32[3,112,128]{2,1,0:T(8,128)S(1)}) custom-call(s32[13]{0:T(128)S(1)} %pad_add_fusion.places, f32[8,128]{1,0:T(8,128)S(1)} %mark.5.unread, bf16[2,8,256,512]{3,2,1,0:T(8,128)(2,1)} %refs_0_.5, bf16[2,8,256,512]{3,2,1,0:T(8,128)(2,1)} %refs_0_.5, ...), custom_call_target="tpu_custom_call" | custom-call | bytes 1048576 | tf_op jit(solution)/shard_map/pair_products/pallas_call | solution.py:133
  119.2 1.7 %collective-permute-done.10.refs_5_ = f32[3,96,128]{2,1,0:T(8,128)S(1)} collective-permute-done((f32[3,96,128]{2,1,0:T(8,128)S(1)}, f32[3,96,128]{2,1,0:T(8,128)S(1)}, u32[]{:S(2)}, u32[]{:S(2)}) %collective-permute-start.10) | collective-permute-done | bytes 147488 | tf_op jit(solution)/shard_map/ppermute | solution.py:226
  120.9 2.2 %collective-permute-start.17 = (f32[3,112,128]{2,1,0:T(8,128)S(1)}, f32[3,112,128]{2,1,0:T(8,128)S(1)}, u32[]{:S(2)}, u32[]{:S(2)}) collective-permute-start(f32[3,112,128]{2,1,0:T(8,128)S(1)} %get-tuple-element.56), channel_id=1, source_target_pairs={{0,3},{1,0},{2,1},{3,2},{4,7},{5,4},{6,5},{7,6},{8,11},{9,8},{10,9... | collective-permute-start | bytes 516104 | tf_op jit(solution)/shard_map/ppermute | solution.py:226
  123.8 4.2 %collective-permute-done.17.refs_11_ = f32[3,112,128]{2,1,0:T(8,128)S(1)} collective-permute-done((f32[3,112,128]{2,1,0:T(8,128)S(1)}, f32[3,112,128]{2,1,0:T(8,128)S(1)}, u32[]{:S(2)}, u32[]{:S(2)}) %collective-permute-start.17) | collective-permute-done | bytes 172064 | tf_op jit(solution)/shard_map/ppermute | solution.py:226
  128.0 10.2 %collective-permute-done.16.refs_10_ = f32[3,112,128]{2,1,0:T(8,128)S(1)} collective-permute-done((f32[3,112,128]{2,1,0:T(8,128)S(1)}, f32[3,112,128]{2,1,0:T(8,128)S(1)}, u32[]{:S(2)}, u32[]{:S(2)}) %collective-permute-start.16) | collective-permute-done | bytes 172064 | tf_op jit(solution)/shard_map/ppermute | solution.py:226
  138.1 0.9 sum_terms.1
  (18 shorter events, 0.9 us)
Async XLA Ops:
  1.0 9.4 %collective-permute-start.1 = (bf16[2,8,256,512]{3,2,1,0:T(8,128)(2,1)}, bf16[2,8,256,512]{3,2,1,0:T(8,128)(2,1)}, u32[]{:S(2)}, u32[]{:S(2)}) collective-permute-start(bf16[2,8,256,512]{3,2,1,0:T(8,128)(2,1)} %refs_0_.5), channel_id=1, source_target_pairs={{4,0},{12,8},{20,16},{28,24},{8,12},{24,28},{5,1},{13,9},{21,17},{... | collective-permute-start | bytes 12582920 | tf_op jit(solution)/shard_map/ppermute | solution.py:208
  2.3 51.7 %collective-permute-start = (bf16[2,8,256,512]{3,2,1,0:T(8,128)(2,1)}, bf16[2,8,256,512]{3,2,1,0:T(8,128)(2,1)}, u32[]{:S(2)}, u32[]{:S(2)}) collective-permute-start(bf16[2,8,256,512]{3,2,1,0:T(8,128)(2,1)} %refs_0_.5), channel_id=1, source_target_pairs={{16,0},{12,4},{20,12},{0,16},{28,20},{4,28},{17,1},{13,5},{21,13},... | collective-permute-start | bytes 12582920 | tf_op jit(solution)/shard_map/ppermute | solution.py:207
  56.2 14.2 %collective-permute-start.3 = (bf16[2,8,48,512]{3,2,1,0:T(8,128)(2,1)}, bf16[2,8,48,512]{3,2,1,0:T(8,128)(2,1)}, u32[]{:S(2)}, u32[]{:S(2)}) collective-permute-start(bf16[2,8,48,512]{3,2,1,0:T(8,128)(2,1)} %pack_ranges.2), channel_id=1, source_target_pairs={{0,8},{8,0},{28,12},{16,24},{24,16},{12,28},{1,9},{9,1},{29,13},{1... | collective-permute-start | bytes 2359304 | tf_op jit(solution)/shard_map/ppermute | solution.py:215
  61.4 25.8 %collective-permute-start.8 = (bf16[2,8,96,512]{3,2,1,0:T(8,128)(2,1)}, bf16[2,8,96,512]{3,2,1,0:T(8,128)(2,1)}, u32[]{:S(2)}, u32[]{:S(2)}) collective-permute-start(bf16[2,8,96,512]{3,2,1,0:T(8,128)(2,1)} %get-tuple-element.39), channel_id=1, source_target_pairs={{0,8},{8,0},{28,12},{16,24},{24,16},{12,28},{1,9},{9,1},{29,13},{1... | collective-permute-start | bytes 4718600 | tf_op jit(solution)/shard_map/ppermute | solution.py:215
  65.4 10.0 %collective-permute-start.2 = (bf16[2,8,256,512]{3,2,1,0:T(8,128)(2,1)}, bf16[2,8,256,512]{3,2,1,0:T(8,128)(2,1)}, u32[]{:S(2)}, u32[]{:S(2)}) collective-permute-start(bf16[2,8,256,512]{3,2,1,0:T(8,128)(2,1)} %collective-permute-done.refs_0_.refs_2_), channel_id=1, source_target_pairs={{4,0},{12,8},{20,16},{28,24},{0,4},{16,20},{5,1},{13,9},{21,17},{2... | collective-permute-start | bytes 12582920 | tf_op jit(solution)/shard_map/ppermute | solution.py:209
  70.4 5.1 %collective-permute-start.4 = (bf16[2,8,48,512]{3,2,1,0:T(8,128)(2,1)}, bf16[2,8,48,512]{3,2,1,0:T(8,128)(2,1)S(1)}, u32[]{:S(2)}, u32[]{:S(2)}) collective-permute-start(bf16[2,8,48,512]{3,2,1,0:T(8,128)(2,1)} %collective-permute-done.3.refs_4_), channel_id=1, source_target_pairs={{0,4},{8,12},{16,20},{24,28},{1,5},{9,13},{17,21},{25,29},{2,6},{1... | collective-permute-start | bytes 2359304 | tf_op jit(solution)/shard_map/ppermute | solution.py:217
  79.8 28.6 %collective-permute-start.13 = (bf16[2,8,112,512]{3,2,1,0:T(8,128)(2,1)S(1)}, bf16[2,8,112,512]{3,2,1,0:T(8,128)(2,1)S(1)}, u32[]{:S(2)}, u32[]{:S(2)}) collective-permute-start(bf16[2,8,112,512]{3,2,1,0:T(8,128)(2,1)S(1)} %get-tuple-element.48.value), channel_id=1, source_target_pairs={{0,8},{8,0},{28,12},{16,24},{24,16},{12,28},{1,9},{9,1},{29,13},{1... | collective-permute-start | bytes 5505032 | tf_op jit(solution)/shard_map/ppermute | solution.py:215
  83.4 5.3 %collective-permute-start.6 = (f32[3,48,128]{2,1,0:T(8,128)S(1)}, f32[3,48,128]{2,1,0:T(8,128)S(1)}, u32[]{:S(2)}, u32[]{:S(2)}) collective-permute-start(f32[3,48,128]{2,1,0:T(8,128)S(1)} %get-tuple-element.37), channel_id=1, source_target_pairs={{0,2},{1,3},{2,0},{3,1},{4,6},{5,7},{6,4},{7,5},{8,10},{9,11},{10,... | collective-permute-start | bytes 221192 | tf_op jit(solution)/shard_map/ppermute | solution.py:226
  88.7 5.8 %collective-permute-start.9 = (bf16[2,8,96,512]{3,2,1,0:T(8,128)(2,1)}, bf16[2,8,96,512]{3,2,1,0:T(8,128)(2,1)S(1)}, u32[]{:S(2)}, u32[]{:S(2)}) collective-permute-start(bf16[2,8,96,512]{3,2,1,0:T(8,128)(2,1)} %collective-permute-done.8.refs_4_), channel_id=1, source_target_pairs={{0,4},{8,12},{16,20},{24,28},{1,5},{9,13},{17,21},{25,29},{2,6},{1... | collective-permute-start | bytes 4718600 | tf_op jit(solution)/shard_map/ppermute | solution.py:217
  90.1 9.5 %collective-permute-start.5 = (f32[3,48,128]{2,1,0:T(8,128)S(1)}, f32[3,48,128]{2,1,0:T(8,128)S(1)}, u32[]{:S(2)}, u32[]{:S(2)}) collective-permute-start(f32[3,48,128]{2,1,0:T(8,128)S(1)} %get-tuple-element.36), channel_id=1, source_target_pairs={{0,1},{1,2},{2,3},{3,0},{4,5},{5,6},{6,7},{7,4},{8,9},{9,10},{10,1... | collective-permute-start | bytes 221192 | tf_op jit(solution)/shard_map/ppermute | solution.py:226
  91.8 7.8 %collective-permute-start.7 = (f32[3,48,128]{2,1,0:T(8,128)S(1)}, f32[3,48,128]{2,1,0:T(8,128)S(1)}, u32[]{:S(2)}, u32[]{:S(2)}) collective-permute-start(f32[3,48,128]{2,1,0:T(8,128)S(1)} %get-tuple-element.38), channel_id=1, source_target_pairs={{0,3},{1,0},{2,1},{3,2},{4,7},{5,4},{6,5},{7,6},{8,11},{9,8},{10,9... | collective-permute-start | bytes 221192 | tf_op jit(solution)/shard_map/ppermute | solution.py:226
  99.6 8.8 %collective-permute-start.11 = (f32[3,96,128]{2,1,0:T(8,128)S(1)}, f32[3,96,128]{2,1,0:T(8,128)S(1)}, u32[]{:S(2)}, u32[]{:S(2)}) collective-permute-start(f32[3,96,128]{2,1,0:T(8,128)S(1)} %get-tuple-element.45), channel_id=1, source_target_pairs={{0,2},{1,3},{2,0},{3,1},{4,6},{5,7},{6,4},{7,5},{8,10},{9,11},{10,... | collective-permute-start | bytes 442376 | tf_op jit(solution)/shard_map/ppermute | solution.py:226
  108.4 5.6 %collective-permute-start.14 = (bf16[2,8,112,512]{3,2,1,0:T(8,128)(2,1)S(1)}, bf16[2,8,112,512]{3,2,1,0:T(8,128)(2,1)S(1)}, u32[]{:S(2)}, u32[]{:S(2)}) collective-permute-start(bf16[2,8,112,512]{3,2,1,0:T(8,128)(2,1)S(1)} %collective-permute-done.13.refs_4_), channel_id=1, source_target_pairs={{0,4},{8,12},{16,20},{24,28},{1,5},{9,13},{17,21},{25,29},{2,6},{1... | collective-permute-start | bytes 5505032 | tf_op jit(solution)/shard_map/ppermute | solution.py:217
  109.8 9.4 %collective-permute-start.12 = (f32[3,96,128]{2,1,0:T(8,128)S(1)}, f32[3,96,128]{2,1,0:T(8,128)S(1)}, u32[]{:S(2)}, u32[]{:S(2)}) collective-permute-start(f32[3,96,128]{2,1,0:T(8,128)S(1)} %get-tuple-element.47), channel_id=1, source_target_pairs={{0,3},{1,0},{2,1},{3,2},{4,7},{5,4},{6,5},{7,6},{8,11},{9,8},{10,9... | collective-permute-start | bytes 442376 | tf_op jit(solution)/shard_map/ppermute | solution.py:226
  114.0 6.9 %collective-permute-start.10 = (f32[3,96,128]{2,1,0:T(8,128)S(1)}, f32[3,96,128]{2,1,0:T(8,128)S(1)}, u32[]{:S(2)}, u32[]{:S(2)}) collective-permute-start(f32[3,96,128]{2,1,0:T(8,128)S(1)} %get-tuple-element.43), channel_id=1, source_target_pairs={{0,1},{1,2},{2,3},{3,0},{4,5},{5,6},{6,7},{7,4},{8,9},{9,10},{10,1... | collective-permute-start | bytes 442376 | tf_op jit(solution)/shard_map/ppermute | solution.py:226
  120.9 7.0 %collective-permute-start.17 = (f32[3,112,128]{2,1,0:T(8,128)S(1)}, f32[3,112,128]{2,1,0:T(8,128)S(1)}, u32[]{:S(2)}, u32[]{:S(2)}) collective-permute-start(f32[3,112,128]{2,1,0:T(8,128)S(1)} %get-tuple-element.56), channel_id=1, source_target_pairs={{0,3},{1,0},{2,1},{3,2},{4,7},{5,4},{6,5},{7,6},{8,11},{9,8},{10,9... | collective-permute-start | bytes 516104 | tf_op jit(solution)/shard_map/ppermute | solution.py:226
  123.1 15.0 %collective-permute-start.16 = (f32[3,112,128]{2,1,0:T(8,128)S(1)}, f32[3,112,128]{2,1,0:T(8,128)S(1)}, u32[]{:S(2)}, u32[]{:S(2)}) collective-permute-start(f32[3,112,128]{2,1,0:T(8,128)S(1)} %get-tuple-element.54), channel_id=1, source_target_pairs={{0,2},{1,3},{2,0},{3,1},{4,6},{5,7},{6,4},{7,5},{8,10},{9,11},{10,... | collective-permute-start | bytes 516104 | tf_op jit(solution)/shard_map/ppermute | solution.py:226
  123.7 14.4 %collective-permute-start.15 = (f32[3,112,128]{2,1,0:T(8,128)S(1)}, f32[3,112,128]{2,1,0:T(8,128)S(1)}, u32[]{:S(2)}, u32[]{:S(2)}) collective-permute-start(f32[3,112,128]{2,1,0:T(8,128)S(1)} %get-tuple-element.52), channel_id=1, source_target_pairs={{0,1},{1,2},{2,3},{3,0},{4,5},{5,6},{6,7},{7,4},{8,9},{9,10},{10,1... | collective-permute-start | bytes 516104 | tf_op jit(solution)/shard_map/ppermute | solution.py:226

commit v3 on v2

--- a/solution.py
+++ b/solution.py
@@ -202,9 +202,10 @@
     live = lax.broadcasted_iota(jnp.int32, (blocks, slots), 1) < pair_count[:, None]
     places = jnp.concatenate([jnp.where(live, source, -1).reshape(-1), lax.rem(relative, blocks).reshape(-1)])
     places = jnp.concatenate([places, lax.axis_index("aux").astype(jnp.int32).reshape(1)])
-    which = jnp.where(even, 3 * core, 1 + core).astype(jnp.int32).reshape(1)
 
     one = lax.ppermute(factors, "ao", early)
+    which = after(jnp.where(even, 3 * core, 1 + core).astype(jnp.int32).reshape(1), one)
+    which = jnp.minimum(which, 3)
     mate = lax.ppermute(after(factors, places), "ao", to_core_0 + to_core_1[1::2])
     one_mate = lax.ppermute(one, "ao", to_core_0 + to_core_1[::2])
     senders = [one, in_hbm(factors), mate]
@@ -213,7 +214,7 @@
     twos, made, terms, marks = [], [], [], [mark(sent[-1], 10**12)]
     for turn, piece in enumerate(PIECES):
         twos.append(lax.ppermute(after(sent[turn], *made[: max(turn - 1, 0)][-1:]), "ao", late))
-        earlier = terms[-parts // 2 : 1 - parts // 2] if turn else []
+        earlier = terms[1 - parts : 2 - parts] if turn else []
         two_mate = lax.ppermute(after(twos[turn], marks[turn], *earlier), "ao", to_core_1)
         columns = [factors, mate, one, one_mate, twos[turn], two_mate]
         products = pair_products(places, marks[turn], factors, columns, piece, parts, slots)

time: 139 us -> 136 us (0.978); the launches traced: 139 us -> 134 us
  starting transfers between devices: 37.3 us -> 34.1 us
  waiting for transfers between devices: 79.5 us -> 77.2 us
    ppermute x3, waiting for transfers between devices: 4.14 us -> 7.35 us  [squares(): lax.ppermute(after(sent[turn], *made[:max(turn - 1, 0)][-1:]), 'ao', late)]
    ppermute x1, waiting for transfers between devices: 3.2 us -> 0.01 us  [squares(): lax.ppermute(after(factors, places), 'ao', to_core_0 + to_core_1[1::2])]
    ppermute x9, waiting for transfers between devices: 24.9 us -> 21.7 us  [squares(): lax.ppermute(after(products[step], *others), 'aux', [(z, (z + step) % par...]
    ppermute x3, starting transfers between devices: 9.46 us -> 7.78 us  [squares(): lax.ppermute(after(sent[turn], *made[:max(turn - 1, 0)][-1:]), 'ao', late)]
    ppermute x9, starting transfers between devices: 15.6 us -> 14.2 us  [squares(): lax.ppermute(after(products[step], *others), 'aux', [(z, (z + step) % par...]
  transfers between devices with their start and end apart: 18 -> 18, of which waited for: 10 -> 10; matrix products, arithmetic and copies ran while one was open for 0% -> 1% of each run, Pallas kernels for 13% -> 14%
where the time goes in v3:
time: 136 us; the launch traced here: 134 us
  waiting for transfers between devices  77.2 us (57%)
  starting transfers between devices  34.1 us (25%)
  Pallas kernels  21.7 us (16%)
    ppermute x1, waiting for transfers between devices, squares(): one = lax.ppermute(factors, 'ao', early)  44.4 us
    ppermute x9, waiting for transfers between devices, squares(): lax.ppermute(after(products[step], *others), 'aux', [(z, (z + step) % par...  21.7 us
    pallas_call x3, Pallas kernels, pair_products(): pl.pallas_call(functools.partial(pair_kernel, slots, first, wide, parts),...  15.3 us
    ppermute x9, starting transfers between devices, squares(): lax.ppermute(after(products[step], *others), 'aux', [(z, (z + step) % par...  14.2 us
    ppermute x3, starting transfers between devices, squares(): lax.ppermute(after(sent[turn], *made[:max(turn - 1, 0)][-1:]), 'ao', late)  7.78 us
    ppermute x3, waiting for transfers between devices, squares(): lax.ppermute(after(sent[turn], *made[:max(turn - 1, 0)][-1:]), 'ao', late)  7.35 us
    pallas_call x2, Pallas kernels, pack(): pl.pallas_call(functools.partial(pack_kernel, pieces), in_specs=[pl.Block...  5.52 us
    ppermute x1, starting transfers between devices, squares(): one = lax.ppermute(factors, 'ao', early)  4.87 us
  transfers between devices with their start and end apart: 18, of which 10 were waited for; matrix products, arithmetic and copies ran while one was open for 1% of the time, Pallas kernels for 14%

profile of v3, /device:TPU:0, one launch (start us, length us, event | category | flops | bytes accessed | tf_op | source)
XLA Modules:
  0.0 134.3 jit_solution(17164939286632134641)
XLA Ops:
  0.0 4.9 %collective-permute-start = (bf16[2,8,256,512]{3,2,1,0:T(8,128)(2,1)}, bf16[2,8,256,512]{3,2,1,0:T(8,128)(2,1)}, u32[]{:S(2)}, u32[]{:S(2)}) collective-permute-start(bf16[2,8,256,512]{3,2,1,0:T(8,128)(2,1)} %refs_0_.5), channel_id=1, source_target_pairs={{16,0},{12,4},{20,12},{0,16},{28,20},{4,28},{17,1},{13,5},{21,13},... | collective-permute-start | bytes 12582920 | tf_op jit(solution)/shard_map/ppermute | solution.py:206
  5.9 1.3 collective-permute-start.1
  7.2 44.4 %collective-permute-done.refs_0_.refs_2_ = bf16[2,8,256,512]{3,2,1,0:T(8,128)(2,1)} collective-permute-done((bf16[2,8,256,512]{3,2,1,0:T(8,128)(2,1)}, bf16[2,8,256,512]{3,2,1,0:T(8,128)(2,1)}, u32[]{:S(2)}, u32[]{:S(2)}) %collective-permute-start) | collective-permute-done | bytes 4194336 | tf_op jit(solution)/shard_map/ppermute | solution.py:206
  51.7 2.2 %pack_ranges.2 = bf16[2,8,48,512]{3,2,1,0:T(8,128)(2,1)} custom-call(s32[1]{0:T(128)S(6)} %min.3.which, bf16[2,8,256,512]{3,2,1,0:T(8,128)(2,1)} %collective-permute-done.refs_0_.refs_2_, bf16[2,8,256,512]{3,2,1,0:T(8,128)(2,1)} %refs_0_.5, bf16[2,8,256,512]{3,2,1,0:T(8,128)(2,1)} %collective-permute-done.1.refs_2_.refs_1_), custom_call_target="tpu_custom_call" | custom-call | bytes 1048576 | tf_op jit(solution)/shard_map/pack_ranges/pallas_call | solution.py:50
  53.8 1.9 %collective-permute-start.3 = (bf16[2,8,48,512]{3,2,1,0:T(8,128)(2,1)}, bf16[2,8,48,512]{3,2,1,0:T(8,128)(2,1)}, u32[]{:S(2)}, u32[]{:S(2)}) collective-permute-start(bf16[2,8,48,512]{3,2,1,0:T(8,128)(2,1)} %pack_ranges.2), channel_id=1, source_target_pairs={{0,8},{8,0},{28,12},{16,24},{24,16},{12,28},{1,9},{9,1},{29,13},{1... | collective-permute-start | bytes 2359304 | tf_op jit(solution)/shard_map/ppermute | solution.py:216
  55.8 3.3 %pack_ranges.3 = (bf16[2,8,96,512]{3,2,1,0:T(8,128)(2,1)}, bf16[2,8,112,512]{3,2,1,0:T(8,128)(2,1)S(1)}) custom-call(s32[1]{0:T(128)S(6)} %min.3.which, bf16[2,8,256,512]{3,2,1,0:T(8,128)(2,1)} %collective-permute-done.refs_0_.refs_2_, bf16[2,8,256,512]{3,2,1,0:T(8,128)(2,1)} %refs_0_.5, bf16[2,8,256,512]{3,2,1,0:T(8,128)(2,1)} %collective-permute-done.1.refs_2_.refs_1_), custom_call_target="tpu_custom_call" | custom-call | bytes 1048576 | tf_op jit(solution)/shard_map/pack_ranges/pallas_call | solution.py:50
  59.1 3.9 %collective-permute-start.8 = (bf16[2,8,96,512]{3,2,1,0:T(8,128)(2,1)}, bf16[2,8,96,512]{3,2,1,0:T(8,128)(2,1)}, u32[]{:S(2)}, u32[]{:S(2)}) collective-permute-start(bf16[2,8,96,512]{3,2,1,0:T(8,128)(2,1)} %get-tuple-element.41), channel_id=1, source_target_pairs={{0,8},{8,0},{28,12},{16,24},{24,16},{12,28},{1,9},{9,1},{29,13},{1... | collective-permute-start | bytes 4718600 | tf_op jit(solution)/shard_map/ppermute | solution.py:216
  63.1 1.9 %collective-permute-start.2 = (bf16[2,8,256,512]{3,2,1,0:T(8,128)(2,1)}, bf16[2,8,256,512]{3,2,1,0:T(8,128)(2,1)}, u32[]{:S(2)}, u32[]{:S(2)}) collective-permute-start(bf16[2,8,256,512]{3,2,1,0:T(8,128)(2,1)} %collective-permute-done.refs_0_.refs_2_), channel_id=1, source_target_pairs={{4,0},{12,8},{20,16},{28,24},{0,4},{16,20},{5,1},{13,9},{21,17},{2... | collective-permute-start | bytes 12582920 | tf_op jit(solution)/shard_map/ppermute | solution.py:210
  65.0 3.0 %collective-permute-done.3.refs_4_ = bf16[2,8,48,512]{3,2,1,0:T(8,128)(2,1)} collective-permute-done((bf16[2,8,48,512]{3,2,1,0:T(8,128)(2,1)}, bf16[2,8,48,512]{3,2,1,0:T(8,128)(2,1)}, u32[]{:S(2)}, u32[]{:S(2)}) %collective-permute-start.3) | collective-permute-done | bytes 786464 | tf_op jit(solution)/shard_map/ppermute | solution.py:216
  68.0 1.3 collective-permute-start.4
  69.4 3.7 %collective-permute-done.4.refs_5_ = bf16[2,8,48,512]{3,2,1,0:T(8,128)(2,1)S(1)} collective-permute-done((bf16[2,8,48,512]{3,2,1,0:T(8,128)(2,1)}, bf16[2,8,48,512]{3,2,1,0:T(8,128)(2,1)S(1)}, u32[]{:S(2)}, u32[]{:S(2)}) %collective-permute-start.4) | collective-permute-done | bytes 786464 | tf_op jit(solution)/shard_map/ppermute | solution.py:218
  73.1 4.5 %pair_products.3 = (f32[3,48,128]{2,1,0:T(8,128)S(1)}, f32[3,48,128]{2,1,0:T(8,128)S(1)}, f32[3,48,128]{2,1,0:T(8,128)S(1)}, f32[3,48,128]{2,1,0:T(8,128)S(1)}) custom-call(s32[13]{0:T(128)S(1)} %pad_add_fusion.places, f32[8,128]{1,0:T(8,128)S(1)} %mark.3.unread, bf16[2,8,256,512]{3,2,1,0:T(8,128)(2,1)} %refs_0_.5, bf16[2,8,256,512]{3,2,1,0:T(8,128)(2,1)} %refs_0_.5, ...), custom_call_target="tpu_custom_call" | custom-call | bytes 1048576 | tf_op jit(solution)/shard_map/pair_products/pallas_call | solution.py:133
  77.7 1.9 %collective-permute-start.13 = (bf16[2,8,112,512]{3,2,1,0:T(8,128)(2,1)S(1)}, bf16[2,8,112,512]{3,2,1,0:T(8,128)(2,1)S(1)}, u32[]{:S(2)}, u32[]{:S(2)}) collective-permute-start(bf16[2,8,112,512]{3,2,1,0:T(8,128)(2,1)S(1)} %get-tuple-element.50.value), channel_id=1, source_target_pairs={{0,8},{8,0},{28,12},{16,24},{24,16},{12,28},{1,9},{9,1},{29,13},{1... | collective-permute-start | bytes 5505032 | tf_op jit(solution)/shard_map/ppermute | solution.py:216
  79.6 2.1 %collective-permute-start.5 = (f32[3,48,128]{2,1,0:T(8,128)S(1)}, f32[3,48,128]{2,1,0:T(8,128)S(1)}, u32[]{:S(2)}, u32[]{:S(2)}) collective-permute-start(f32[3,48,128]{2,1,0:T(8,128)S(1)} %get-tuple-element.38), channel_id=1, source_target_pairs={{0,1},{1,2},{2,3},{3,0},{4,5},{5,6},{6,7},{7,4},{8,9},{9,10},{10,1... | collective-permute-start | bytes 221192 | tf_op jit(solution)/shard_map/ppermute | solution.py:227
  81.7 3.2 %collective-permute-done.8.refs_4_ = bf16[2,8,96,512]{3,2,1,0:T(8,128)(2,1)} collective-permute-done((bf16[2,8,96,512]{3,2,1,0:T(8,128)(2,1)}, bf16[2,8,96,512]{3,2,1,0:T(8,128)(2,1)}, u32[]{:S(2)}, u32[]{:S(2)}) %collective-permute-start.8) | collective-permute-done | bytes 1572896 | tf_op jit(solution)/shard_map/ppermute | solution.py:216
  84.9 1.2 collective-permute-done.5.refs_1_
  86.1 1.4 %collective-permute-start.9 = (bf16[2,8,96,512]{3,2,1,0:T(8,128)(2,1)}, bf16[2,8,96,512]{3,2,1,0:T(8,128)(2,1)S(1)}, u32[]{:S(2)}, u32[]{:S(2)}) collective-permute-start(bf16[2,8,96,512]{3,2,1,0:T(8,128)(2,1)} %collective-permute-done.8.refs_4_), channel_id=1, source_target_pairs={{0,4},{8,12},{16,20},{24,28},{1,5},{9,13},{17,21},{25,29},{2,6},{1... | collective-permute-start | bytes 4718600 | tf_op jit(solution)/shard_map/ppermute | solution.py:218
  87.5 1.9 %collective-permute-start.6 = (f32[3,48,128]{2,1,0:T(8,128)S(1)}, f32[3,48,128]{2,1,0:T(8,128)S(1)}, u32[]{:S(2)}, u32[]{:S(2)}) collective-permute-start(f32[3,48,128]{2,1,0:T(8,128)S(1)} %get-tuple-element.39), channel_id=1, source_target_pairs={{0,2},{1,3},{2,0},{3,1},{4,6},{5,7},{6,4},{7,5},{8,10},{9,11},{10,... | collective-permute-start | bytes 221192 | tf_op jit(solution)/shard_map/ppermute | solution.py:227
  89.4 1.3 %collective-permute-start.7 = (f32[3,48,128]{2,1,0:T(8,128)S(1)}, f32[3,48,128]{2,1,0:T(8,128)S(1)}, u32[]{:S(2)}, u32[]{:S(2)}) collective-permute-start(f32[3,48,128]{2,1,0:T(8,128)S(1)} %get-tuple-element.40), channel_id=1, source_target_pairs={{0,3},{1,0},{2,1},{3,2},{4,7},{5,4},{6,5},{7,6},{8,11},{9,8},{10,9... | collective-permute-start | bytes 221192 | tf_op jit(solution)/shard_map/ppermute | solution.py:227
  90.8 5.3 %pair_products.4 = (f32[3,96,128]{2,1,0:T(8,128)S(1)}, f32[3,96,128]{2,1,0:T(8,128)S(1)}, f32[3,96,128]{2,1,0:T(8,128)S(1)}, f32[3,96,128]{2,1,0:T(8,128)S(1)}) custom-call(s32[13]{0:T(128)S(1)} %pad_add_fusion.places, f32[8,128]{1,0:T(8,128)S(1)} %mark.4.unread, bf16[2,8,256,512]{3,2,1,0:T(8,128)(2,1)} %refs_0_.5, bf16[2,8,256,512]{3,2,1,0:T(8,128)(2,1)} %refs_0_.5, ...), custom_call_target="tpu_custom_call" | custom-call | bytes 1048576 | tf_op jit(solution)/shard_map/pair_products/pallas_call | solution.py:133
  96.1 0.8 collective-permute-start.10
  96.9 6.4 %collective-permute-done.10.refs_5_ = f32[3,96,128]{2,1,0:T(8,128)S(1)} collective-permute-done((f32[3,96,128]{2,1,0:T(8,128)S(1)}, f32[3,96,128]{2,1,0:T(8,128)S(1)}, u32[]{:S(2)}, u32[]{:S(2)}) %collective-permute-start.10) | collective-permute-done | bytes 147488 | tf_op jit(solution)/shard_map/ppermute | solution.py:227
  103.3 1.2 collective-permute-done.13.refs_4_
  104.5 1.4 %collective-permute-start.14 = (bf16[2,8,112,512]{3,2,1,0:T(8,128)(2,1)S(1)}, bf16[2,8,112,512]{3,2,1,0:T(8,128)(2,1)S(1)}, u32[]{:S(2)}, u32[]{:S(2)}) collective-permute-start(bf16[2,8,112,512]{3,2,1,0:T(8,128)(2,1)S(1)} %collective-permute-done.13.refs_4_), channel_id=1, source_target_pairs={{0,4},{8,12},{16,20},{24,28},{1,5},{9,13},{17,21},{25,29},{2,6},{1... | collective-permute-start | bytes 5505032 | tf_op jit(solution)/shard_map/ppermute | solution.py:218
  105.9 4.1 %collective-permute-start.12 = (f32[3,96,128]{2,1,0:T(8,128)S(1)}, f32[3,96,128]{2,1,0:T(8,128)S(1)}, u32[]{:S(2)}, u32[]{:S(2)}) collective-permute-start(f32[3,96,128]{2,1,0:T(8,128)S(1)} %get-tuple-element.49), channel_id=1, source_target_pairs={{0,3},{1,0},{2,1},{3,2},{4,7},{5,4},{6,5},{7,6},{8,11},{9,8},{10,9... | collective-permute-start | bytes 442376 | tf_op jit(solution)/shard_map/ppermute | solution.py:227
  110.0 5.5 %pair_products.5 = (f32[3,112,128]{2,1,0:T(8,128)S(1)}, f32[3,112,128]{2,1,0:T(8,128)S(1)}, f32[3,112,128]{2,1,0:T(8,128)S(1)}, f32[3,112,128]{2,1,0:T(8,128)S(1)}) custom-call(s32[13]{0:T(128)S(1)} %pad_add_fusion.places, f32[8,128]{1,0:T(8,128)S(1)} %mark.5.unread, bf16[2,8,256,512]{3,2,1,0:T(8,128)(2,1)} %refs_0_.5, bf16[2,8,256,512]{3,2,1,0:T(8,128)(2,1)} %refs_0_.5, ...), custom_call_target="tpu_custom_call" | custom-call | bytes 1048576 | tf_op jit(solution)/shard_map/pair_products/pallas_call | solution.py:133
  115.5 1.2 collective-permute-done.11.refs_6_
  116.7 2.9 %collective-permute-start.17 = (f32[3,112,128]{2,1,0:T(8,128)S(1)}, f32[3,112,128]{2,1,0:T(8,128)S(1)}, u32[]{:S(2)}, u32[]{:S(2)}) collective-permute-start(f32[3,112,128]{2,1,0:T(8,128)S(1)} %get-tuple-element.58), channel_id=1, source_target_pairs={{0,3},{1,0},{2,1},{3,2},{4,7},{5,4},{6,5},{7,6},{8,11},{9,8},{10,9... | collective-permute-start | bytes 516104 | tf_op jit(solution)/shard_map/ppermute | solution.py:227
  119.7 0.8 collective-permute-start.15
  120.5 4.0 %collective-permute-done.17.refs_11_ = f32[3,112,128]{2,1,0:T(8,128)S(1)} collective-permute-done((f32[3,112,128]{2,1,0:T(8,128)S(1)}, f32[3,112,128]{2,1,0:T(8,128)S(1)}, u32[]{:S(2)}, u32[]{:S(2)}) %collective-permute-start.17) | collective-permute-done | bytes 172064 | tf_op jit(solution)/shard_map/ppermute | solution.py:227
  124.5 8.8 %collective-permute-done.16.refs_10_ = f32[3,112,128]{2,1,0:T(8,128)S(1)} collective-permute-done((f32[3,112,128]{2,1,0:T(8,128)S(1)}, f32[3,112,128]{2,1,0:T(8,128)S(1)}, u32[]{:S(2)}, u32[]{:S(2)}) %collective-permute-start.16) | collective-permute-done | bytes 172064 | tf_op jit(solution)/shard_map/ppermute | solution.py:227
  133.4 0.9 sum_terms.1
  (18 shorter events, 1.1 us)
Async XLA Ops:
  0.0 51.7 %collective-permute-start = (bf16[2,8,256,512]{3,2,1,0:T(8,128)(2,1)}, bf16[2,8,256,512]{3,2,1,0:T(8,128)(2,1)}, u32[]{:S(2)}, u32[]{:S(2)}) collective-permute-start(bf16[2,8,256,512]{3,2,1,0:T(8,128)(2,1)} %refs_0_.5), channel_id=1, source_target_pairs={{16,0},{12,4},{20,12},{0,16},{28,20},{4,28},{17,1},{13,5},{21,13},... | collective-permute-start | bytes 12582920 | tf_op jit(solution)/shard_map/ppermute | solution.py:206
  5.9 45.8 %collective-permute-start.1 = (bf16[2,8,256,512]{3,2,1,0:T(8,128)(2,1)}, bf16[2,8,256,512]{3,2,1,0:T(8,128)(2,1)}, u32[]{:S(2)}, u32[]{:S(2)}) collective-permute-start(bf16[2,8,256,512]{3,2,1,0:T(8,128)(2,1)} %refs_0_.5), channel_id=1, source_target_pairs={{4,0},{12,8},{20,16},{28,24},{8,12},{24,28},{5,1},{13,9},{21,17},{... | collective-permute-start | bytes 12582920 | tf_op jit(solution)/shard_map/ppermute | solution.py:209
  53.8 14.2 %collective-permute-start.3 = (bf16[2,8,48,512]{3,2,1,0:T(8,128)(2,1)}, bf16[2,8,48,512]{3,2,1,0:T(8,128)(2,1)}, u32[]{:S(2)}, u32[]{:S(2)}) collective-permute-start(bf16[2,8,48,512]{3,2,1,0:T(8,128)(2,1)} %pack_ranges.2), channel_id=1, source_target_pairs={{0,8},{8,0},{28,12},{16,24},{24,16},{12,28},{1,9},{9,1},{29,13},{1... | collective-permute-start | bytes 2359304 | tf_op jit(solution)/shard_map/ppermute | solution.py:216
  59.1 25.8 %collective-permute-start.8 = (bf16[2,8,96,512]{3,2,1,0:T(8,128)(2,1)}, bf16[2,8,96,512]{3,2,1,0:T(8,128)(2,1)}, u32[]{:S(2)}, u32[]{:S(2)}) collective-permute-start(bf16[2,8,96,512]{3,2,1,0:T(8,128)(2,1)} %get-tuple-element.41), channel_id=1, source_target_pairs={{0,8},{8,0},{28,12},{16,24},{24,16},{12,28},{1,9},{9,1},{29,13},{1... | collective-permute-start | bytes 4718600 | tf_op jit(solution)/shard_map/ppermute | solution.py:216
  63.1 10.0 %collective-permute-start.2 = (bf16[2,8,256,512]{3,2,1,0:T(8,128)(2,1)}, bf16[2,8,256,512]{3,2,1,0:T(8,128)(2,1)}, u32[]{:S(2)}, u32[]{:S(2)}) collective-permute-start(bf16[2,8,256,512]{3,2,1,0:T(8,128)(2,1)} %collective-permute-done.refs_0_.refs_2_), channel_id=1, source_target_pairs={{4,0},{12,8},{20,16},{28,24},{0,4},{16,20},{5,1},{13,9},{21,17},{2... | collective-permute-start | bytes 12582920 | tf_op jit(solution)/shard_map/ppermute | solution.py:210
  68.0 5.1 %collective-permute-start.4 = (bf16[2,8,48,512]{3,2,1,0:T(8,128)(2,1)}, bf16[2,8,48,512]{3,2,1,0:T(8,128)(2,1)S(1)}, u32[]{:S(2)}, u32[]{:S(2)}) collective-permute-start(bf16[2,8,48,512]{3,2,1,0:T(8,128)(2,1)} %collective-permute-done.3.refs_4_), channel_id=1, source_target_pairs={{0,4},{8,12},{16,20},{24,28},{1,5},{9,13},{17,21},{25,29},{2,6},{1... | collective-permute-start | bytes 2359304 | tf_op jit(solution)/shard_map/ppermute | solution.py:218
  77.7 26.8 %collective-permute-start.13 = (bf16[2,8,112,512]{3,2,1,0:T(8,128)(2,1)S(1)}, bf16[2,8,112,512]{3,2,1,0:T(8,128)(2,1)S(1)}, u32[]{:S(2)}, u32[]{:S(2)}) collective-permute-start(bf16[2,8,112,512]{3,2,1,0:T(8,128)(2,1)S(1)} %get-tuple-element.50.value), channel_id=1, source_target_pairs={{0,8},{8,0},{28,12},{16,24},{24,16},{12,28},{1,9},{9,1},{29,13},{1... | collective-permute-start | bytes 5505032 | tf_op jit(solution)/shard_map/ppermute | solution.py:216
  79.6 6.5 %collective-permute-start.5 = (f32[3,48,128]{2,1,0:T(8,128)S(1)}, f32[3,48,128]{2,1,0:T(8,128)S(1)}, u32[]{:S(2)}, u32[]{:S(2)}) collective-permute-start(f32[3,48,128]{2,1,0:T(8,128)S(1)} %get-tuple-element.38), channel_id=1, source_target_pairs={{0,1},{1,2},{2,3},{3,0},{4,5},{5,6},{6,7},{7,4},{8,9},{9,10},{10,1... | collective-permute-start | bytes 221192 | tf_op jit(solution)/shard_map/ppermute | solution.py:227
  86.1 4.7 %collective-permute-start.9 = (bf16[2,8,96,512]{3,2,1,0:T(8,128)(2,1)}, bf16[2,8,96,512]{3,2,1,0:T(8,128)(2,1)S(1)}, u32[]{:S(2)}, u32[]{:S(2)}) collective-permute-start(bf16[2,8,96,512]{3,2,1,0:T(8,128)(2,1)} %collective-permute-done.8.refs_4_), channel_id=1, source_target_pairs={{0,4},{8,12},{16,20},{24,28},{1,5},{9,13},{17,21},{25,29},{2,6},{1... | collective-permute-start | bytes 4718600 | tf_op jit(solution)/shard_map/ppermute | solution.py:218
  87.5 8.6 %collective-permute-start.6 = (f32[3,48,128]{2,1,0:T(8,128)S(1)}, f32[3,48,128]{2,1,0:T(8,128)S(1)}, u32[]{:S(2)}, u32[]{:S(2)}) collective-permute-start(f32[3,48,128]{2,1,0:T(8,128)S(1)} %get-tuple-element.39), channel_id=1, source_target_pairs={{0,2},{1,3},{2,0},{3,1},{4,6},{5,7},{6,4},{7,5},{8,10},{9,11},{10,... | collective-permute-start | bytes 221192 | tf_op jit(solution)/shard_map/ppermute | solution.py:227
  89.4 6.7 %collective-permute-start.7 = (f32[3,48,128]{2,1,0:T(8,128)S(1)}, f32[3,48,128]{2,1,0:T(8,128)S(1)}, u32[]{:S(2)}, u32[]{:S(2)}) collective-permute-start(f32[3,48,128]{2,1,0:T(8,128)S(1)} %get-tuple-element.40), channel_id=1, source_target_pairs={{0,3},{1,0},{2,1},{3,2},{4,7},{5,4},{6,5},{7,6},{8,11},{9,8},{10,9... | collective-permute-start | bytes 221192 | tf_op jit(solution)/shard_map/ppermute | solution.py:227
  96.1 7.2 %collective-permute-start.10 = (f32[3,96,128]{2,1,0:T(8,128)S(1)}, f32[3,96,128]{2,1,0:T(8,128)S(1)}, u32[]{:S(2)}, u32[]{:S(2)}) collective-permute-start(f32[3,96,128]{2,1,0:T(8,128)S(1)} %get-tuple-element.45), channel_id=1, source_target_pairs={{0,1},{1,2},{2,3},{3,0},{4,5},{5,6},{6,7},{7,4},{8,9},{9,10},{10,1... | collective-permute-start | bytes 442376 | tf_op jit(solution)/shard_map/ppermute | solution.py:227
  104.5 5.6 %collective-permute-start.14 = (bf16[2,8,112,512]{3,2,1,0:T(8,128)(2,1)S(1)}, bf16[2,8,112,512]{3,2,1,0:T(8,128)(2,1)S(1)}, u32[]{:S(2)}, u32[]{:S(2)}) collective-permute-start(bf16[2,8,112,512]{3,2,1,0:T(8,128)(2,1)S(1)} %collective-permute-done.13.refs_4_), channel_id=1, source_target_pairs={{0,4},{8,12},{16,20},{24,28},{1,5},{9,13},{17,21},{25,29},{2,6},{1... | collective-permute-start | bytes 5505032 | tf_op jit(solution)/shard_map/ppermute | solution.py:218
  105.9 9.6 %collective-permute-start.12 = (f32[3,96,128]{2,1,0:T(8,128)S(1)}, f32[3,96,128]{2,1,0:T(8,128)S(1)}, u32[]{:S(2)}, u32[]{:S(2)}) collective-permute-start(f32[3,96,128]{2,1,0:T(8,128)S(1)} %get-tuple-element.49), channel_id=1, source_target_pairs={{0,3},{1,0},{2,1},{3,2},{4,7},{5,4},{6,5},{7,6},{8,11},{9,8},{10,9... | collective-permute-start | bytes 442376 | tf_op jit(solution)/shard_map/ppermute | solution.py:227
  110.0 6.7 %collective-permute-start.11 = (f32[3,96,128]{2,1,0:T(8,128)S(1)}, f32[3,96,128]{2,1,0:T(8,128)S(1)}, u32[]{:S(2)}, u32[]{:S(2)}) collective-permute-start(f32[3,96,128]{2,1,0:T(8,128)S(1)} %get-tuple-element.47), channel_id=1, source_target_pairs={{0,2},{1,3},{2,0},{3,1},{4,6},{5,7},{6,4},{7,5},{8,10},{9,11},{10,... | collective-permute-start | bytes 442376 | tf_op jit(solution)/shard_map/ppermute | solution.py:227
  116.7 7.8 %collective-permute-start.17 = (f32[3,112,128]{2,1,0:T(8,128)S(1)}, f32[3,112,128]{2,1,0:T(8,128)S(1)}, u32[]{:S(2)}, u32[]{:S(2)}) collective-permute-start(f32[3,112,128]{2,1,0:T(8,128)S(1)} %get-tuple-element.58), channel_id=1, source_target_pairs={{0,3},{1,0},{2,1},{3,2},{4,7},{5,4},{6,5},{7,6},{8,11},{9,8},{10,9... | collective-permute-start | bytes 516104 | tf_op jit(solution)/shard_map/ppermute | solution.py:227
  119.7 13.7 %collective-permute-start.16 = (f32[3,112,128]{2,1,0:T(8,128)S(1)}, f32[3,112,128]{2,1,0:T(8,128)S(1)}, u32[]{:S(2)}, u32[]{:S(2)}) collective-permute-start(f32[3,112,128]{2,1,0:T(8,128)S(1)} %get-tuple-element.56), channel_id=1, source_target_pairs={{0,2},{1,3},{2,0},{3,1},{4,6},{5,7},{6,4},{7,5},{8,10},{9,11},{10,... | collective-permute-start | bytes 516104 | tf_op jit(solution)/shard_map/ppermute | solution.py:227
  119.7 13.7 %collective-permute-start.15 = (f32[3,112,128]{2,1,0:T(8,128)S(1)}, f32[3,112,128]{2,1,0:T(8,128)S(1)}, u32[]{:S(2)}, u32[]{:S(2)}) collective-permute-start(f32[3,112,128]{2,1,0:T(8,128)S(1)} %get-tuple-element.54), channel_id=1, source_target_pairs={{0,1},{1,2},{2,3},{3,0},{4,5},{5,6},{6,7},{7,4},{8,9},{9,10},{10,1... | collective-permute-start | bytes 516104 | tf_op jit(solution)/shard_map/ppermute | solution.py:227

commit v4 on v3

--- a/solution.py
+++ b/solution.py
@@ -214,7 +214,7 @@
     twos, made, terms, marks = [], [], [], [mark(sent[-1], 10**12)]
     for turn, piece in enumerate(PIECES):
         twos.append(lax.ppermute(after(sent[turn], *made[: max(turn - 1, 0)][-1:]), "ao", late))
-        earlier = terms[1 - parts : 2 - parts] if turn else []
+        earlier = terms[1 - parts :: 2][: min(turn, 2)] if turn else []
         two_mate = lax.ppermute(after(twos[turn], marks[turn], *earlier), "ao", to_core_1)
         columns = [factors, mate, one, one_mate, twos[turn], two_mate]
         products = pair_products(places, marks[turn], factors, columns, piece, parts, slots)

time: 136 us -> 137 us (level)
  waiting for transfers between devices: 77.2 us -> 80.2 us
    ppermute x9, waiting for transfers between devices: 21.7 us -> 23.8 us  [squares(): lax.ppermute(after(products[step], *others), 'aux', [(z, (z + step) % par...]
    ppermute x3, waiting for transfers between devices: 3.72 us -> 5.56 us  [squares(): lax.ppermute(after(twos[turn], marks[turn], *earlier), 'ao', to_core_1)]
  transfers between devices with their start and end apart: 18 -> 18, of which waited for: 10 -> 11; matrix products, arithmetic and copies ran while one was open for 1% -> 1% of each run, Pallas kernels for 14% -> 13%
where the time goes in v4:
time: 137 us; the launch traced here: 136 us
  waiting for transfers between devices  80.2 us (59%)
  starting transfers between devices  33.1 us (24%)
  Pallas kernels  21.2 us (15%)
    ppermute x1, waiting for transfers between devices, squares(): one = lax.ppermute(factors, 'ao', early)  44.4 us
    ppermute x9, waiting for transfers between devices, squares(): lax.ppermute(after(products[step], *others), 'aux', [(z, (z + step) % par...  23.8 us
    pallas_call x3, Pallas kernels, pair_products(): pl.pallas_call(functools.partial(pair_kernel, slots, first, wide, parts),...  14.8 us
    ppermute x9, starting transfers between devices, squares(): lax.ppermute(after(products[step], *others), 'aux', [(z, (z + step) % par...  13.1 us
    ppermute x3, starting transfers between devices, squares(): lax.ppermute(after(sent[turn], *made[:max(turn - 1, 0)][-1:]), 'ao', late)  7.78 us
    ppermute x3, waiting for transfers between devices, squares(): lax.ppermute(after(sent[turn], *made[:max(turn - 1, 0)][-1:]), 'ao', late)  6.34 us
    ppermute x3, waiting for transfers between devices, squares(): lax.ppermute(after(twos[turn], marks[turn], *earlier), 'ao', to_core_1)  5.56 us
    pallas_call x2, Pallas kernels, pack(): pl.pallas_call(functools.partial(pack_kernel, pieces), in_specs=[pl.Block...  5.52 us
  transfers between devices with their start and end apart: 18, of which 11 were waited for; matrix products, arithmetic and copies ran while one was open for 1% of the time, Pallas kernels for 13%

profile of v4, /device:TPU:0, one launch (start us, length us, event | category | flops | bytes accessed | tf_op | source)
XLA Modules:
  0.0 135.7 jit_solution(6732057516368488482)
XLA Ops:
  0.0 4.9 %collective-permute-start = (bf16[2,8,256,512]{3,2,1,0:T(8,128)(2,1)}, bf16[2,8,256,512]{3,2,1,0:T(8,128)(2,1)}, u32[]{:S(2)}, u32[]{:S(2)}) collective-permute-start(bf16[2,8,256,512]{3,2,1,0:T(8,128)(2,1)} %refs_0_.5), channel_id=1, source_target_pairs={{16,0},{12,4},{20,12},{0,16},{28,20},{4,28},{17,1},{13,5},{21,13},... | collective-permute-start | bytes 12582920 | tf_op jit(solution)/shard_map/ppermute | solution.py:206
  4.9 0.8 compare_select_fusion.4
  5.9 1.3 collective-permute-start.1
  7.2 44.4 %collective-permute-done.refs_0_.refs_2_ = bf16[2,8,256,512]{3,2,1,0:T(8,128)(2,1)} collective-permute-done((bf16[2,8,256,512]{3,2,1,0:T(8,128)(2,1)}, bf16[2,8,256,512]{3,2,1,0:T(8,128)(2,1)}, u32[]{:S(2)}, u32[]{:S(2)}) %collective-permute-start) | collective-permute-done | bytes 4194336 | tf_op jit(solution)/shard_map/ppermute | solution.py:206
  51.7 2.2 %pack_ranges.2 = bf16[2,8,48,512]{3,2,1,0:T(8,128)(2,1)} custom-call(s32[1]{0:T(128)S(6)} %min.3.which, bf16[2,8,256,512]{3,2,1,0:T(8,128)(2,1)} %collective-permute-done.refs_0_.refs_2_, bf16[2,8,256,512]{3,2,1,0:T(8,128)(2,1)} %refs_0_.5, bf16[2,8,256,512]{3,2,1,0:T(8,128)(2,1)} %collective-permute-done.1.refs_2_.refs_1_), custom_call_target="tpu_custom_call" | custom-call | bytes 1048576 | tf_op jit(solution)/shard_map/pack_ranges/pallas_call | solution.py:50
  53.8 1.9 %collective-permute-start.3 = (bf16[2,8,48,512]{3,2,1,0:T(8,128)(2,1)}, bf16[2,8,48,512]{3,2,1,0:T(8,128)(2,1)}, u32[]{:S(2)}, u32[]{:S(2)}) collective-permute-start(bf16[2,8,48,512]{3,2,1,0:T(8,128)(2,1)} %pack_ranges.2), channel_id=1, source_target_pairs={{0,8},{8,0},{28,12},{16,24},{24,16},{12,28},{1,9},{9,1},{29,13},{1... | collective-permute-start | bytes 2359304 | tf_op jit(solution)/shard_map/ppermute | solution.py:216
  55.8 3.3 %pack_ranges.3 = (bf16[2,8,96,512]{3,2,1,0:T(8,128)(2,1)}, bf16[2,8,112,512]{3,2,1,0:T(8,128)(2,1)S(1)}) custom-call(s32[1]{0:T(128)S(6)} %min.3.which, bf16[2,8,256,512]{3,2,1,0:T(8,128)(2,1)} %collective-permute-done.refs_0_.refs_2_, bf16[2,8,256,512]{3,2,1,0:T(8,128)(2,1)} %refs_0_.5, bf16[2,8,256,512]{3,2,1,0:T(8,128)(2,1)} %collective-permute-done.1.refs_2_.refs_1_), custom_call_target="tpu_custom_call" | custom-call | bytes 1048576 | tf_op jit(solution)/shard_map/pack_ranges/pallas_call | solution.py:50
  59.1 3.9 %collective-permute-start.8 = (bf16[2,8,96,512]{3,2,1,0:T(8,128)(2,1)}, bf16[2,8,96,512]{3,2,1,0:T(8,128)(2,1)}, u32[]{:S(2)}, u32[]{:S(2)}) collective-permute-start(bf16[2,8,96,512]{3,2,1,0:T(8,128)(2,1)} %get-tuple-element.41), channel_id=1, source_target_pairs={{0,8},{8,0},{28,12},{16,24},{24,16},{12,28},{1,9},{9,1},{29,13},{1... | collective-permute-start | bytes 4718600 | tf_op jit(solution)/shard_map/ppermute | solution.py:216
  63.1 1.9 %collective-permute-start.2 = (bf16[2,8,256,512]{3,2,1,0:T(8,128)(2,1)}, bf16[2,8,256,512]{3,2,1,0:T(8,128)(2,1)}, u32[]{:S(2)}, u32[]{:S(2)}) collective-permute-start(bf16[2,8,256,512]{3,2,1,0:T(8,128)(2,1)} %collective-permute-done.refs_0_.refs_2_), channel_id=1, source_target_pairs={{4,0},{12,8},{20,16},{28,24},{0,4},{16,20},{5,1},{13,9},{21,17},{2... | collective-permute-start | bytes 12582920 | tf_op jit(solution)/shard_map/ppermute | solution.py:210
  65.0 3.0 %collective-permute-done.3.refs_4_ = bf16[2,8,48,512]{3,2,1,0:T(8,128)(2,1)} collective-permute-done((bf16[2,8,48,512]{3,2,1,0:T(8,128)(2,1)}, bf16[2,8,48,512]{3,2,1,0:T(8,128)(2,1)}, u32[]{:S(2)}, u32[]{:S(2)}) %collective-permute-start.3) | collective-permute-done | bytes 786464 | tf_op jit(solution)/shard_map/ppermute | solution.py:216
  68.0 1.3 collective-permute-start.4
  69.4 3.7 %collective-permute-done.4.refs_5_ = bf16[2,8,48,512]{3,2,1,0:T(8,128)(2,1)S(1)} collective-permute-done((bf16[2,8,48,512]{3,2,1,0:T(8,128)(2,1)}, bf16[2,8,48,512]{3,2,1,0:T(8,128)(2,1)S(1)}, u32[]{:S(2)}, u32[]{:S(2)}) %collective-permute-start.4) | collective-permute-done | bytes 786464 | tf_op jit(solution)/shard_map/ppermute | solution.py:218
  73.1 4.4 %pair_products.3 = (f32[3,48,128]{2,1,0:T(8,128)S(1)}, f32[3,48,128]{2,1,0:T(8,128)S(1)}, f32[3,48,128]{2,1,0:T(8,128)S(1)}, f32[3,48,128]{2,1,0:T(8,128)S(1)}) custom-call(s32[13]{0:T(128)S(1)} %pad_add_fusion.places, f32[8,128]{1,0:T(8,128)S(1)} %mark.3.unread, bf16[2,8,256,512]{3,2,1,0:T(8,128)(2,1)} %refs_0_.5, bf16[2,8,256,512]{3,2,1,0:T(8,128)(2,1)} %refs_0_.5, ...), custom_call_target="tpu_custom_call" | custom-call | bytes 1048576 | tf_op jit(solution)/shard_map/pair_products/pallas_call | solution.py:133
  77.5 1.9 %collective-permute-start.13 = (bf16[2,8,112,512]{3,2,1,0:T(8,128)(2,1)S(1)}, bf16[2,8,112,512]{3,2,1,0:T(8,128)(2,1)S(1)}, u32[]{:S(2)}, u32[]{:S(2)}) collective-permute-start(bf16[2,8,112,512]{3,2,1,0:T(8,128)(2,1)S(1)} %get-tuple-element.50.value), channel_id=1, source_target_pairs={{0,8},{8,0},{28,12},{16,24},{24,16},{12,28},{1,9},{9,1},{29,13},{1... | collective-permute-start | bytes 5505032 | tf_op jit(solution)/shard_map/ppermute | solution.py:216
  79.4 2.1 %collective-permute-start.5 = (f32[3,48,128]{2,1,0:T(8,128)S(1)}, f32[3,48,128]{2,1,0:T(8,128)S(1)}, u32[]{:S(2)}, u32[]{:S(2)}) collective-permute-start(f32[3,48,128]{2,1,0:T(8,128)S(1)} %get-tuple-element.38), channel_id=1, source_target_pairs={{0,1},{1,2},{2,3},{3,0},{4,5},{5,6},{6,7},{7,4},{8,9},{9,10},{10,1... | collective-permute-start | bytes 221192 | tf_op jit(solution)/shard_map/ppermute | solution.py:227
  81.6 3.3 %collective-permute-done.8.refs_4_ = bf16[2,8,96,512]{3,2,1,0:T(8,128)(2,1)} collective-permute-done((bf16[2,8,96,512]{3,2,1,0:T(8,128)(2,1)}, bf16[2,8,96,512]{3,2,1,0:T(8,128)(2,1)}, u32[]{:S(2)}, u32[]{:S(2)}) %collective-permute-start.8) | collective-permute-done | bytes 1572896 | tf_op jit(solution)/shard_map/ppermute | solution.py:216
  84.9 1.1 collective-permute-done.5.refs_1_
  86.0 1.4 %collective-permute-start.9 = (bf16[2,8,96,512]{3,2,1,0:T(8,128)(2,1)}, bf16[2,8,96,512]{3,2,1,0:T(8,128)(2,1)S(1)}, u32[]{:S(2)}, u32[]{:S(2)}) collective-permute-start(bf16[2,8,96,512]{3,2,1,0:T(8,128)(2,1)} %collective-permute-done.8.refs_4_), channel_id=1, source_target_pairs={{0,4},{8,12},{16,20},{24,28},{1,5},{9,13},{17,21},{25,29},{2,6},{1... | collective-permute-start | bytes 4718600 | tf_op jit(solution)/shard_map/ppermute | solution.py:218
  87.4 2.1 %collective-permute-start.6 = (f32[3,48,128]{2,1,0:T(8,128)S(1)}, f32[3,48,128]{2,1,0:T(8,128)S(1)}, u32[]{:S(2)}, u32[]{:S(2)}) collective-permute-start(f32[3,48,128]{2,1,0:T(8,128)S(1)} %get-tuple-element.39), channel_id=1, source_target_pairs={{0,2},{1,3},{2,0},{3,1},{4,6},{5,7},{6,4},{7,5},{8,10},{9,11},{10,... | collective-permute-start | bytes 221192 | tf_op jit(solution)/shard_map/ppermute | solution.py:227
  89.4 1.3 collective-permute-start.7
  90.8 5.0 %pair_products.4 = (f32[3,96,128]{2,1,0:T(8,128)S(1)}, f32[3,96,128]{2,1,0:T(8,128)S(1)}, f32[3,96,128]{2,1,0:T(8,128)S(1)}, f32[3,96,128]{2,1,0:T(8,128)S(1)}) custom-call(s32[13]{0:T(128)S(1)} %pad_add_fusion.places, f32[8,128]{1,0:T(8,128)S(1)} %mark.4.unread, bf16[2,8,256,512]{3,2,1,0:T(8,128)(2,1)} %refs_0_.5, bf16[2,8,256,512]{3,2,1,0:T(8,128)(2,1)} %refs_0_.5, ...), custom_call_target="tpu_custom_call" | custom-call | bytes 1048576 | tf_op jit(solution)/shard_map/pair_products/pallas_call | solution.py:133
  95.9 2.8 %collective-permute-start.12 = (f32[3,96,128]{2,1,0:T(8,128)S(1)}, f32[3,96,128]{2,1,0:T(8,128)S(1)}, u32[]{:S(2)}, u32[]{:S(2)}) collective-permute-start(f32[3,96,128]{2,1,0:T(8,128)S(1)} %get-tuple-element.49), channel_id=1, source_target_pairs={{0,3},{1,0},{2,1},{3,2},{4,7},{5,4},{6,5},{7,6},{8,11},{9,8},{10,9... | collective-permute-start | bytes 442376 | tf_op jit(solution)/shard_map/ppermute | solution.py:227
  98.7 4.3 %collective-permute-done.12.refs_7_ = f32[3,96,128]{2,1,0:T(8,128)S(1)} collective-permute-done((f32[3,96,128]{2,1,0:T(8,128)S(1)}, f32[3,96,128]{2,1,0:T(8,128)S(1)}, u32[]{:S(2)}, u32[]{:S(2)}) %collective-permute-start.12) | collective-permute-done | bytes 147488 | tf_op jit(solution)/shard_map/ppermute | solution.py:227
  102.9 3.2 %collective-permute-done.10.refs_5_ = f32[3,96,128]{2,1,0:T(8,128)S(1)} collective-permute-done((f32[3,96,128]{2,1,0:T(8,128)S(1)}, f32[3,96,128]{2,1,0:T(8,128)S(1)}, u32[]{:S(2)}, u32[]{:S(2)}) %collective-permute-start.10) | collective-permute-done | bytes 147488 | tf_op jit(solution)/shard_map/ppermute | solution.py:227
  106.2 1.4 %collective-permute-start.14 = (bf16[2,8,112,512]{3,2,1,0:T(8,128)(2,1)S(1)}, bf16[2,8,112,512]{3,2,1,0:T(8,128)(2,1)S(1)}, u32[]{:S(2)}, u32[]{:S(2)}) collective-permute-start(bf16[2,8,112,512]{3,2,1,0:T(8,128)(2,1)S(1)} %collective-permute-done.13.refs_4_), channel_id=1, source_target_pairs={{0,4},{8,12},{16,20},{24,28},{1,5},{9,13},{17,21},{25,29},{2,6},{1... | collective-permute-start | bytes 5505032 | tf_op jit(solution)/shard_map/ppermute | solution.py:218
  107.6 1.4 %collective-permute-start.11 = (f32[3,96,128]{2,1,0:T(8,128)S(1)}, f32[3,96,128]{2,1,0:T(8,128)S(1)}, u32[]{:S(2)}, u32[]{:S(2)}) collective-permute-start(f32[3,96,128]{2,1,0:T(8,128)S(1)} %get-tuple-element.47), channel_id=1, source_target_pairs={{0,2},{1,3},{2,0},{3,1},{4,6},{5,7},{6,4},{7,5},{8,10},{9,11},{10,... | collective-permute-start | bytes 442376 | tf_op jit(solution)/shard_map/ppermute | solution.py:227
  109.0 1.8 %collective-permute-done.14.refs_5_ = bf16[2,8,112,512]{3,2,1,0:T(8,128)(2,1)S(1)} collective-permute-done((bf16[2,8,112,512]{3,2,1,0:T(8,128)(2,1)S(1)}, bf16[2,8,112,512]{3,2,1,0:T(8,128)(2,1)S(1)}, u32[]{:S(2)}, u32[]{:S(2)}) %collective-permute-start.14) | collective-permute-done | bytes 1835040 | tf_op jit(solution)/shard_map/ppermute | solution.py:218
  110.8 5.3 %pair_products.5 = (f32[3,112,128]{2,1,0:T(8,128)S(1)}, f32[3,112,128]{2,1,0:T(8,128)S(1)}, f32[3,112,128]{2,1,0:T(8,128)S(1)}, f32[3,112,128]{2,1,0:T(8,128)S(1)}) custom-call(s32[13]{0:T(128)S(1)} %pad_add_fusion.places, f32[8,128]{1,0:T(8,128)S(1)} %mark.5.unread, bf16[2,8,256,512]{3,2,1,0:T(8,128)(2,1)} %refs_0_.5, bf16[2,8,256,512]{3,2,1,0:T(8,128)(2,1)} %refs_0_.5, ...), custom_call_target="tpu_custom_call" | custom-call | bytes 1048576 | tf_op jit(solution)/shard_map/pair_products/pallas_call | solution.py:133
  116.4 2.3 %collective-permute-start.17 = (f32[3,112,128]{2,1,0:T(8,128)S(1)}, f32[3,112,128]{2,1,0:T(8,128)S(1)}, u32[]{:S(2)}, u32[]{:S(2)}) collective-permute-start(f32[3,112,128]{2,1,0:T(8,128)S(1)} %get-tuple-element.58), channel_id=1, source_target_pairs={{0,3},{1,0},{2,1},{3,2},{4,7},{5,4},{6,5},{7,6},{8,11},{9,8},{10,9... | collective-permute-start | bytes 516104 | tf_op jit(solution)/shard_map/ppermute | solution.py:227
  119.7 3.8 %collective-permute-done.17.refs_11_ = f32[3,112,128]{2,1,0:T(8,128)S(1)} collective-permute-done((f32[3,112,128]{2,1,0:T(8,128)S(1)}, f32[3,112,128]{2,1,0:T(8,128)S(1)}, u32[]{:S(2)}, u32[]{:S(2)}) %collective-permute-start.17) | collective-permute-done | bytes 172064 | tf_op jit(solution)/shard_map/ppermute | solution.py:227
  123.5 11.3 %collective-permute-done.16.refs_10_ = f32[3,112,128]{2,1,0:T(8,128)S(1)} collective-permute-done((f32[3,112,128]{2,1,0:T(8,128)S(1)}, f32[3,112,128]{2,1,0:T(8,128)S(1)}, u32[]{:S(2)}, u32[]{:S(2)}) %collective-permute-start.16) | collective-permute-done | bytes 172064 | tf_op jit(solution)/shard_map/ppermute | solution.py:227
  134.8 0.9 sum_terms.1
  (18 shorter events, 1.5 us)
Async XLA Ops:
  0.0 51.7 %collective-permute-start = (bf16[2,8,256,512]{3,2,1,0:T(8,128)(2,1)}, bf16[2,8,256,512]{3,2,1,0:T(8,128)(2,1)}, u32[]{:S(2)}, u32[]{:S(2)}) collective-permute-start(bf16[2,8,256,512]{3,2,1,0:T(8,128)(2,1)} %refs_0_.5), channel_id=1, source_target_pairs={{16,0},{12,4},{20,12},{0,16},{28,20},{4,28},{17,1},{13,5},{21,13},... | collective-permute-start | bytes 12582920 | tf_op jit(solution)/shard_map/ppermute | solution.py:206
  5.9 45.8 %collective-permute-start.1 = (bf16[2,8,256,512]{3,2,1,0:T(8,128)(2,1)}, bf16[2,8,256,512]{3,2,1,0:T(8,128)(2,1)}, u32[]{:S(2)}, u32[]{:S(2)}) collective-permute-start(bf16[2,8,256,512]{3,2,1,0:T(8,128)(2,1)} %refs_0_.5), channel_id=1, source_target_pairs={{4,0},{12,8},{20,16},{28,24},{8,12},{24,28},{5,1},{13,9},{21,17},{... | collective-permute-start | bytes 12582920 | tf_op jit(solution)/shard_map/ppermute | solution.py:209
  53.8 14.2 %collective-permute-start.3 = (bf16[2,8,48,512]{3,2,1,0:T(8,128)(2,1)}, bf16[2,8,48,512]{3,2,1,0:T(8,128)(2,1)}, u32[]{:S(2)}, u32[]{:S(2)}) collective-permute-start(bf16[2,8,48,512]{3,2,1,0:T(8,128)(2,1)} %pack_ranges.2), channel_id=1, source_target_pairs={{0,8},{8,0},{28,12},{16,24},{24,16},{12,28},{1,9},{9,1},{29,13},{1... | collective-permute-start | bytes 2359304 | tf_op jit(solution)/shard_map/ppermute | solution.py:216
  59.1 25.8 %collective-permute-start.8 = (bf16[2,8,96,512]{3,2,1,0:T(8,128)(2,1)}, bf16[2,8,96,512]{3,2,1,0:T(8,128)(2,1)}, u32[]{:S(2)}, u32[]{:S(2)}) collective-permute-start(bf16[2,8,96,512]{3,2,1,0:T(8,128)(2,1)} %get-tuple-element.41), channel_id=1, source_target_pairs={{0,8},{8,0},{28,12},{16,24},{24,16},{12,28},{1,9},{9,1},{29,13},{1... | collective-permute-start | bytes 4718600 | tf_op jit(solution)/shard_map/ppermute | solution.py:216
  63.1 10.0 %collective-permute-start.2 = (bf16[2,8,256,512]{3,2,1,0:T(8,128)(2,1)}, bf16[2,8,256,512]{3,2,1,0:T(8,128)(2,1)}, u32[]{:S(2)}, u32[]{:S(2)}) collective-permute-start(bf16[2,8,256,512]{3,2,1,0:T(8,128)(2,1)} %collective-permute-done.refs_0_.refs_2_), channel_id=1, source_target_pairs={{4,0},{12,8},{20,16},{28,24},{0,4},{16,20},{5,1},{13,9},{21,17},{2... | collective-permute-start | bytes 12582920 | tf_op jit(solution)/shard_map/ppermute | solution.py:210
  68.0 5.1 %collective-permute-start.4 = (bf16[2,8,48,512]{3,2,1,0:T(8,128)(2,1)}, bf16[2,8,48,512]{3,2,1,0:T(8,128)(2,1)S(1)}, u32[]{:S(2)}, u32[]{:S(2)}) collective-permute-start(bf16[2,8,48,512]{3,2,1,0:T(8,128)(2,1)} %collective-permute-done.3.refs_4_), channel_id=1, source_target_pairs={{0,4},{8,12},{16,20},{24,28},{1,5},{9,13},{17,21},{25,29},{2,6},{1... | collective-permute-start | bytes 2359304 | tf_op jit(solution)/shard_map/ppermute | solution.py:218
  77.5 28.6 %collective-permute-start.13 = (bf16[2,8,112,512]{3,2,1,0:T(8,128)(2,1)S(1)}, bf16[2,8,112,512]{3,2,1,0:T(8,128)(2,1)S(1)}, u32[]{:S(2)}, u32[]{:S(2)}) collective-permute-start(bf16[2,8,112,512]{3,2,1,0:T(8,128)(2,1)S(1)} %get-tuple-element.50.value), channel_id=1, source_target_pairs={{0,8},{8,0},{28,12},{16,24},{24,16},{12,28},{1,9},{9,1},{29,13},{1... | collective-permute-start | bytes 5505032 | tf_op jit(solution)/shard_map/ppermute | solution.py:216
  79.4 6.5 %collective-permute-start.5 = (f32[3,48,128]{2,1,0:T(8,128)S(1)}, f32[3,48,128]{2,1,0:T(8,128)S(1)}, u32[]{:S(2)}, u32[]{:S(2)}) collective-permute-start(f32[3,48,128]{2,1,0:T(8,128)S(1)} %get-tuple-element.38), channel_id=1, source_target_pairs={{0,1},{1,2},{2,3},{3,0},{4,5},{5,6},{6,7},{7,4},{8,9},{9,10},{10,1... | collective-permute-start | bytes 221192 | tf_op jit(solution)/shard_map/ppermute | solution.py:227
  86.0 4.8 %collective-permute-start.9 = (bf16[2,8,96,512]{3,2,1,0:T(8,128)(2,1)}, bf16[2,8,96,512]{3,2,1,0:T(8,128)(2,1)S(1)}, u32[]{:S(2)}, u32[]{:S(2)}) collective-permute-start(bf16[2,8,96,512]{3,2,1,0:T(8,128)(2,1)} %collective-permute-done.8.refs_4_), channel_id=1, source_target_pairs={{0,4},{8,12},{16,20},{24,28},{1,5},{9,13},{17,21},{25,29},{2,6},{1... | collective-permute-start | bytes 4718600 | tf_op jit(solution)/shard_map/ppermute | solution.py:218
  87.4 8.5 %collective-permute-start.6 = (f32[3,48,128]{2,1,0:T(8,128)S(1)}, f32[3,48,128]{2,1,0:T(8,128)S(1)}, u32[]{:S(2)}, u32[]{:S(2)}) collective-permute-start(f32[3,48,128]{2,1,0:T(8,128)S(1)} %get-tuple-element.39), channel_id=1, source_target_pairs={{0,2},{1,3},{2,0},{3,1},{4,6},{5,7},{6,4},{7,5},{8,10},{9,11},{10,... | collective-permute-start | bytes 221192 | tf_op jit(solution)/shard_map/ppermute | solution.py:227
  89.4 6.4 %collective-permute-start.7 = (f32[3,48,128]{2,1,0:T(8,128)S(1)}, f32[3,48,128]{2,1,0:T(8,128)S(1)}, u32[]{:S(2)}, u32[]{:S(2)}) collective-permute-start(f32[3,48,128]{2,1,0:T(8,128)S(1)} %get-tuple-element.40), channel_id=1, source_target_pairs={{0,3},{1,0},{2,1},{3,2},{4,7},{5,4},{6,5},{7,6},{8,11},{9,8},{10,9... | collective-permute-start | bytes 221192 | tf_op jit(solution)/shard_map/ppermute | solution.py:227
  95.9 7.1 %collective-permute-start.12 = (f32[3,96,128]{2,1,0:T(8,128)S(1)}, f32[3,96,128]{2,1,0:T(8,128)S(1)}, u32[]{:S(2)}, u32[]{:S(2)}) collective-permute-start(f32[3,96,128]{2,1,0:T(8,128)S(1)} %get-tuple-element.49), channel_id=1, source_target_pairs={{0,3},{1,0},{2,1},{3,2},{4,7},{5,4},{6,5},{7,6},{8,11},{9,8},{10,9... | collective-permute-start | bytes 442376 | tf_op jit(solution)/shard_map/ppermute | solution.py:227
  98.7 7.5 %collective-permute-start.10 = (f32[3,96,128]{2,1,0:T(8,128)S(1)}, f32[3,96,128]{2,1,0:T(8,128)S(1)}, u32[]{:S(2)}, u32[]{:S(2)}) collective-permute-start(f32[3,96,128]{2,1,0:T(8,128)S(1)} %get-tuple-element.45), channel_id=1, source_target_pairs={{0,1},{1,2},{2,3},{3,0},{4,5},{5,6},{6,7},{7,4},{8,9},{9,10},{10,1... | collective-permute-start | bytes 442376 | tf_op jit(solution)/shard_map/ppermute | solution.py:227
  106.2 4.7 %collective-permute-start.14 = (bf16[2,8,112,512]{3,2,1,0:T(8,128)(2,1)S(1)}, bf16[2,8,112,512]{3,2,1,0:T(8,128)(2,1)S(1)}, u32[]{:S(2)}, u32[]{:S(2)}) collective-permute-start(bf16[2,8,112,512]{3,2,1,0:T(8,128)(2,1)S(1)} %collective-permute-done.13.refs_4_), channel_id=1, source_target_pairs={{0,4},{8,12},{16,20},{24,28},{1,5},{9,13},{17,21},{25,29},{2,6},{1... | collective-permute-start | bytes 5505032 | tf_op jit(solution)/shard_map/ppermute | solution.py:218
  107.6 8.8 %collective-permute-start.11 = (f32[3,96,128]{2,1,0:T(8,128)S(1)}, f32[3,96,128]{2,1,0:T(8,128)S(1)}, u32[]{:S(2)}, u32[]{:S(2)}) collective-permute-start(f32[3,96,128]{2,1,0:T(8,128)S(1)} %get-tuple-element.47), channel_id=1, source_target_pairs={{0,2},{1,3},{2,0},{3,1},{4,6},{5,7},{6,4},{7,5},{8,10},{9,11},{10,... | collective-permute-start | bytes 442376 | tf_op jit(solution)/shard_map/ppermute | solution.py:227
  116.4 7.1 %collective-permute-start.17 = (f32[3,112,128]{2,1,0:T(8,128)S(1)}, f32[3,112,128]{2,1,0:T(8,128)S(1)}, u32[]{:S(2)}, u32[]{:S(2)}) collective-permute-start(f32[3,112,128]{2,1,0:T(8,128)S(1)} %get-tuple-element.58), channel_id=1, source_target_pairs={{0,3},{1,0},{2,1},{3,2},{4,7},{5,4},{6,5},{7,6},{8,11},{9,8},{10,9... | collective-permute-start | bytes 516104 | tf_op jit(solution)/shard_map/ppermute | solution.py:227
  118.7 16.1 %collective-permute-start.16 = (f32[3,112,128]{2,1,0:T(8,128)S(1)}, f32[3,112,128]{2,1,0:T(8,128)S(1)}, u32[]{:S(2)}, u32[]{:S(2)}) collective-permute-start(f32[3,112,128]{2,1,0:T(8,128)S(1)} %get-tuple-element.56), channel_id=1, source_target_pairs={{0,2},{1,3},{2,0},{3,1},{4,6},{5,7},{6,4},{7,5},{8,10},{9,11},{10,... | collective-permute-start | bytes 516104 | tf_op jit(solution)/shard_map/ppermute | solution.py:227
  119.4 15.4 %collective-permute-start.15 = (f32[3,112,128]{2,1,0:T(8,128)S(1)}, f32[3,112,128]{2,1,0:T(8,128)S(1)}, u32[]{:S(2)}, u32[]{:S(2)}) collective-permute-start(f32[3,112,128]{2,1,0:T(8,128)S(1)} %get-tuple-element.54), channel_id=1, source_target_pairs={{0,1},{1,2},{2,3},{3,0},{4,5},{5,6},{6,7},{7,4},{8,9},{9,10},{10,1... | collective-permute-start | bytes 516104 | tf_op jit(solution)/shard_map/ppermute | solution.py:227

commit v5 on v3

--- a/solution.py
+++ b/solution.py
@@ -10,7 +10,7 @@
 LANES = 128
 PIECES = ((0, 48), (48, 96), (144, 112))
 GROUPS = 4
-KERNEL_BYTES = 14 << 20
+KERNEL_BYTES = 10 << 20
 MARK_FLOPS = 10**6
 
 
@@ -42,6 +42,22 @@
 
 def in_hbm(value):
     return pltpu.with_memory_space_constraint(value, pltpu.HBM)
+
+
+def hold_kernel(source, out, sem):
+    pltpu.async_copy(source, out, sem).wait()
+
+
+def hold(value):
+    return pl.pallas_call(
+        hold_kernel,
+        in_specs=[pl.BlockSpec(memory_space=pl.ANY)],
+        out_specs=pl.BlockSpec(memory_space=pl.ANY),
+        scratch_shapes=[pltpu.SemaphoreType.DMA],
+        out_shape=pltpu.VMEM(value.shape, value.dtype),
+        compiler_params=pltpu.CompilerParams(vmem_limit_bytes=1 << 20),
+        name="hold_rows",
+    )(in_hbm(value))
 
 
 def pack(which, sources, pieces):
@@ -59,16 +75,12 @@
     )(which, *sources)
 
 
-def pair_kernel(slots, first, wide, parts, places, unread, rows_hbm, *refs):
-    *refs, rows, held, total, row_sems, column_sems = refs
+def pair_kernel(slots, first, wide, parts, places, unread, rows, *refs):
+    *refs, held, total, column_sems = refs
     sources, outs = refs[:-parts], refs[-parts:]
     blocks, depth, height, inner = rows.shape
     count = blocks * slots
     group = depth // GROUPS
-
-    def row_copy(g):
-        part = pl.ds(g * group, group)
-        return pltpu.make_async_copy(rows_hbm.at[:, part], rows.at[:, part], row_sems.at[g])
 
     def column_copy(source, slot, g):
         part = pl.ds(g * group, group)
@@ -80,7 +92,6 @@
         )
 
     for g in range(GROUPS):
-        row_copy(g).start()
         for slot in range(count):
             for index, source in enumerate(sources):
 
@@ -89,7 +100,6 @@
                     column_copy(source, slot, g).start()
 
     for g in range(GROUPS):
-        row_copy(g).wait()
         for slot in range(count):
 
             @pl.when(places[slot] >= 0)
@@ -132,21 +142,24 @@
     shape = (count // fold, wide, height // parts * fold)
     return pl.pallas_call(
         functools.partial(pair_kernel, slots, first, wide, parts),
-        in_specs=[pl.BlockSpec(memory_space=pltpu.SMEM)] + [pl.BlockSpec(memory_space=pl.ANY)]
-        + [pl.BlockSpec(memory_space=pl.ANY)] * (1 + len(columns)),
+        in_specs=[pl.BlockSpec(memory_space=pltpu.SMEM)] + [pl.BlockSpec(memory_space=pl.ANY), pl.BlockSpec(memory_space=pltpu.VMEM)]
+        + [pl.BlockSpec(memory_space=pl.ANY)] * len(columns),
         out_specs=[pl.BlockSpec(memory_space=pltpu.VMEM)] * parts,
         scratch_shapes=[
-            pltpu.VMEM(rows.shape, rows.dtype),
             pltpu.VMEM((blocks, depth, slots * wide, inner), rows.dtype),
             pltpu.VMEM((blocks, slots * wide, height), jnp.float32),
-            pltpu.SemaphoreType.DMA((GROUPS,)),
             pltpu.SemaphoreType.DMA((count, GROUPS)),
         ],
         out_shape=[jax.ShapeDtypeStruct(shape, jnp.float32)] * parts,
         compiler_params=pltpu.CompilerParams(vmem_limit_bytes=KERNEL_BYTES),
         cost_estimate=pl.CostEstimate(flops=0, bytes_accessed=1 << 20, transcendentals=0),
         name="pair_products",
-    )(places, begun, *(in_hbm(a) if a.shape == rows.shape else a for a in (rows, *columns)))
+    )(
+        places,
+        begun,
+        pltpu.with_memory_space_constraint(rows, pltpu.VMEM),
+        *(in_hbm(a) if a.shape == rows.shape else a for a in columns),
+    )
 
 
 def sum_kernel(parts, *refs):
@@ -208,6 +221,7 @@
     which = jnp.minimum(which, 3)
     mate = lax.ppermute(after(factors, places), "ao", to_core_0 + to_core_1[1::2])
     one_mate = lax.ppermute(one, "ao", to_core_0 + to_core_1[::2])
+    rows = hold(after(factors, mate))
     senders = [one, in_hbm(factors), mate]
     sent = pack(which, senders, PIECES[:1])
     sent += pack(after(which, places, *sent), senders, PIECES[1:])
@@ -217,7 +231,7 @@
         earlier = terms[1 - parts : 2 - parts] if turn else []
         two_mate = lax.ppermute(after(twos[turn], marks[turn], *earlier), "ao", to_core_1)
         columns = [factors, mate, one, one_mate, twos[turn], two_mate]
-        products = pair_products(places, marks[turn], factors, columns, piece, parts, slots)
+        products = pair_products(places, marks[turn], rows, columns, piece, parts, slots)
         made.append(products[0])
         if turn + 1 < len(PIECES):
             marks.append(mark(products[0]))

time: 136 us -> 136 us (level)
    pallas_call x3, Pallas kernels: 15.3 us -> 12.8 us  [pair_products(): pl.pallas_call(functools.partial(pair_kernel, slots, first, wide, parts),...]
    ppermute x3, waiting for transfers between devices: 3.72 us -> 1.52 us  [squares(): lax.ppermute(after(twos[turn], marks[turn], *earlier), 'ao', to_core_1)]
    pallas_call x0 -> x1, Pallas kernels: none -> 2.2 us  [hold(): pl.pallas_call(hold_kernel, in_specs=[pl.BlockSpec(memory_space=pl.ANY)],...]
    ppermute x3, waiting for transfers between devices: 7.35 us -> 8.99 us  [squares(): lax.ppermute(after(sent[turn], *made[:max(turn - 1, 0)][-1:]), 'ao', late)]
where the time goes in v5:
time: 136 us; the launch traced here: 134 us
  waiting for transfers between devices  76.9 us (57%)
  starting transfers between devices  34.5 us (25%)
  Pallas kernels  21.4 us (16%)
    ppermute x1, waiting for transfers between devices, squares(): one = lax.ppermute(factors, 'ao', early)  44.4 us
    ppermute x9, waiting for transfers between devices, squares(): lax.ppermute(after(products[step], *others), 'aux', [(z, (z + step) % par...  21.9 us
    ppermute x9, starting transfers between devices, squares(): lax.ppermute(after(products[step], *others), 'aux', [(z, (z + step) % par...  14.5 us
    pallas_call x3, Pallas kernels, pair_products(): pl.pallas_call(functools.partial(pair_kernel, slots, first, wide, parts),...  12.8 us
    ppermute x3, waiting for transfers between devices, squares(): lax.ppermute(after(sent[turn], *made[:max(turn - 1, 0)][-1:]), 'ao', late)  8.99 us
    ppermute x3, starting transfers between devices, squares(): lax.ppermute(after(sent[turn], *made[:max(turn - 1, 0)][-1:]), 'ao', late)  7.78 us
    pallas_call x2, Pallas kernels, pack(): pl.pallas_call(functools.partial(pack_kernel, pieces), in_specs=[pl.Block...  5.52 us
    ppermute x1, starting transfers between devices, squares(): one = lax.ppermute(factors, 'ao', early)  4.87 us
  transfers between devices with their start and end apart: 18, of which 10 were waited for; matrix products, arithmetic and copies ran while one was open for 1% of the time, Pallas kernels for 14%

profile of v5, /device:TPU:0, one launch (start us, length us, event | category | flops | bytes accessed | tf_op | source)
XLA Modules:
  0.0 134.0 jit_solution(10036298165221885737)
XLA Ops:
  0.0 4.9 %collective-permute-start = (bf16[2,8,256,512]{3,2,1,0:T(8,128)(2,1)}, bf16[2,8,256,512]{3,2,1,0:T(8,128)(2,1)}, u32[]{:S(2)}, u32[]{:S(2)}) collective-permute-start(bf16[2,8,256,512]{3,2,1,0:T(8,128)(2,1)} %refs_0_.5), channel_id=1, source_target_pairs={{16,0},{12,4},{20,12},{0,16},{28,20},{4,28},{17,1},{13,5},{21,13},... | collective-permute-start | bytes 12582920 | tf_op jit(solution)/shard_map/ppermute | solution.py:219
  4.9 0.8 compare_select_fusion.4
  5.9 1.3 collective-permute-start.1
  7.2 44.4 %collective-permute-done.refs_0_.refs_2_ = bf16[2,8,256,512]{3,2,1,0:T(8,128)(2,1)} collective-permute-done((bf16[2,8,256,512]{3,2,1,0:T(8,128)(2,1)}, bf16[2,8,256,512]{3,2,1,0:T(8,128)(2,1)}, u32[]{:S(2)}, u32[]{:S(2)}) %collective-permute-start) | collective-permute-done | bytes 4194336 | tf_op jit(solution)/shard_map/ppermute | solution.py:219
  51.7 2.2 %pack_ranges.2 = bf16[2,8,48,512]{3,2,1,0:T(8,128)(2,1)} custom-call(s32[1]{0:T(128)S(6)} %min.3.which, bf16[2,8,256,512]{3,2,1,0:T(8,128)(2,1)} %collective-permute-done.refs_0_.refs_2_, bf16[2,8,256,512]{3,2,1,0:T(8,128)(2,1)} %refs_0_.5, bf16[2,8,256,512]{3,2,1,0:T(8,128)(2,1)} %collective-permute-done.1.refs_2_.refs_1_), custom_call_target="tpu_custom_call" | custom-call | bytes 1048576 | tf_op jit(solution)/shard_map/pack_ranges/pallas_call | solution.py:66
  53.8 1.9 %collective-permute-start.3 = (bf16[2,8,48,512]{3,2,1,0:T(8,128)(2,1)}, bf16[2,8,48,512]{3,2,1,0:T(8,128)(2,1)}, u32[]{:S(2)}, u32[]{:S(2)}) collective-permute-start(bf16[2,8,48,512]{3,2,1,0:T(8,128)(2,1)} %pack_ranges.2), channel_id=1, source_target_pairs={{0,8},{8,0},{28,12},{16,24},{24,16},{12,28},{1,9},{9,1},{29,13},{1... | collective-permute-start | bytes 2359304 | tf_op jit(solution)/shard_map/ppermute | solution.py:230
  55.8 3.3 %pack_ranges.3 = (bf16[2,8,96,512]{3,2,1,0:T(8,128)(2,1)}, bf16[2,8,112,512]{3,2,1,0:T(8,128)(2,1)S(1)}) custom-call(s32[1]{0:T(128)S(6)} %min.3.which, bf16[2,8,256,512]{3,2,1,0:T(8,128)(2,1)} %collective-permute-done.refs_0_.refs_2_, bf16[2,8,256,512]{3,2,1,0:T(8,128)(2,1)} %refs_0_.5, bf16[2,8,256,512]{3,2,1,0:T(8,128)(2,1)} %collective-permute-done.1.refs_2_.refs_1_), custom_call_target="tpu_custom_call" | custom-call | bytes 1048576 | tf_op jit(solution)/shard_map/pack_ranges/pallas_call | solution.py:66
  59.1 3.9 %collective-permute-start.8 = (bf16[2,8,96,512]{3,2,1,0:T(8,128)(2,1)}, bf16[2,8,96,512]{3,2,1,0:T(8,128)(2,1)}, u32[]{:S(2)}, u32[]{:S(2)}) collective-permute-start(bf16[2,8,96,512]{3,2,1,0:T(8,128)(2,1)} %get-tuple-element.43), channel_id=1, source_target_pairs={{0,8},{8,0},{28,12},{16,24},{24,16},{12,28},{1,9},{9,1},{29,13},{1... | collective-permute-start | bytes 4718600 | tf_op jit(solution)/shard_map/ppermute | solution.py:230
  63.1 1.9 %collective-permute-start.2 = (bf16[2,8,256,512]{3,2,1,0:T(8,128)(2,1)}, bf16[2,8,256,512]{3,2,1,0:T(8,128)(2,1)}, u32[]{:S(2)}, u32[]{:S(2)}) collective-permute-start(bf16[2,8,256,512]{3,2,1,0:T(8,128)(2,1)} %collective-permute-done.refs_0_.refs_2_), channel_id=1, source_target_pairs={{4,0},{12,8},{20,16},{28,24},{0,4},{16,20},{5,1},{13,9},{21,17},{2... | collective-permute-start | bytes 12582920 | tf_op jit(solution)/shard_map/ppermute | solution.py:223
  65.0 3.0 %collective-permute-done.3.refs_4_ = bf16[2,8,48,512]{3,2,1,0:T(8,128)(2,1)} collective-permute-done((bf16[2,8,48,512]{3,2,1,0:T(8,128)(2,1)}, bf16[2,8,48,512]{3,2,1,0:T(8,128)(2,1)}, u32[]{:S(2)}, u32[]{:S(2)}) %collective-permute-start.3) | collective-permute-done | bytes 786464 | tf_op jit(solution)/shard_map/ppermute | solution.py:230
  68.0 1.3 collective-permute-start.4
  69.4 2.2 %hold_rows.1.rows = bf16[2,8,256,512]{3,2,1,0:T(8,128)(2,1)S(1)} custom-call(bf16[2,8,256,512]{3,2,1,0:T(8,128)(2,1)} %refs_0_.5), custom_call_target="tpu_custom_call" | custom-call | tf_op jit(solution)/shard_map/hold_rows/pallas_call | solution.py:52
  71.6 1.5 %collective-permute-done.4.refs_5_ = bf16[2,8,48,512]{3,2,1,0:T(8,128)(2,1)S(1)} collective-permute-done((bf16[2,8,48,512]{3,2,1,0:T(8,128)(2,1)}, bf16[2,8,48,512]{3,2,1,0:T(8,128)(2,1)S(1)}, u32[]{:S(2)}, u32[]{:S(2)}) %collective-permute-start.4) | collective-permute-done | bytes 786464 | tf_op jit(solution)/shard_map/ppermute | solution.py:232
  73.1 3.9 %pair_products.3 = (f32[3,48,128]{2,1,0:T(8,128)S(1)}, f32[3,48,128]{2,1,0:T(8,128)S(1)}, f32[3,48,128]{2,1,0:T(8,128)S(1)}, f32[3,48,128]{2,1,0:T(8,128)S(1)}) custom-call(s32[13]{0:T(128)S(1)} %pad_add_fusion.places, f32[8,128]{1,0:T(8,128)S(1)} %mark.3.unread, bf16[2,8,256,512]{3,2,1,0:T(8,128)(2,1)S(1)} %hold_rows.1.rows, ...), custom_call_target="tpu_custom_call" | custom-call | bytes 1048576 | tf_op jit(solution)/shard_map/pair_products/pallas_call | solution.py:143
  77.0 1.9 %collective-permute-start.13 = (bf16[2,8,112,512]{3,2,1,0:T(8,128)(2,1)S(1)}, bf16[2,8,112,512]{3,2,1,0:T(8,128)(2,1)S(1)}, u32[]{:S(2)}, u32[]{:S(2)}) collective-permute-start(bf16[2,8,112,512]{3,2,1,0:T(8,128)(2,1)S(1)} %get-tuple-element.52.value), channel_id=1, source_target_pairs={{0,8},{8,0},{28,12},{16,24},{24,16},{12,28},{1,9},{9,1},{29,13},{1... | collective-permute-start | bytes 5505032 | tf_op jit(solution)/shard_map/ppermute | solution.py:230
  78.9 2.1 %collective-permute-start.5 = (f32[3,48,128]{2,1,0:T(8,128)S(1)}, f32[3,48,128]{2,1,0:T(8,128)S(1)}, u32[]{:S(2)}, u32[]{:S(2)}) collective-permute-start(f32[3,48,128]{2,1,0:T(8,128)S(1)} %get-tuple-element.40), channel_id=1, source_target_pairs={{0,1},{1,2},{2,3},{3,0},{4,5},{5,6},{6,7},{7,4},{8,9},{9,10},{10,1... | collective-permute-start | bytes 221192 | tf_op jit(solution)/shard_map/ppermute | solution.py:241
  81.1 3.8 %collective-permute-done.8.refs_4_ = bf16[2,8,96,512]{3,2,1,0:T(8,128)(2,1)} collective-permute-done((bf16[2,8,96,512]{3,2,1,0:T(8,128)(2,1)}, bf16[2,8,96,512]{3,2,1,0:T(8,128)(2,1)}, u32[]{:S(2)}, u32[]{:S(2)}) %collective-permute-start.8) | collective-permute-done | bytes 1572896 | tf_op jit(solution)/shard_map/ppermute | solution.py:230
  85.4 1.4 %collective-permute-start.9 = (bf16[2,8,96,512]{3,2,1,0:T(8,128)(2,1)}, bf16[2,8,96,512]{3,2,1,0:T(8,128)(2,1)S(1)}, u32[]{:S(2)}, u32[]{:S(2)}) collective-permute-start(bf16[2,8,96,512]{3,2,1,0:T(8,128)(2,1)} %collective-permute-done.8.refs_4_), channel_id=1, source_target_pairs={{0,4},{8,12},{16,20},{24,28},{1,5},{9,13},{17,21},{25,29},{2,6},{1... | collective-permute-start | bytes 4718600 | tf_op jit(solution)/shard_map/ppermute | solution.py:232
  86.8 2.6 %collective-permute-start.6 = (f32[3,48,128]{2,1,0:T(8,128)S(1)}, f32[3,48,128]{2,1,0:T(8,128)S(1)}, u32[]{:S(2)}, u32[]{:S(2)}) collective-permute-start(f32[3,48,128]{2,1,0:T(8,128)S(1)} %get-tuple-element.41), channel_id=1, source_target_pairs={{0,2},{1,3},{2,0},{3,1},{4,6},{5,7},{6,4},{7,5},{8,10},{9,11},{10,... | collective-permute-start | bytes 221192 | tf_op jit(solution)/shard_map/ppermute | solution.py:241
  89.4 1.3 %collective-permute-start.7 = (f32[3,48,128]{2,1,0:T(8,128)S(1)}, f32[3,48,128]{2,1,0:T(8,128)S(1)}, u32[]{:S(2)}, u32[]{:S(2)}) collective-permute-start(f32[3,48,128]{2,1,0:T(8,128)S(1)} %get-tuple-element.42), channel_id=1, source_target_pairs={{0,3},{1,0},{2,1},{3,2},{4,7},{5,4},{6,5},{7,6},{8,11},{9,8},{10,9... | collective-permute-start | bytes 221192 | tf_op jit(solution)/shard_map/ppermute | solution.py:241
  90.8 4.3 %pair_products.4 = (f32[3,96,128]{2,1,0:T(8,128)S(1)}, f32[3,96,128]{2,1,0:T(8,128)S(1)}, f32[3,96,128]{2,1,0:T(8,128)S(1)}, f32[3,96,128]{2,1,0:T(8,128)S(1)}) custom-call(s32[13]{0:T(128)S(1)} %pad_add_fusion.places, f32[8,128]{1,0:T(8,128)S(1)} %mark.4.unread, bf16[2,8,256,512]{3,2,1,0:T(8,128)(2,1)S(1)} %hold_rows.1.rows, ...), custom_call_target="tpu_custom_call" | custom-call | bytes 1048576 | tf_op jit(solution)/shard_map/pair_products/pallas_call | solution.py:143
  95.1 0.8 collective-permute-start.10
  95.9 6.4 %collective-permute-done.10.refs_5_ = f32[3,96,128]{2,1,0:T(8,128)S(1)} collective-permute-done((f32[3,96,128]{2,1,0:T(8,128)S(1)}, f32[3,96,128]{2,1,0:T(8,128)S(1)}, u32[]{:S(2)}, u32[]{:S(2)}) %collective-permute-start.10) | collective-permute-done | bytes 147488 | tf_op jit(solution)/shard_map/ppermute | solution.py:241
  102.3 2.1 %collective-permute-done.13.refs_4_ = bf16[2,8,112,512]{3,2,1,0:T(8,128)(2,1)S(1)} collective-permute-done((bf16[2,8,112,512]{3,2,1,0:T(8,128)(2,1)S(1)}, bf16[2,8,112,512]{3,2,1,0:T(8,128)(2,1)S(1)}, u32[]{:S(2)}, u32[]{:S(2)}) %collective-permute-start.13) | collective-permute-done | bytes 1835040 | tf_op jit(solution)/shard_map/ppermute | solution.py:230
  104.5 1.4 %collective-permute-start.14 = (bf16[2,8,112,512]{3,2,1,0:T(8,128)(2,1)S(1)}, bf16[2,8,112,512]{3,2,1,0:T(8,128)(2,1)S(1)}, u32[]{:S(2)}, u32[]{:S(2)}) collective-permute-start(bf16[2,8,112,512]{3,2,1,0:T(8,128)(2,1)S(1)} %collective-permute-done.13.refs_4_), channel_id=1, source_target_pairs={{0,4},{8,12},{16,20},{24,28},{1,5},{9,13},{17,21},{25,29},{2,6},{1... | collective-permute-start | bytes 5505032 | tf_op jit(solution)/shard_map/ppermute | solution.py:232
  105.9 4.1 %collective-permute-start.12 = (f32[3,96,128]{2,1,0:T(8,128)S(1)}, f32[3,96,128]{2,1,0:T(8,128)S(1)}, u32[]{:S(2)}, u32[]{:S(2)}) collective-permute-start(f32[3,96,128]{2,1,0:T(8,128)S(1)} %get-tuple-element.51), channel_id=1, source_target_pairs={{0,3},{1,0},{2,1},{3,2},{4,7},{5,4},{6,5},{7,6},{8,11},{9,8},{10,9... | collective-permute-start | bytes 442376 | tf_op jit(solution)/shard_map/ppermute | solution.py:241
  110.0 4.6 %pair_products.5 = (f32[3,112,128]{2,1,0:T(8,128)S(1)}, f32[3,112,128]{2,1,0:T(8,128)S(1)}, f32[3,112,128]{2,1,0:T(8,128)S(1)}, f32[3,112,128]{2,1,0:T(8,128)S(1)}) custom-call(s32[13]{0:T(128)S(1)} %pad_add_fusion.places, f32[8,128]{1,0:T(8,128)S(1)} %mark.5.unread, bf16[2,8,256,512]{3,2,1,0:T(8,128)(2,1)S(1)} %hold_rows.1.rows, ...), custom_call_target="tpu_custom_call" | custom-call | bytes 1048576 | tf_op jit(solution)/shard_map/pair_products/pallas_call | solution.py:143
  114.7 2.1 %collective-permute-done.11.refs_6_ = f32[3,96,128]{2,1,0:T(8,128)S(1)} collective-permute-done((f32[3,96,128]{2,1,0:T(8,128)S(1)}, f32[3,96,128]{2,1,0:T(8,128)S(1)}, u32[]{:S(2)}, u32[]{:S(2)}) %collective-permute-start.11) | collective-permute-done | bytes 147488 | tf_op jit(solution)/shard_map/ppermute | solution.py:241
  116.7 2.9 %collective-permute-start.17 = (f32[3,112,128]{2,1,0:T(8,128)S(1)}, f32[3,112,128]{2,1,0:T(8,128)S(1)}, u32[]{:S(2)}, u32[]{:S(2)}) collective-permute-start(f32[3,112,128]{2,1,0:T(8,128)S(1)} %get-tuple-element.60), channel_id=1, source_target_pairs={{0,3},{1,0},{2,1},{3,2},{4,7},{5,4},{6,5},{7,6},{8,11},{9,8},{10,9... | collective-permute-start | bytes 516104 | tf_op jit(solution)/shard_map/ppermute | solution.py:241
  120.2 4.3 %collective-permute-done.17.refs_11_ = f32[3,112,128]{2,1,0:T(8,128)S(1)} collective-permute-done((f32[3,112,128]{2,1,0:T(8,128)S(1)}, f32[3,112,128]{2,1,0:T(8,128)S(1)}, u32[]{:S(2)}, u32[]{:S(2)}) %collective-permute-start.17) | collective-permute-done | bytes 172064 | tf_op jit(solution)/shard_map/ppermute | solution.py:241
  124.5 8.6 %collective-permute-done.16.refs_10_ = f32[3,112,128]{2,1,0:T(8,128)S(1)} collective-permute-done((f32[3,112,128]{2,1,0:T(8,128)S(1)}, f32[3,112,128]{2,1,0:T(8,128)S(1)}, u32[]{:S(2)}, u32[]{:S(2)}) %collective-permute-start.16) | collective-permute-done | bytes 172064 | tf_op jit(solution)/shard_map/ppermute | solution.py:241
  133.1 0.9 sum_terms.1
  (19 shorter events, 1.4 us)
Async XLA Ops:
  0.0 51.7 %collective-permute-start = (bf16[2,8,256,512]{3,2,1,0:T(8,128)(2,1)}, bf16[2,8,256,512]{3,2,1,0:T(8,128)(2,1)}, u32[]{:S(2)}, u32[]{:S(2)}) collective-permute-start(bf16[2,8,256,512]{3,2,1,0:T(8,128)(2,1)} %refs_0_.5), channel_id=1, source_target_pairs={{16,0},{12,4},{20,12},{0,16},{28,20},{4,28},{17,1},{13,5},{21,13},... | collective-permute-start | bytes 12582920 | tf_op jit(solution)/shard_map/ppermute | solution.py:219
  5.9 45.8 %collective-permute-start.1 = (bf16[2,8,256,512]{3,2,1,0:T(8,128)(2,1)}, bf16[2,8,256,512]{3,2,1,0:T(8,128)(2,1)}, u32[]{:S(2)}, u32[]{:S(2)}) collective-permute-start(bf16[2,8,256,512]{3,2,1,0:T(8,128)(2,1)} %refs_0_.5), channel_id=1, source_target_pairs={{4,0},{12,8},{20,16},{28,24},{8,12},{24,28},{5,1},{13,9},{21,17},{... | collective-permute-start | bytes 12582920 | tf_op jit(solution)/shard_map/ppermute | solution.py:222
  53.8 14.2 %collective-permute-start.3 = (bf16[2,8,48,512]{3,2,1,0:T(8,128)(2,1)}, bf16[2,8,48,512]{3,2,1,0:T(8,128)(2,1)}, u32[]{:S(2)}, u32[]{:S(2)}) collective-permute-start(bf16[2,8,48,512]{3,2,1,0:T(8,128)(2,1)} %pack_ranges.2), channel_id=1, source_target_pairs={{0,8},{8,0},{28,12},{16,24},{24,16},{12,28},{1,9},{9,1},{29,13},{1... | collective-permute-start | bytes 2359304 | tf_op jit(solution)/shard_map/ppermute | solution.py:230
  59.1 25.8 %collective-permute-start.8 = (bf16[2,8,96,512]{3,2,1,0:T(8,128)(2,1)}, bf16[2,8,96,512]{3,2,1,0:T(8,128)(2,1)}, u32[]{:S(2)}, u32[]{:S(2)}) collective-permute-start(bf16[2,8,96,512]{3,2,1,0:T(8,128)(2,1)} %get-tuple-element.43), channel_id=1, source_target_pairs={{0,8},{8,0},{28,12},{16,24},{24,16},{12,28},{1,9},{9,1},{29,13},{1... | collective-permute-start | bytes 4718600 | tf_op jit(solution)/shard_map/ppermute | solution.py:230
  63.1 10.0 %collective-permute-start.2 = (bf16[2,8,256,512]{3,2,1,0:T(8,128)(2,1)}, bf16[2,8,256,512]{3,2,1,0:T(8,128)(2,1)}, u32[]{:S(2)}, u32[]{:S(2)}) collective-permute-start(bf16[2,8,256,512]{3,2,1,0:T(8,128)(2,1)} %collective-permute-done.refs_0_.refs_2_), channel_id=1, source_target_pairs={{4,0},{12,8},{20,16},{28,24},{0,4},{16,20},{5,1},{13,9},{21,17},{2... | collective-permute-start | bytes 12582920 | tf_op jit(solution)/shard_map/ppermute | solution.py:223
  68.0 5.1 %collective-permute-start.4 = (bf16[2,8,48,512]{3,2,1,0:T(8,128)(2,1)}, bf16[2,8,48,512]{3,2,1,0:T(8,128)(2,1)S(1)}, u32[]{:S(2)}, u32[]{:S(2)}) collective-permute-start(bf16[2,8,48,512]{3,2,1,0:T(8,128)(2,1)} %collective-permute-done.3.refs_4_), channel_id=1, source_target_pairs={{0,4},{8,12},{16,20},{24,28},{1,5},{9,13},{17,21},{25,29},{2,6},{1... | collective-permute-start | bytes 2359304 | tf_op jit(solution)/shard_map/ppermute | solution.py:232
  77.0 27.5 %collective-permute-start.13 = (bf16[2,8,112,512]{3,2,1,0:T(8,128)(2,1)S(1)}, bf16[2,8,112,512]{3,2,1,0:T(8,128)(2,1)S(1)}, u32[]{:S(2)}, u32[]{:S(2)}) collective-permute-start(bf16[2,8,112,512]{3,2,1,0:T(8,128)(2,1)S(1)} %get-tuple-element.52.value), channel_id=1, source_target_pairs={{0,8},{8,0},{28,12},{16,24},{24,16},{12,28},{1,9},{9,1},{29,13},{1... | collective-permute-start | bytes 5505032 | tf_op jit(solution)/shard_map/ppermute | solution.py:230
  78.9 6.5 %collective-permute-start.5 = (f32[3,48,128]{2,1,0:T(8,128)S(1)}, f32[3,48,128]{2,1,0:T(8,128)S(1)}, u32[]{:S(2)}, u32[]{:S(2)}) collective-permute-start(f32[3,48,128]{2,1,0:T(8,128)S(1)} %get-tuple-element.40), channel_id=1, source_target_pairs={{0,1},{1,2},{2,3},{3,0},{4,5},{5,6},{6,7},{7,4},{8,9},{9,10},{10,1... | collective-permute-start | bytes 221192 | tf_op jit(solution)/shard_map/ppermute | solution.py:241
  85.4 5.3 %collective-permute-start.9 = (bf16[2,8,96,512]{3,2,1,0:T(8,128)(2,1)}, bf16[2,8,96,512]{3,2,1,0:T(8,128)(2,1)S(1)}, u32[]{:S(2)}, u32[]{:S(2)}) collective-permute-start(bf16[2,8,96,512]{3,2,1,0:T(8,128)(2,1)} %collective-permute-done.8.refs_4_), channel_id=1, source_target_pairs={{0,4},{8,12},{16,20},{24,28},{1,5},{9,13},{17,21},{25,29},{2,6},{1... | collective-permute-start | bytes 4718600 | tf_op jit(solution)/shard_map/ppermute | solution.py:232
  86.8 8.2 %collective-permute-start.6 = (f32[3,48,128]{2,1,0:T(8,128)S(1)}, f32[3,48,128]{2,1,0:T(8,128)S(1)}, u32[]{:S(2)}, u32[]{:S(2)}) collective-permute-start(f32[3,48,128]{2,1,0:T(8,128)S(1)} %get-tuple-element.41), channel_id=1, source_target_pairs={{0,2},{1,3},{2,0},{3,1},{4,6},{5,7},{6,4},{7,5},{8,10},{9,11},{10,... | collective-permute-start | bytes 221192 | tf_op jit(solution)/shard_map/ppermute | solution.py:241
  89.4 5.6 %collective-permute-start.7 = (f32[3,48,128]{2,1,0:T(8,128)S(1)}, f32[3,48,128]{2,1,0:T(8,128)S(1)}, u32[]{:S(2)}, u32[]{:S(2)}) collective-permute-start(f32[3,48,128]{2,1,0:T(8,128)S(1)} %get-tuple-element.42), channel_id=1, source_target_pairs={{0,3},{1,0},{2,1},{3,2},{4,7},{5,4},{6,5},{7,6},{8,11},{9,8},{10,9... | collective-permute-start | bytes 221192 | tf_op jit(solution)/shard_map/ppermute | solution.py:241
  95.1 7.2 %collective-permute-start.10 = (f32[3,96,128]{2,1,0:T(8,128)S(1)}, f32[3,96,128]{2,1,0:T(8,128)S(1)}, u32[]{:S(2)}, u32[]{:S(2)}) collective-permute-start(f32[3,96,128]{2,1,0:T(8,128)S(1)} %get-tuple-element.47), channel_id=1, source_target_pairs={{0,1},{1,2},{2,3},{3,0},{4,5},{5,6},{6,7},{7,4},{8,9},{9,10},{10,1... | collective-permute-start | bytes 442376 | tf_op jit(solution)/shard_map/ppermute | solution.py:241
  104.5 5.6 %collective-permute-start.14 = (bf16[2,8,112,512]{3,2,1,0:T(8,128)(2,1)S(1)}, bf16[2,8,112,512]{3,2,1,0:T(8,128)(2,1)S(1)}, u32[]{:S(2)}, u32[]{:S(2)}) collective-permute-start(bf16[2,8,112,512]{3,2,1,0:T(8,128)(2,1)S(1)} %collective-permute-done.13.refs_4_), channel_id=1, source_target_pairs={{0,4},{8,12},{16,20},{24,28},{1,5},{9,13},{17,21},{25,29},{2,6},{1... | collective-permute-start | bytes 5505032 | tf_op jit(solution)/shard_map/ppermute | solution.py:232
  105.9 8.8 %collective-permute-start.12 = (f32[3,96,128]{2,1,0:T(8,128)S(1)}, f32[3,96,128]{2,1,0:T(8,128)S(1)}, u32[]{:S(2)}, u32[]{:S(2)}) collective-permute-start(f32[3,96,128]{2,1,0:T(8,128)S(1)} %get-tuple-element.51), channel_id=1, source_target_pairs={{0,3},{1,0},{2,1},{3,2},{4,7},{5,4},{6,5},{7,6},{8,11},{9,8},{10,9... | collective-permute-start | bytes 442376 | tf_op jit(solution)/shard_map/ppermute | solution.py:241
  110.0 6.7 %collective-permute-start.11 = (f32[3,96,128]{2,1,0:T(8,128)S(1)}, f32[3,96,128]{2,1,0:T(8,128)S(1)}, u32[]{:S(2)}, u32[]{:S(2)}) collective-permute-start(f32[3,96,128]{2,1,0:T(8,128)S(1)} %get-tuple-element.49), channel_id=1, source_target_pairs={{0,2},{1,3},{2,0},{3,1},{4,6},{5,7},{6,4},{7,5},{8,10},{9,11},{10,... | collective-permute-start | bytes 442376 | tf_op jit(solution)/shard_map/ppermute | solution.py:241
  116.7 7.8 %collective-permute-start.17 = (f32[3,112,128]{2,1,0:T(8,128)S(1)}, f32[3,112,128]{2,1,0:T(8,128)S(1)}, u32[]{:S(2)}, u32[]{:S(2)}) collective-permute-start(f32[3,112,128]{2,1,0:T(8,128)S(1)} %get-tuple-element.60), channel_id=1, source_target_pairs={{0,3},{1,0},{2,1},{3,2},{4,7},{5,4},{6,5},{7,6},{8,11},{9,8},{10,9... | collective-permute-start | bytes 516104 | tf_op jit(solution)/shard_map/ppermute | solution.py:241
  119.7 13.4 %collective-permute-start.16 = (f32[3,112,128]{2,1,0:T(8,128)S(1)}, f32[3,112,128]{2,1,0:T(8,128)S(1)}, u32[]{:S(2)}, u32[]{:S(2)}) collective-permute-start(f32[3,112,128]{2,1,0:T(8,128)S(1)} %get-tuple-element.58), channel_id=1, source_target_pairs={{0,2},{1,3},{2,0},{3,1},{4,6},{5,7},{6,4},{7,5},{8,10},{9,11},{10,... | collective-permute-start | bytes 516104 | tf_op jit(solution)/shard_map/ppermute | solution.py:241
  119.7 13.4 %collective-permute-start.15 = (f32[3,112,128]{2,1,0:T(8,128)S(1)}, f32[3,112,128]{2,1,0:T(8,128)S(1)}, u32[]{:S(2)}, u32[]{:S(2)}) collective-permute-start(f32[3,112,128]{2,1,0:T(8,128)S(1)} %get-tuple-element.56), channel_id=1, source_target_pairs={{0,1},{1,2},{2,3},{3,0},{4,5},{5,6},{6,7},{7,4},{8,9},{9,10},{10,1... | collective-permute-start | bytes 516104 | tf_op jit(solution)/shard_map/ppermute | solution.py:241

commit v6 on v5

--- a/solution.py
+++ b/solution.py
@@ -228,7 +228,7 @@
     twos, made, terms, marks = [], [], [], [mark(sent[-1], 10**12)]
     for turn, piece in enumerate(PIECES):
         twos.append(lax.ppermute(after(sent[turn], *made[: max(turn - 1, 0)][-1:]), "ao", late))
-        earlier = terms[1 - parts : 2 - parts] if turn else []
+        earlier = terms[1 - parts :: 2][: min(turn, 2)] if turn else []
         two_mate = lax.ppermute(after(twos[turn], marks[turn], *earlier), "ao", to_core_1)
         columns = [factors, mate, one, one_mate, twos[turn], two_mate]
         products = pair_products(places, marks[turn], rows, columns, piece, parts, slots)

time: 136 us -> 136 us (level); the launches traced: 134 us -> 136 us
  waiting for transfers between devices: 76.9 us -> 80.2 us
  starting transfers between devices: 34.5 us -> 33 us
    ppermute x9, waiting for transfers between devices: 21.9 us -> 25.7 us  [squares(): lax.ppermute(after(products[step], *others), 'aux', [(z, (z + step) % par...]
    ppermute x3, waiting for transfers between devices: 8.99 us -> 6.9 us  [squares(): lax.ppermute(after(sent[turn], *made[:max(turn - 1, 0)][-1:]), 'ao', late)]
    ppermute x3, waiting for transfers between devices: 1.52 us -> 3.19 us  [squares(): lax.ppermute(after(twos[turn], marks[turn], *earlier), 'ao', to_core_1)]
    ppermute x9, starting transfers between devices: 14.5 us -> 12.9 us  [squares(): lax.ppermute(after(products[step], *others), 'aux', [(z, (z + step) % par...]
  transfers between devices with their start and end apart: 18 -> 18, of which waited for: 10 -> 11; matrix products, arithmetic and copies ran while one was open for 1% -> 1% of each run, Pallas kernels for 14% -> 13%
where the time goes in v6:
time: 136 us
  waiting for transfers between devices  80.2 us (59%)
  starting transfers between devices  33 us (24%)
  Pallas kernels  21.2 us (16%)
    ppermute x1, waiting for transfers between devices, squares(): one = lax.ppermute(factors, 'ao', early)  44.4 us
    ppermute x9, waiting for transfers between devices, squares(): lax.ppermute(after(products[step], *others), 'aux', [(z, (z + step) % par...  25.7 us
    ppermute x9, starting transfers between devices, squares(): lax.ppermute(after(products[step], *others), 'aux', [(z, (z + step) % par...  12.9 us
    pallas_call x3, Pallas kernels, pair_products(): pl.pallas_call(functools.partial(pair_kernel, slots, first, wide, parts),...  12.6 us
    ppermute x3, starting transfers between devices, squares(): lax.ppermute(after(sent[turn], *made[:max(turn - 1, 0)][-1:]), 'ao', late)  7.78 us
    ppermute x3, waiting for transfers between devices, squares(): lax.ppermute(after(sent[turn], *made[:max(turn - 1, 0)][-1:]), 'ao', late)  6.9 us
    pallas_call x2, Pallas kernels, pack(): pl.pallas_call(functools.partial(pack_kernel, pieces), in_specs=[pl.Block...  5.52 us
    ppermute x1, starting transfers between devices, squares(): one = lax.ppermute(factors, 'ao', early)  4.87 us
  transfers between devices with their start and end apart: 18, of which 11 were waited for; matrix products, arithmetic and copies ran while one was open for 1% of the time, Pallas kernels for 13%

profile of v6, /device:TPU:0, one launch (start us, length us, event | category | flops | bytes accessed | tf_op | source)
XLA Modules:
  0.0 135.7 jit_solution(3040100896571457869)
XLA Ops:
  0.0 4.9 %collective-permute-start = (bf16[2,8,256,512]{3,2,1,0:T(8,128)(2,1)}, bf16[2,8,256,512]{3,2,1,0:T(8,128)(2,1)}, u32[]{:S(2)}, u32[]{:S(2)}) collective-permute-start(bf16[2,8,256,512]{3,2,1,0:T(8,128)(2,1)} %refs_0_.5), channel_id=1, source_target_pairs={{16,0},{12,4},{20,12},{0,16},{28,20},{4,28},{17,1},{13,5},{21,13},... | collective-permute-start | bytes 12582920 | tf_op jit(solution)/shard_map/ppermute | solution.py:219
  5.9 1.3 collective-permute-start.1
  7.2 44.4 %collective-permute-done.refs_0_.refs_2_ = bf16[2,8,256,512]{3,2,1,0:T(8,128)(2,1)} collective-permute-done((bf16[2,8,256,512]{3,2,1,0:T(8,128)(2,1)}, bf16[2,8,256,512]{3,2,1,0:T(8,128)(2,1)}, u32[]{:S(2)}, u32[]{:S(2)}) %collective-permute-start) | collective-permute-done | bytes 4194336 | tf_op jit(solution)/shard_map/ppermute | solution.py:219
  51.7 2.2 %pack_ranges.2 = bf16[2,8,48,512]{3,2,1,0:T(8,128)(2,1)} custom-call(s32[1]{0:T(128)S(6)} %min.3.which, bf16[2,8,256,512]{3,2,1,0:T(8,128)(2,1)} %collective-permute-done.refs_0_.refs_2_, bf16[2,8,256,512]{3,2,1,0:T(8,128)(2,1)} %refs_0_.5, bf16[2,8,256,512]{3,2,1,0:T(8,128)(2,1)} %collective-permute-done.1.refs_2_.refs_1_), custom_call_target="tpu_custom_call" | custom-call | bytes 1048576 | tf_op jit(solution)/shard_map/pack_ranges/pallas_call | solution.py:66
  53.8 1.9 %collective-permute-start.3 = (bf16[2,8,48,512]{3,2,1,0:T(8,128)(2,1)}, bf16[2,8,48,512]{3,2,1,0:T(8,128)(2,1)}, u32[]{:S(2)}, u32[]{:S(2)}) collective-permute-start(bf16[2,8,48,512]{3,2,1,0:T(8,128)(2,1)} %pack_ranges.2), channel_id=1, source_target_pairs={{0,8},{8,0},{28,12},{16,24},{24,16},{12,28},{1,9},{9,1},{29,13},{1... | collective-permute-start | bytes 2359304 | tf_op jit(solution)/shard_map/ppermute | solution.py:230
  55.8 3.3 %pack_ranges.3 = (bf16[2,8,96,512]{3,2,1,0:T(8,128)(2,1)}, bf16[2,8,112,512]{3,2,1,0:T(8,128)(2,1)S(1)}) custom-call(s32[1]{0:T(128)S(6)} %min.3.which, bf16[2,8,256,512]{3,2,1,0:T(8,128)(2,1)} %collective-permute-done.refs_0_.refs_2_, bf16[2,8,256,512]{3,2,1,0:T(8,128)(2,1)} %refs_0_.5, bf16[2,8,256,512]{3,2,1,0:T(8,128)(2,1)} %collective-permute-done.1.refs_2_.refs_1_), custom_call_target="tpu_custom_call" | custom-call | bytes 1048576 | tf_op jit(solution)/shard_map/pack_ranges/pallas_call | solution.py:66
  59.1 3.9 %collective-permute-start.8 = (bf16[2,8,96,512]{3,2,1,0:T(8,128)(2,1)}, bf16[2,8,96,512]{3,2,1,0:T(8,128)(2,1)}, u32[]{:S(2)}, u32[]{:S(2)}) collective-permute-start(bf16[2,8,96,512]{3,2,1,0:T(8,128)(2,1)} %get-tuple-element.43), channel_id=1, source_target_pairs={{0,8},{8,0},{28,12},{16,24},{24,16},{12,28},{1,9},{9,1},{29,13},{1... | collective-permute-start | bytes 4718600 | tf_op jit(solution)/shard_map/ppermute | solution.py:230
  63.1 1.9 %collective-permute-start.2 = (bf16[2,8,256,512]{3,2,1,0:T(8,128)(2,1)}, bf16[2,8,256,512]{3,2,1,0:T(8,128)(2,1)}, u32[]{:S(2)}, u32[]{:S(2)}) collective-permute-start(bf16[2,8,256,512]{3,2,1,0:T(8,128)(2,1)} %collective-permute-done.refs_0_.refs_2_), channel_id=1, source_target_pairs={{4,0},{12,8},{20,16},{28,24},{0,4},{16,20},{5,1},{13,9},{21,17},{2... | collective-permute-start | bytes 12582920 | tf_op jit(solution)/shard_map/ppermute | solution.py:223
  65.0 3.0 %collective-permute-done.3.refs_4_ = bf16[2,8,48,512]{3,2,1,0:T(8,128)(2,1)} collective-permute-done((bf16[2,8,48,512]{3,2,1,0:T(8,128)(2,1)}, bf16[2,8,48,512]{3,2,1,0:T(8,128)(2,1)}, u32[]{:S(2)}, u32[]{:S(2)}) %collective-permute-start.3) | collective-permute-done | bytes 786464 | tf_op jit(solution)/shard_map/ppermute | solution.py:230
  68.0 1.3 collective-permute-start.4
  69.4 2.2 %hold_rows.1.rows = bf16[2,8,256,512]{3,2,1,0:T(8,128)(2,1)S(1)} custom-call(bf16[2,8,256,512]{3,2,1,0:T(8,128)(2,1)} %refs_0_.5), custom_call_target="tpu_custom_call" | custom-call | tf_op jit(solution)/shard_map/hold_rows/pallas_call | solution.py:52
  71.6 1.5 %collective-permute-done.4.refs_5_ = bf16[2,8,48,512]{3,2,1,0:T(8,128)(2,1)S(1)} collective-permute-done((bf16[2,8,48,512]{3,2,1,0:T(8,128)(2,1)}, bf16[2,8,48,512]{3,2,1,0:T(8,128)(2,1)S(1)}, u32[]{:S(2)}, u32[]{:S(2)}) %collective-permute-start.4) | collective-permute-done | bytes 786464 | tf_op jit(solution)/shard_map/ppermute | solution.py:232
  73.1 3.9 %pair_products.3 = (f32[3,48,128]{2,1,0:T(8,128)S(1)}, f32[3,48,128]{2,1,0:T(8,128)S(1)}, f32[3,48,128]{2,1,0:T(8,128)S(1)}, f32[3,48,128]{2,1,0:T(8,128)S(1)}) custom-call(s32[13]{0:T(128)S(1)} %pad_add_fusion.places, f32[8,128]{1,0:T(8,128)S(1)} %mark.3.unread, bf16[2,8,256,512]{3,2,1,0:T(8,128)(2,1)S(1)} %hold_rows.1.rows, ...), custom_call_target="tpu_custom_call" | custom-call | bytes 1048576 | tf_op jit(solution)/shard_map/pair_products/pallas_call | solution.py:143
  77.0 1.9 %collective-permute-start.13 = (bf16[2,8,112,512]{3,2,1,0:T(8,128)(2,1)S(1)}, bf16[2,8,112,512]{3,2,1,0:T(8,128)(2,1)S(1)}, u32[]{:S(2)}, u32[]{:S(2)}) collective-permute-start(bf16[2,8,112,512]{3,2,1,0:T(8,128)(2,1)S(1)} %get-tuple-element.52.value), channel_id=1, source_target_pairs={{0,8},{8,0},{28,12},{16,24},{24,16},{12,28},{1,9},{9,1},{29,13},{1... | collective-permute-start | bytes 5505032 | tf_op jit(solution)/shard_map/ppermute | solution.py:230
  78.9 2.1 %collective-permute-start.5 = (f32[3,48,128]{2,1,0:T(8,128)S(1)}, f32[3,48,128]{2,1,0:T(8,128)S(1)}, u32[]{:S(2)}, u32[]{:S(2)}) collective-permute-start(f32[3,48,128]{2,1,0:T(8,128)S(1)} %get-tuple-element.40), channel_id=1, source_target_pairs={{0,1},{1,2},{2,3},{3,0},{4,5},{5,6},{6,7},{7,4},{8,9},{9,10},{10,1... | collective-permute-start | bytes 221192 | tf_op jit(solution)/shard_map/ppermute | solution.py:241
  81.0 3.9 %collective-permute-done.8.refs_4_ = bf16[2,8,96,512]{3,2,1,0:T(8,128)(2,1)} collective-permute-done((bf16[2,8,96,512]{3,2,1,0:T(8,128)(2,1)}, bf16[2,8,96,512]{3,2,1,0:T(8,128)(2,1)}, u32[]{:S(2)}, u32[]{:S(2)}) %collective-permute-start.8) | collective-permute-done | bytes 1572896 | tf_op jit(solution)/shard_map/ppermute | solution.py:230
  85.4 1.4 %collective-permute-start.9 = (bf16[2,8,96,512]{3,2,1,0:T(8,128)(2,1)}, bf16[2,8,96,512]{3,2,1,0:T(8,128)(2,1)S(1)}, u32[]{:S(2)}, u32[]{:S(2)}) collective-permute-start(bf16[2,8,96,512]{3,2,1,0:T(8,128)(2,1)} %collective-permute-done.8.refs_4_), channel_id=1, source_target_pairs={{0,4},{8,12},{16,20},{24,28},{1,5},{9,13},{17,21},{25,29},{2,6},{1... | collective-permute-start | bytes 4718600 | tf_op jit(solution)/shard_map/ppermute | solution.py:232
  86.8 2.6 %collective-permute-start.6 = (f32[3,48,128]{2,1,0:T(8,128)S(1)}, f32[3,48,128]{2,1,0:T(8,128)S(1)}, u32[]{:S(2)}, u32[]{:S(2)}) collective-permute-start(f32[3,48,128]{2,1,0:T(8,128)S(1)} %get-tuple-element.41), channel_id=1, source_target_pairs={{0,2},{1,3},{2,0},{3,1},{4,6},{5,7},{6,4},{7,5},{8,10},{9,11},{10,... | collective-permute-start | bytes 221192 | tf_op jit(solution)/shard_map/ppermute | solution.py:241
  89.4 1.3 collective-permute-start.7
  90.8 4.2 %pair_products.4 = (f32[3,96,128]{2,1,0:T(8,128)S(1)}, f32[3,96,128]{2,1,0:T(8,128)S(1)}, f32[3,96,128]{2,1,0:T(8,128)S(1)}, f32[3,96,128]{2,1,0:T(8,128)S(1)}) custom-call(s32[13]{0:T(128)S(1)} %pad_add_fusion.places, f32[8,128]{1,0:T(8,128)S(1)} %mark.4.unread, bf16[2,8,256,512]{3,2,1,0:T(8,128)(2,1)S(1)} %hold_rows.1.rows, ...), custom_call_target="tpu_custom_call" | custom-call | bytes 1048576 | tf_op jit(solution)/shard_map/pair_products/pallas_call | solution.py:143
  95.0 2.8 %collective-permute-start.12 = (f32[3,96,128]{2,1,0:T(8,128)S(1)}, f32[3,96,128]{2,1,0:T(8,128)S(1)}, u32[]{:S(2)}, u32[]{:S(2)}) collective-permute-start(f32[3,96,128]{2,1,0:T(8,128)S(1)} %get-tuple-element.51), channel_id=1, source_target_pairs={{0,3},{1,0},{2,1},{3,2},{4,7},{5,4},{6,5},{7,6},{8,11},{9,8},{10,9... | collective-permute-start | bytes 442376 | tf_op jit(solution)/shard_map/ppermute | solution.py:241
  97.8 4.3 %collective-permute-done.12.refs_7_ = f32[3,96,128]{2,1,0:T(8,128)S(1)} collective-permute-done((f32[3,96,128]{2,1,0:T(8,128)S(1)}, f32[3,96,128]{2,1,0:T(8,128)S(1)}, u32[]{:S(2)}, u32[]{:S(2)}) %collective-permute-start.12) | collective-permute-done | bytes 147488 | tf_op jit(solution)/shard_map/ppermute | solution.py:241
  102.1 3.7 %collective-permute-done.10.refs_5_ = f32[3,96,128]{2,1,0:T(8,128)S(1)} collective-permute-done((f32[3,96,128]{2,1,0:T(8,128)S(1)}, f32[3,96,128]{2,1,0:T(8,128)S(1)}, u32[]{:S(2)}, u32[]{:S(2)}) %collective-permute-start.10) | collective-permute-done | bytes 147488 | tf_op jit(solution)/shard_map/ppermute | solution.py:241
  105.8 1.6 %collective-permute-start.14 = (bf16[2,8,112,512]{3,2,1,0:T(8,128)(2,1)S(1)}, bf16[2,8,112,512]{3,2,1,0:T(8,128)(2,1)S(1)}, u32[]{:S(2)}, u32[]{:S(2)}) collective-permute-start(bf16[2,8,112,512]{3,2,1,0:T(8,128)(2,1)S(1)} %collective-permute-done.13.refs_4_), channel_id=1, source_target_pairs={{0,4},{8,12},{16,20},{24,28},{1,5},{9,13},{17,21},{25,29},{2,6},{1... | collective-permute-start | bytes 5505032 | tf_op jit(solution)/shard_map/ppermute | solution.py:232
  107.4 1.6 %collective-permute-start.11 = (f32[3,96,128]{2,1,0:T(8,128)S(1)}, f32[3,96,128]{2,1,0:T(8,128)S(1)}, u32[]{:S(2)}, u32[]{:S(2)}) collective-permute-start(f32[3,96,128]{2,1,0:T(8,128)S(1)} %get-tuple-element.49), channel_id=1, source_target_pairs={{0,2},{1,3},{2,0},{3,1},{4,6},{5,7},{6,4},{7,5},{8,10},{9,11},{10,... | collective-permute-start | bytes 442376 | tf_op jit(solution)/shard_map/ppermute | solution.py:241
  109.0 1.7 %collective-permute-done.14.refs_5_ = bf16[2,8,112,512]{3,2,1,0:T(8,128)(2,1)S(1)} collective-permute-done((bf16[2,8,112,512]{3,2,1,0:T(8,128)(2,1)S(1)}, bf16[2,8,112,512]{3,2,1,0:T(8,128)(2,1)S(1)}, u32[]{:S(2)}, u32[]{:S(2)}) %collective-permute-start.14) | collective-permute-done | bytes 1835040 | tf_op jit(solution)/shard_map/ppermute | solution.py:232
  110.7 4.5 %pair_products.5 = (f32[3,112,128]{2,1,0:T(8,128)S(1)}, f32[3,112,128]{2,1,0:T(8,128)S(1)}, f32[3,112,128]{2,1,0:T(8,128)S(1)}, f32[3,112,128]{2,1,0:T(8,128)S(1)}) custom-call(s32[13]{0:T(128)S(1)} %pad_add_fusion.places, f32[8,128]{1,0:T(8,128)S(1)} %mark.5.unread, bf16[2,8,256,512]{3,2,1,0:T(8,128)(2,1)S(1)} %hold_rows.1.rows, ...), custom_call_target="tpu_custom_call" | custom-call | bytes 1048576 | tf_op jit(solution)/shard_map/pair_products/pallas_call | solution.py:143
  115.2 1.3 collective-permute-done.11.refs_6_
  116.6 1.6 %collective-permute-start.17 = (f32[3,112,128]{2,1,0:T(8,128)S(1)}, f32[3,112,128]{2,1,0:T(8,128)S(1)}, u32[]{:S(2)}, u32[]{:S(2)}) collective-permute-start(f32[3,112,128]{2,1,0:T(8,128)S(1)} %get-tuple-element.60), channel_id=1, source_target_pairs={{0,3},{1,0},{2,1},{3,2},{4,7},{5,4},{6,5},{7,6},{8,11},{9,8},{10,9... | collective-permute-start | bytes 516104 | tf_op jit(solution)/shard_map/ppermute | solution.py:241
  118.9 4.0 %collective-permute-done.17.refs_11_ = f32[3,112,128]{2,1,0:T(8,128)S(1)} collective-permute-done((f32[3,112,128]{2,1,0:T(8,128)S(1)}, f32[3,112,128]{2,1,0:T(8,128)S(1)}, u32[]{:S(2)}, u32[]{:S(2)}) %collective-permute-start.17) | collective-permute-done | bytes 172064 | tf_op jit(solution)/shard_map/ppermute | solution.py:241
  122.9 11.8 %collective-permute-done.16.refs_10_ = f32[3,112,128]{2,1,0:T(8,128)S(1)} collective-permute-done((f32[3,112,128]{2,1,0:T(8,128)S(1)}, f32[3,112,128]{2,1,0:T(8,128)S(1)}, u32[]{:S(2)}, u32[]{:S(2)}) %collective-permute-start.16) | collective-permute-done | bytes 172064 | tf_op jit(solution)/shard_map/ppermute | solution.py:241
  134.7 0.9 sum_terms.1
  (19 shorter events, 2.3 us)
Async XLA Ops:
  0.0 51.7 %collective-permute-start = (bf16[2,8,256,512]{3,2,1,0:T(8,128)(2,1)}, bf16[2,8,256,512]{3,2,1,0:T(8,128)(2,1)}, u32[]{:S(2)}, u32[]{:S(2)}) collective-permute-start(bf16[2,8,256,512]{3,2,1,0:T(8,128)(2,1)} %refs_0_.5), channel_id=1, source_target_pairs={{16,0},{12,4},{20,12},{0,16},{28,20},{4,28},{17,1},{13,5},{21,13},... | collective-permute-start | bytes 12582920 | tf_op jit(solution)/shard_map/ppermute | solution.py:219
  5.9 45.8 %collective-permute-start.1 = (bf16[2,8,256,512]{3,2,1,0:T(8,128)(2,1)}, bf16[2,8,256,512]{3,2,1,0:T(8,128)(2,1)}, u32[]{:S(2)}, u32[]{:S(2)}) collective-permute-start(bf16[2,8,256,512]{3,2,1,0:T(8,128)(2,1)} %refs_0_.5), channel_id=1, source_target_pairs={{4,0},{12,8},{20,16},{28,24},{8,12},{24,28},{5,1},{13,9},{21,17},{... | collective-permute-start | bytes 12582920 | tf_op jit(solution)/shard_map/ppermute | solution.py:222
  53.8 14.2 %collective-permute-start.3 = (bf16[2,8,48,512]{3,2,1,0:T(8,128)(2,1)}, bf16[2,8,48,512]{3,2,1,0:T(8,128)(2,1)}, u32[]{:S(2)}, u32[]{:S(2)}) collective-permute-start(bf16[2,8,48,512]{3,2,1,0:T(8,128)(2,1)} %pack_ranges.2), channel_id=1, source_target_pairs={{0,8},{8,0},{28,12},{16,24},{24,16},{12,28},{1,9},{9,1},{29,13},{1... | collective-permute-start | bytes 2359304 | tf_op jit(solution)/shard_map/ppermute | solution.py:230
  59.1 25.8 %collective-permute-start.8 = (bf16[2,8,96,512]{3,2,1,0:T(8,128)(2,1)}, bf16[2,8,96,512]{3,2,1,0:T(8,128)(2,1)}, u32[]{:S(2)}, u32[]{:S(2)}) collective-permute-start(bf16[2,8,96,512]{3,2,1,0:T(8,128)(2,1)} %get-tuple-element.43), channel_id=1, source_target_pairs={{0,8},{8,0},{28,12},{16,24},{24,16},{12,28},{1,9},{9,1},{29,13},{1... | collective-permute-start | bytes 4718600 | tf_op jit(solution)/shard_map/ppermute | solution.py:230
  63.1 10.0 %collective-permute-start.2 = (bf16[2,8,256,512]{3,2,1,0:T(8,128)(2,1)}, bf16[2,8,256,512]{3,2,1,0:T(8,128)(2,1)}, u32[]{:S(2)}, u32[]{:S(2)}) collective-permute-start(bf16[2,8,256,512]{3,2,1,0:T(8,128)(2,1)} %collective-permute-done.refs_0_.refs_2_), channel_id=1, source_target_pairs={{4,0},{12,8},{20,16},{28,24},{0,4},{16,20},{5,1},{13,9},{21,17},{2... | collective-permute-start | bytes 12582920 | tf_op jit(solution)/shard_map/ppermute | solution.py:223
  68.0 5.1 %collective-permute-start.4 = (bf16[2,8,48,512]{3,2,1,0:T(8,128)(2,1)}, bf16[2,8,48,512]{3,2,1,0:T(8,128)(2,1)S(1)}, u32[]{:S(2)}, u32[]{:S(2)}) collective-permute-start(bf16[2,8,48,512]{3,2,1,0:T(8,128)(2,1)} %collective-permute-done.3.refs_4_), channel_id=1, source_target_pairs={{0,4},{8,12},{16,20},{24,28},{1,5},{9,13},{17,21},{25,29},{2,6},{1... | collective-permute-start | bytes 2359304 | tf_op jit(solution)/shard_map/ppermute | solution.py:232
  77.0 28.8 %collective-permute-start.13 = (bf16[2,8,112,512]{3,2,1,0:T(8,128)(2,1)S(1)}, bf16[2,8,112,512]{3,2,1,0:T(8,128)(2,1)S(1)}, u32[]{:S(2)}, u32[]{:S(2)}) collective-permute-start(bf16[2,8,112,512]{3,2,1,0:T(8,128)(2,1)S(1)} %get-tuple-element.52.value), channel_id=1, source_target_pairs={{0,8},{8,0},{28,12},{16,24},{24,16},{12,28},{1,9},{9,1},{29,13},{1... | collective-permute-start | bytes 5505032 | tf_op jit(solution)/shard_map/ppermute | solution.py:230
  78.9 6.5 %collective-permute-start.5 = (f32[3,48,128]{2,1,0:T(8,128)S(1)}, f32[3,48,128]{2,1,0:T(8,128)S(1)}, u32[]{:S(2)}, u32[]{:S(2)}) collective-permute-start(f32[3,48,128]{2,1,0:T(8,128)S(1)} %get-tuple-element.40), channel_id=1, source_target_pairs={{0,1},{1,2},{2,3},{3,0},{4,5},{5,6},{6,7},{7,4},{8,9},{9,10},{10,1... | collective-permute-start | bytes 221192 | tf_op jit(solution)/shard_map/ppermute | solution.py:241
  85.4 5.4 %collective-permute-start.9 = (bf16[2,8,96,512]{3,2,1,0:T(8,128)(2,1)}, bf16[2,8,96,512]{3,2,1,0:T(8,128)(2,1)S(1)}, u32[]{:S(2)}, u32[]{:S(2)}) collective-permute-start(bf16[2,8,96,512]{3,2,1,0:T(8,128)(2,1)} %collective-permute-done.8.refs_4_), channel_id=1, source_target_pairs={{0,4},{8,12},{16,20},{24,28},{1,5},{9,13},{17,21},{25,29},{2,6},{1... | collective-permute-start | bytes 4718600 | tf_op jit(solution)/shard_map/ppermute | solution.py:232
  86.8 8.2 %collective-permute-start.6 = (f32[3,48,128]{2,1,0:T(8,128)S(1)}, f32[3,48,128]{2,1,0:T(8,128)S(1)}, u32[]{:S(2)}, u32[]{:S(2)}) collective-permute-start(f32[3,48,128]{2,1,0:T(8,128)S(1)} %get-tuple-element.41), channel_id=1, source_target_pairs={{0,2},{1,3},{2,0},{3,1},{4,6},{5,7},{6,4},{7,5},{8,10},{9,11},{10,... | collective-permute-start | bytes 221192 | tf_op jit(solution)/shard_map/ppermute | solution.py:241
  89.4 5.6 %collective-permute-start.7 = (f32[3,48,128]{2,1,0:T(8,128)S(1)}, f32[3,48,128]{2,1,0:T(8,128)S(1)}, u32[]{:S(2)}, u32[]{:S(2)}) collective-permute-start(f32[3,48,128]{2,1,0:T(8,128)S(1)} %get-tuple-element.42), channel_id=1, source_target_pairs={{0,3},{1,0},{2,1},{3,2},{4,7},{5,4},{6,5},{7,6},{8,11},{9,8},{10,9... | collective-permute-start | bytes 221192 | tf_op jit(solution)/shard_map/ppermute | solution.py:241
  95.0 7.1 %collective-permute-start.12 = (f32[3,96,128]{2,1,0:T(8,128)S(1)}, f32[3,96,128]{2,1,0:T(8,128)S(1)}, u32[]{:S(2)}, u32[]{:S(2)}) collective-permute-start(f32[3,96,128]{2,1,0:T(8,128)S(1)} %get-tuple-element.51), channel_id=1, source_target_pairs={{0,3},{1,0},{2,1},{3,2},{4,7},{5,4},{6,5},{7,6},{8,11},{9,8},{10,9... | collective-permute-start | bytes 442376 | tf_op jit(solution)/shard_map/ppermute | solution.py:241
  97.8 8.0 %collective-permute-start.10 = (f32[3,96,128]{2,1,0:T(8,128)S(1)}, f32[3,96,128]{2,1,0:T(8,128)S(1)}, u32[]{:S(2)}, u32[]{:S(2)}) collective-permute-start(f32[3,96,128]{2,1,0:T(8,128)S(1)} %get-tuple-element.47), channel_id=1, source_target_pairs={{0,1},{1,2},{2,3},{3,0},{4,5},{5,6},{6,7},{7,4},{8,9},{9,10},{10,1... | collective-permute-start | bytes 442376 | tf_op jit(solution)/shard_map/ppermute | solution.py:241
  105.8 4.9 %collective-permute-start.14 = (bf16[2,8,112,512]{3,2,1,0:T(8,128)(2,1)S(1)}, bf16[2,8,112,512]{3,2,1,0:T(8,128)(2,1)S(1)}, u32[]{:S(2)}, u32[]{:S(2)}) collective-permute-start(bf16[2,8,112,512]{3,2,1,0:T(8,128)(2,1)S(1)} %collective-permute-done.13.refs_4_), channel_id=1, source_target_pairs={{0,4},{8,12},{16,20},{24,28},{1,5},{9,13},{17,21},{25,29},{2,6},{1... | collective-permute-start | bytes 5505032 | tf_op jit(solution)/shard_map/ppermute | solution.py:232
  107.4 9.1 %collective-permute-start.11 = (f32[3,96,128]{2,1,0:T(8,128)S(1)}, f32[3,96,128]{2,1,0:T(8,128)S(1)}, u32[]{:S(2)}, u32[]{:S(2)}) collective-permute-start(f32[3,96,128]{2,1,0:T(8,128)S(1)} %get-tuple-element.49), channel_id=1, source_target_pairs={{0,2},{1,3},{2,0},{3,1},{4,6},{5,7},{6,4},{7,5},{8,10},{9,11},{10,... | collective-permute-start | bytes 442376 | tf_op jit(solution)/shard_map/ppermute | solution.py:241
  116.6 6.3 %collective-permute-start.17 = (f32[3,112,128]{2,1,0:T(8,128)S(1)}, f32[3,112,128]{2,1,0:T(8,128)S(1)}, u32[]{:S(2)}, u32[]{:S(2)}) collective-permute-start(f32[3,112,128]{2,1,0:T(8,128)S(1)} %get-tuple-element.60), channel_id=1, source_target_pairs={{0,3},{1,0},{2,1},{3,2},{4,7},{5,4},{6,5},{7,6},{8,11},{9,8},{10,9... | collective-permute-start | bytes 516104 | tf_op jit(solution)/shard_map/ppermute | solution.py:241
  118.1 16.6 %collective-permute-start.16 = (f32[3,112,128]{2,1,0:T(8,128)S(1)}, f32[3,112,128]{2,1,0:T(8,128)S(1)}, u32[]{:S(2)}, u32[]{:S(2)}) collective-permute-start(f32[3,112,128]{2,1,0:T(8,128)S(1)} %get-tuple-element.58), channel_id=1, source_target_pairs={{0,2},{1,3},{2,0},{3,1},{4,6},{5,7},{6,4},{7,5},{8,10},{9,11},{10,... | collective-permute-start | bytes 516104 | tf_op jit(solution)/shard_map/ppermute | solution.py:241
  118.6 16.2 %collective-permute-start.15 = (f32[3,112,128]{2,1,0:T(8,128)S(1)}, f32[3,112,128]{2,1,0:T(8,128)S(1)}, u32[]{:S(2)}, u32[]{:S(2)}) collective-permute-start(f32[3,112,128]{2,1,0:T(8,128)S(1)} %get-tuple-element.56), channel_id=1, source_target_pairs={{0,1},{1,2},{2,3},{3,0},{4,5},{5,6},{6,7},{7,4},{8,9},{9,10},{10,1... | collective-permute-start | bytes 516104 | tf_op jit(solution)/shard_map/ppermute | solution.py:241

commit v7 on v5

--- a/solution.py
+++ b/solution.py
@@ -223,7 +223,10 @@
     one_mate = lax.ppermute(one, "ao", to_core_0 + to_core_1[::2])
     rows = hold(after(factors, mate))
     senders = [one, in_hbm(factors), mate]
-    sent = pack(which, senders, PIECES[:1])
+    first, wide = PIECES[0]
+    mine, mates, opposite = (lax.slice_in_dim(a, first, first + wide, axis=2) for a in (factors, mate, one))
+    late_core = which[0] != 1
+    sent = [jnp.where(even, opposite, jnp.where(late_core, mates, mine))]
     sent += pack(after(which, places, *sent), senders, PIECES[1:])
     twos, made, terms, marks = [], [], [], [mark(sent[-1], 10**12)]
     for turn, piece in enumerate(PIECES):

time: 136 us -> 136 us (level)
  other arithmetic: 0.85 us -> 3.48 us
  Pallas kernels: 21.4 us -> 19.6 us
    select_n x0 -> x1, other arithmetic: none -> 2.62 us  [squares(): sent = [jnp.where(even, opposite, jnp.where(late_core, mates, mine))]]
    pallas_call x2 -> x1, Pallas kernels: 5.52 us -> 3.34 us  [pack(): pl.pallas_call(functools.partial(pack_kernel, pieces), in_specs=[pl.Block...]
where the time goes in v7:
time: 136 us; the launch traced here: 134 us
  waiting for transfers between devices  76.2 us (56%)
  starting transfers between devices  34.5 us (25%)
  Pallas kernels  19.6 us (14%)
  other arithmetic  3.48 us (3%)
    ppermute x1, waiting for transfers between devices, squares(): one = lax.ppermute(factors, 'ao', early)  44.4 us
    ppermute x9, waiting for transfers between devices, squares(): lax.ppermute(after(products[step], *others), 'aux', [(z, (z + step) % par...  21 us
    ppermute x9, starting transfers between devices, squares(): lax.ppermute(after(products[step], *others), 'aux', [(z, (z + step) % par...  14.5 us
    pallas_call x3, Pallas kernels, pair_products(): pl.pallas_call(functools.partial(pair_kernel, slots, first, wide, parts),...  13.2 us
    ppermute x3, waiting for transfers between devices, squares(): lax.ppermute(after(sent[turn], *made[:max(turn - 1, 0)][-1:]), 'ao', late)  9.23 us
    ppermute x3, starting transfers between devices, squares(): lax.ppermute(after(sent[turn], *made[:max(turn - 1, 0)][-1:]), 'ao', late)  7.77 us
    ppermute x1, starting transfers between devices, squares(): one = lax.ppermute(factors, 'ao', early)  4.87 us
    ppermute x3, starting transfers between devices, squares(): lax.ppermute(after(twos[turn], marks[turn], *earlier), 'ao', to_core_1)  4.1 us
  transfers between devices with their start and end apart: 18, of which 10 were waited for; matrix products, arithmetic and copies ran while one was open for 1% of the time, Pallas kernels for 14%

profile of v7, /device:TPU:0, one launch (start us, length us, event | category | flops | bytes accessed | tf_op | source)
XLA Modules:
  0.0 134.2 jit_solution(13433655058669792671)
XLA Ops:
  0.0 4.9 %collective-permute-start = (bf16[2,8,256,512]{3,2,1,0:T(8,128)(2,1)}, bf16[2,8,256,512]{3,2,1,0:T(8,128)(2,1)}, u32[]{:S(2)}, u32[]{:S(2)}) collective-permute-start(bf16[2,8,256,512]{3,2,1,0:T(8,128)(2,1)} %refs_0_.5), channel_id=1, source_target_pairs={{16,0},{12,4},{20,12},{0,16},{28,20},{4,28},{17,1},{13,5},{21,13},... | collective-permute-start | bytes 12582920 | tf_op jit(solution)/shard_map/ppermute | solution.py:219
  4.9 0.8 compare_select_fusion.4
  5.9 1.3 collective-permute-start.1
  7.2 44.4 %collective-permute-done.refs_0_.refs_2_ = bf16[2,8,256,512]{3,2,1,0:T(8,128)(2,1)} collective-permute-done((bf16[2,8,256,512]{3,2,1,0:T(8,128)(2,1)}, bf16[2,8,256,512]{3,2,1,0:T(8,128)(2,1)}, u32[]{:S(2)}, u32[]{:S(2)}) %collective-permute-start) | collective-permute-done | bytes 4194336 | tf_op jit(solution)/shard_map/ppermute | solution.py:219
  51.7 2.6 %fusion = bf16[2,8,48,512]{3,2,1,0:T(8,128)(2,1)} fusion(bf16[2,8,256,512]{3,2,1,0:T(8,128)(2,1)} %collective-permute-done.1.refs_2_.refs_1_, bf16[2,8,256,512]{3,2,1,0:T(8,128)(2,1)} %collective-permute-done.refs_0_.refs_2_, bf16[2,8,256,512]{3,2,1,0:T(8,128)(2,1)} %refs_0_.5, pred[]{:T(512)} %bitcast.2, pred[]{:T(512)S(6)} %lt.20), kind=kLoop, calls=%fused_computation.1 | loop fusion | flops 786432 | bytes 3145730 | tf_op jit(solution)/shard_map/jit(_where)/select_n | solution.py:229
  54.3 1.9 %collective-permute-start.3 = (bf16[2,8,48,512]{3,2,1,0:T(8,128)(2,1)}, bf16[2,8,48,512]{3,2,1,0:T(8,128)(2,1)}, u32[]{:S(2)}, u32[]{:S(2)}) collective-permute-start(bf16[2,8,48,512]{3,2,1,0:T(8,128)(2,1)} %fusion), channel_id=1, source_target_pairs={{0,8},{8,0},{28,12},{16,24},{24,16},{12,28},{1,9},{9,1},{29,13},{1... | collective-permute-start | bytes 2359304 | tf_op jit(solution)/shard_map/ppermute | solution.py:233
  56.2 3.3 %pack_ranges.1 = (bf16[2,8,96,512]{3,2,1,0:T(8,128)(2,1)}, bf16[2,8,112,512]{3,2,1,0:T(8,128)(2,1)S(1)}) custom-call(s32[1]{0:T(128)S(6)} %min.3.which, bf16[2,8,256,512]{3,2,1,0:T(8,128)(2,1)} %collective-permute-done.refs_0_.refs_2_, bf16[2,8,256,512]{3,2,1,0:T(8,128)(2,1)} %refs_0_.5, bf16[2,8,256,512]{3,2,1,0:T(8,128)(2,1)} %collective-permute-done.1.refs_2_.refs_1_), custom_call_target="tpu_custom_call" | custom-call | bytes 1048576 | tf_op jit(solution)/shard_map/pack_ranges/pallas_call | solution.py:66
  59.6 3.9 %collective-permute-start.8 = (bf16[2,8,96,512]{3,2,1,0:T(8,128)(2,1)}, bf16[2,8,96,512]{3,2,1,0:T(8,128)(2,1)}, u32[]{:S(2)}, u32[]{:S(2)}) collective-permute-start(bf16[2,8,96,512]{3,2,1,0:T(8,128)(2,1)} %get-tuple-element.43), channel_id=1, source_target_pairs={{0,8},{8,0},{28,12},{16,24},{24,16},{12,28},{1,9},{9,1},{29,13},{1... | collective-permute-start | bytes 4718600 | tf_op jit(solution)/shard_map/ppermute | solution.py:233
  63.5 1.9 %collective-permute-start.2 = (bf16[2,8,256,512]{3,2,1,0:T(8,128)(2,1)}, bf16[2,8,256,512]{3,2,1,0:T(8,128)(2,1)}, u32[]{:S(2)}, u32[]{:S(2)}) collective-permute-start(bf16[2,8,256,512]{3,2,1,0:T(8,128)(2,1)} %collective-permute-done.refs_0_.refs_2_), channel_id=1, source_target_pairs={{4,0},{12,8},{20,16},{28,24},{0,4},{16,20},{5,1},{13,9},{21,17},{2... | collective-permute-start | bytes 12582920 | tf_op jit(solution)/shard_map/ppermute | solution.py:223
  65.4 3.0 %collective-permute-done.3.refs_4_ = bf16[2,8,48,512]{3,2,1,0:T(8,128)(2,1)} collective-permute-done((bf16[2,8,48,512]{3,2,1,0:T(8,128)(2,1)}, bf16[2,8,48,512]{3,2,1,0:T(8,128)(2,1)}, u32[]{:S(2)}, u32[]{:S(2)}) %collective-permute-start.3) | collective-permute-done | bytes 786464 | tf_op jit(solution)/shard_map/ppermute | solution.py:233
  68.5 1.3 collective-permute-start.4
  69.8 2.2 %hold_rows.1.rows = bf16[2,8,256,512]{3,2,1,0:T(8,128)(2,1)S(1)} custom-call(bf16[2,8,256,512]{3,2,1,0:T(8,128)(2,1)} %refs_0_.5), custom_call_target="tpu_custom_call" | custom-call | tf_op jit(solution)/shard_map/hold_rows/pallas_call | solution.py:52
  72.0 1.5 %collective-permute-done.4.refs_5_ = bf16[2,8,48,512]{3,2,1,0:T(8,128)(2,1)S(1)} collective-permute-done((bf16[2,8,48,512]{3,2,1,0:T(8,128)(2,1)}, bf16[2,8,48,512]{3,2,1,0:T(8,128)(2,1)S(1)}, u32[]{:S(2)}, u32[]{:S(2)}) %collective-permute-start.4) | collective-permute-done | bytes 786464 | tf_op jit(solution)/shard_map/ppermute | solution.py:235
  73.5 3.9 %pair_products.3 = (f32[3,48,128]{2,1,0:T(8,128)S(1)}, f32[3,48,128]{2,1,0:T(8,128)S(1)}, f32[3,48,128]{2,1,0:T(8,128)S(1)}, f32[3,48,128]{2,1,0:T(8,128)S(1)}) custom-call(s32[13]{0:T(128)S(1)} %pad_add_fusion.places, f32[8,128]{1,0:T(8,128)S(1)} %mark.3.unread, bf16[2,8,256,512]{3,2,1,0:T(8,128)(2,1)S(1)} %hold_rows.1.rows, ...), custom_call_target="tpu_custom_call" | custom-call | bytes 1048576 | tf_op jit(solution)/shard_map/pair_products/pallas_call | solution.py:143
  77.4 1.9 %collective-permute-start.13 = (bf16[2,8,112,512]{3,2,1,0:T(8,128)(2,1)S(1)}, bf16[2,8,112,512]{3,2,1,0:T(8,128)(2,1)S(1)}, u32[]{:S(2)}, u32[]{:S(2)}) collective-permute-start(bf16[2,8,112,512]{3,2,1,0:T(8,128)(2,1)S(1)} %get-tuple-element.52.value), channel_id=1, source_target_pairs={{0,8},{8,0},{28,12},{16,24},{24,16},{12,28},{1,9},{9,1},{29,13},{1... | collective-permute-start | bytes 5505032 | tf_op jit(solution)/shard_map/ppermute | solution.py:233
  79.4 2.1 %collective-permute-start.5 = (f32[3,48,128]{2,1,0:T(8,128)S(1)}, f32[3,48,128]{2,1,0:T(8,128)S(1)}, u32[]{:S(2)}, u32[]{:S(2)}) collective-permute-start(f32[3,48,128]{2,1,0:T(8,128)S(1)} %get-tuple-element.40), channel_id=1, source_target_pairs={{0,1},{1,2},{2,3},{3,0},{4,5},{5,6},{6,7},{7,4},{8,9},{9,10},{10,1... | collective-permute-start | bytes 221192 | tf_op jit(solution)/shard_map/ppermute | solution.py:244
  81.5 3.8 %collective-permute-done.8.refs_4_ = bf16[2,8,96,512]{3,2,1,0:T(8,128)(2,1)} collective-permute-done((bf16[2,8,96,512]{3,2,1,0:T(8,128)(2,1)}, bf16[2,8,96,512]{3,2,1,0:T(8,128)(2,1)}, u32[]{:S(2)}, u32[]{:S(2)}) %collective-permute-start.8) | collective-permute-done | bytes 1572896 | tf_op jit(solution)/shard_map/ppermute | solution.py:233
  85.9 1.4 %collective-permute-start.9 = (bf16[2,8,96,512]{3,2,1,0:T(8,128)(2,1)}, bf16[2,8,96,512]{3,2,1,0:T(8,128)(2,1)S(1)}, u32[]{:S(2)}, u32[]{:S(2)}) collective-permute-start(bf16[2,8,96,512]{3,2,1,0:T(8,128)(2,1)} %collective-permute-done.8.refs_4_), channel_id=1, source_target_pairs={{0,4},{8,12},{16,20},{24,28},{1,5},{9,13},{17,21},{25,29},{2,6},{1... | collective-permute-start | bytes 4718600 | tf_op jit(solution)/shard_map/ppermute | solution.py:235
  87.3 2.6 %collective-permute-start.6 = (f32[3,48,128]{2,1,0:T(8,128)S(1)}, f32[3,48,128]{2,1,0:T(8,128)S(1)}, u32[]{:S(2)}, u32[]{:S(2)}) collective-permute-start(f32[3,48,128]{2,1,0:T(8,128)S(1)} %get-tuple-element.41), channel_id=1, source_target_pairs={{0,2},{1,3},{2,0},{3,1},{4,6},{5,7},{6,4},{7,5},{8,10},{9,11},{10,... | collective-permute-start | bytes 221192 | tf_op jit(solution)/shard_map/ppermute | solution.py:244
  89.9 1.3 %collective-permute-start.7 = (f32[3,48,128]{2,1,0:T(8,128)S(1)}, f32[3,48,128]{2,1,0:T(8,128)S(1)}, u32[]{:S(2)}, u32[]{:S(2)}) collective-permute-start(f32[3,48,128]{2,1,0:T(8,128)S(1)} %get-tuple-element.42), channel_id=1, source_target_pairs={{0,3},{1,0},{2,1},{3,2},{4,7},{5,4},{6,5},{7,6},{8,11},{9,8},{10,9... | collective-permute-start | bytes 221192 | tf_op jit(solution)/shard_map/ppermute | solution.py:244
  91.2 4.3 %pair_products.4 = (f32[3,96,128]{2,1,0:T(8,128)S(1)}, f32[3,96,128]{2,1,0:T(8,128)S(1)}, f32[3,96,128]{2,1,0:T(8,128)S(1)}, f32[3,96,128]{2,1,0:T(8,128)S(1)}) custom-call(s32[13]{0:T(128)S(1)} %pad_add_fusion.places, f32[8,128]{1,0:T(8,128)S(1)} %mark.4.unread, bf16[2,8,256,512]{3,2,1,0:T(8,128)(2,1)S(1)} %hold_rows.1.rows, ...), custom_call_target="tpu_custom_call" | custom-call | bytes 1048576 | tf_op jit(solution)/shard_map/pair_products/pallas_call | solution.py:143
  95.5 0.8 collective-permute-start.10
  96.3 6.2 %collective-permute-done.10.refs_5_ = f32[3,96,128]{2,1,0:T(8,128)S(1)} collective-permute-done((f32[3,96,128]{2,1,0:T(8,128)S(1)}, f32[3,96,128]{2,1,0:T(8,128)S(1)}, u32[]{:S(2)}, u32[]{:S(2)}) %collective-permute-start.10) | collective-permute-done | bytes 147488 | tf_op jit(solution)/shard_map/ppermute | solution.py:244
  102.5 2.4 %collective-permute-done.13.refs_4_ = bf16[2,8,112,512]{3,2,1,0:T(8,128)(2,1)S(1)} collective-permute-done((bf16[2,8,112,512]{3,2,1,0:T(8,128)(2,1)S(1)}, bf16[2,8,112,512]{3,2,1,0:T(8,128)(2,1)S(1)}, u32[]{:S(2)}, u32[]{:S(2)}) %collective-permute-start.13) | collective-permute-done | bytes 1835040 | tf_op jit(solution)/shard_map/ppermute | solution.py:233
  104.9 1.4 %collective-permute-start.14 = (bf16[2,8,112,512]{3,2,1,0:T(8,128)(2,1)S(1)}, bf16[2,8,112,512]{3,2,1,0:T(8,128)(2,1)S(1)}, u32[]{:S(2)}, u32[]{:S(2)}) collective-permute-start(bf16[2,8,112,512]{3,2,1,0:T(8,128)(2,1)S(1)} %collective-permute-done.13.refs_4_), channel_id=1, source_target_pairs={{0,4},{8,12},{16,20},{24,28},{1,5},{9,13},{17,21},{25,29},{2,6},{1... | collective-permute-start | bytes 5505032 | tf_op jit(solution)/shard_map/ppermute | solution.py:235
  106.3 4.1 %collective-permute-start.12 = (f32[3,96,128]{2,1,0:T(8,128)S(1)}, f32[3,96,128]{2,1,0:T(8,128)S(1)}, u32[]{:S(2)}, u32[]{:S(2)}) collective-permute-start(f32[3,96,128]{2,1,0:T(8,128)S(1)} %get-tuple-element.51), channel_id=1, source_target_pairs={{0,3},{1,0},{2,1},{3,2},{4,7},{5,4},{6,5},{7,6},{8,11},{9,8},{10,9... | collective-permute-start | bytes 442376 | tf_op jit(solution)/shard_map/ppermute | solution.py:244
  110.4 5.0 %pair_products.5 = (f32[3,112,128]{2,1,0:T(8,128)S(1)}, f32[3,112,128]{2,1,0:T(8,128)S(1)}, f32[3,112,128]{2,1,0:T(8,128)S(1)}, f32[3,112,128]{2,1,0:T(8,128)S(1)}) custom-call(s32[13]{0:T(128)S(1)} %pad_add_fusion.places, f32[8,128]{1,0:T(8,128)S(1)} %mark.5.unread, bf16[2,8,256,512]{3,2,1,0:T(8,128)(2,1)S(1)} %hold_rows.1.rows, ...), custom_call_target="tpu_custom_call" | custom-call | bytes 1048576 | tf_op jit(solution)/shard_map/pair_products/pallas_call | solution.py:143
  115.5 1.7 %collective-permute-done.11.refs_6_ = f32[3,96,128]{2,1,0:T(8,128)S(1)} collective-permute-done((f32[3,96,128]{2,1,0:T(8,128)S(1)}, f32[3,96,128]{2,1,0:T(8,128)S(1)}, u32[]{:S(2)}, u32[]{:S(2)}) %collective-permute-start.11) | collective-permute-done | bytes 147488 | tf_op jit(solution)/shard_map/ppermute | solution.py:244
  117.2 2.9 %collective-permute-start.17 = (f32[3,112,128]{2,1,0:T(8,128)S(1)}, f32[3,112,128]{2,1,0:T(8,128)S(1)}, u32[]{:S(2)}, u32[]{:S(2)}) collective-permute-start(f32[3,112,128]{2,1,0:T(8,128)S(1)} %get-tuple-element.60), channel_id=1, source_target_pairs={{0,3},{1,0},{2,1},{3,2},{4,7},{5,4},{6,5},{7,6},{8,11},{9,8},{10,9... | collective-permute-start | bytes 516104 | tf_op jit(solution)/shard_map/ppermute | solution.py:244
  120.7 4.3 %collective-permute-done.17.refs_11_ = f32[3,112,128]{2,1,0:T(8,128)S(1)} collective-permute-done((f32[3,112,128]{2,1,0:T(8,128)S(1)}, f32[3,112,128]{2,1,0:T(8,128)S(1)}, u32[]{:S(2)}, u32[]{:S(2)}) %collective-permute-start.17) | collective-permute-done | bytes 172064 | tf_op jit(solution)/shard_map/ppermute | solution.py:244
  124.9 8.3 %collective-permute-done.16.refs_10_ = f32[3,112,128]{2,1,0:T(8,128)S(1)} collective-permute-done((f32[3,112,128]{2,1,0:T(8,128)S(1)}, f32[3,112,128]{2,1,0:T(8,128)S(1)}, u32[]{:S(2)}, u32[]{:S(2)}) %collective-permute-start.16) | collective-permute-done | bytes 172064 | tf_op jit(solution)/shard_map/ppermute | solution.py:244
  133.2 0.9 sum_terms.1
  (19 shorter events, 1.4 us)
Async XLA Ops:
  0.0 51.7 %collective-permute-start = (bf16[2,8,256,512]{3,2,1,0:T(8,128)(2,1)}, bf16[2,8,256,512]{3,2,1,0:T(8,128)(2,1)}, u32[]{:S(2)}, u32[]{:S(2)}) collective-permute-start(bf16[2,8,256,512]{3,2,1,0:T(8,128)(2,1)} %refs_0_.5), channel_id=1, source_target_pairs={{16,0},{12,4},{20,12},{0,16},{28,20},{4,28},{17,1},{13,5},{21,13},... | collective-permute-start | bytes 12582920 | tf_op jit(solution)/shard_map/ppermute | solution.py:219
  5.9 45.8 %collective-permute-start.1 = (bf16[2,8,256,512]{3,2,1,0:T(8,128)(2,1)}, bf16[2,8,256,512]{3,2,1,0:T(8,128)(2,1)}, u32[]{:S(2)}, u32[]{:S(2)}) collective-permute-start(bf16[2,8,256,512]{3,2,1,0:T(8,128)(2,1)} %refs_0_.5), channel_id=1, source_target_pairs={{4,0},{12,8},{20,16},{28,24},{8,12},{24,28},{5,1},{13,9},{21,17},{... | collective-permute-start | bytes 12582920 | tf_op jit(solution)/shard_map/ppermute | solution.py:222
  54.3 14.2 %collective-permute-start.3 = (bf16[2,8,48,512]{3,2,1,0:T(8,128)(2,1)}, bf16[2,8,48,512]{3,2,1,0:T(8,128)(2,1)}, u32[]{:S(2)}, u32[]{:S(2)}) collective-permute-start(bf16[2,8,48,512]{3,2,1,0:T(8,128)(2,1)} %fusion), channel_id=1, source_target_pairs={{0,8},{8,0},{28,12},{16,24},{24,16},{12,28},{1,9},{9,1},{29,13},{1... | collective-permute-start | bytes 2359304 | tf_op jit(solution)/shard_map/ppermute | solution.py:233
  59.6 25.8 %collective-permute-start.8 = (bf16[2,8,96,512]{3,2,1,0:T(8,128)(2,1)}, bf16[2,8,96,512]{3,2,1,0:T(8,128)(2,1)}, u32[]{:S(2)}, u32[]{:S(2)}) collective-permute-start(bf16[2,8,96,512]{3,2,1,0:T(8,128)(2,1)} %get-tuple-element.43), channel_id=1, source_target_pairs={{0,8},{8,0},{28,12},{16,24},{24,16},{12,28},{1,9},{9,1},{29,13},{1... | collective-permute-start | bytes 4718600 | tf_op jit(solution)/shard_map/ppermute | solution.py:233
  63.5 10.0 %collective-permute-start.2 = (bf16[2,8,256,512]{3,2,1,0:T(8,128)(2,1)}, bf16[2,8,256,512]{3,2,1,0:T(8,128)(2,1)}, u32[]{:S(2)}, u32[]{:S(2)}) collective-permute-start(bf16[2,8,256,512]{3,2,1,0:T(8,128)(2,1)} %collective-permute-done.refs_0_.refs_2_), channel_id=1, source_target_pairs={{4,0},{12,8},{20,16},{28,24},{0,4},{16,20},{5,1},{13,9},{21,17},{2... | collective-permute-start | bytes 12582920 | tf_op jit(solution)/shard_map/ppermute | solution.py:223
  68.5 5.1 %collective-permute-start.4 = (bf16[2,8,48,512]{3,2,1,0:T(8,128)(2,1)}, bf16[2,8,48,512]{3,2,1,0:T(8,128)(2,1)S(1)}, u32[]{:S(2)}, u32[]{:S(2)}) collective-permute-start(bf16[2,8,48,512]{3,2,1,0:T(8,128)(2,1)} %collective-permute-done.3.refs_4_), channel_id=1, source_target_pairs={{0,4},{8,12},{16,20},{24,28},{1,5},{9,13},{17,21},{25,29},{2,6},{1... | collective-permute-start | bytes 2359304 | tf_op jit(solution)/shard_map/ppermute | solution.py:235
  77.4 27.5 %collective-permute-start.13 = (bf16[2,8,112,512]{3,2,1,0:T(8,128)(2,1)S(1)}, bf16[2,8,112,512]{3,2,1,0:T(8,128)(2,1)S(1)}, u32[]{:S(2)}, u32[]{:S(2)}) collective-permute-start(bf16[2,8,112,512]{3,2,1,0:T(8,128)(2,1)S(1)} %get-tuple-element.52.value), channel_id=1, source_target_pairs={{0,8},{8,0},{28,12},{16,24},{24,16},{12,28},{1,9},{9,1},{29,13},{1... | collective-permute-start | bytes 5505032 | tf_op jit(solution)/shard_map/ppermute | solution.py:233
  79.4 6.5 %collective-permute-start.5 = (f32[3,48,128]{2,1,0:T(8,128)S(1)}, f32[3,48,128]{2,1,0:T(8,128)S(1)}, u32[]{:S(2)}, u32[]{:S(2)}) collective-permute-start(f32[3,48,128]{2,1,0:T(8,128)S(1)} %get-tuple-element.40), channel_id=1, source_target_pairs={{0,1},{1,2},{2,3},{3,0},{4,5},{5,6},{6,7},{7,4},{8,9},{9,10},{10,1... | collective-permute-start | bytes 221192 | tf_op jit(solution)/shard_map/ppermute | solution.py:244
  85.9 5.3 %collective-permute-start.9 = (bf16[2,8,96,512]{3,2,1,0:T(8,128)(2,1)}, bf16[2,8,96,512]{3,2,1,0:T(8,128)(2,1)S(1)}, u32[]{:S(2)}, u32[]{:S(2)}) collective-permute-start(bf16[2,8,96,512]{3,2,1,0:T(8,128)(2,1)} %collective-permute-done.8.refs_4_), channel_id=1, source_target_pairs={{0,4},{8,12},{16,20},{24,28},{1,5},{9,13},{17,21},{25,29},{2,6},{1... | collective-permute-start | bytes 4718600 | tf_op jit(solution)/shard_map/ppermute | solution.py:235
  87.3 8.2 %collective-permute-start.6 = (f32[3,48,128]{2,1,0:T(8,128)S(1)}, f32[3,48,128]{2,1,0:T(8,128)S(1)}, u32[]{:S(2)}, u32[]{:S(2)}) collective-permute-start(f32[3,48,128]{2,1,0:T(8,128)S(1)} %get-tuple-element.41), channel_id=1, source_target_pairs={{0,2},{1,3},{2,0},{3,1},{4,6},{5,7},{6,4},{7,5},{8,10},{9,11},{10,... | collective-permute-start | bytes 221192 | tf_op jit(solution)/shard_map/ppermute | solution.py:244
  89.9 5.6 %collective-permute-start.7 = (f32[3,48,128]{2,1,0:T(8,128)S(1)}, f32[3,48,128]{2,1,0:T(8,128)S(1)}, u32[]{:S(2)}, u32[]{:S(2)}) collective-permute-start(f32[3,48,128]{2,1,0:T(8,128)S(1)} %get-tuple-element.42), channel_id=1, source_target_pairs={{0,3},{1,0},{2,1},{3,2},{4,7},{5,4},{6,5},{7,6},{8,11},{9,8},{10,9... | collective-permute-start | bytes 221192 | tf_op jit(solution)/shard_map/ppermute | solution.py:244
  95.5 7.0 %collective-permute-start.10 = (f32[3,96,128]{2,1,0:T(8,128)S(1)}, f32[3,96,128]{2,1,0:T(8,128)S(1)}, u32[]{:S(2)}, u32[]{:S(2)}) collective-permute-start(f32[3,96,128]{2,1,0:T(8,128)S(1)} %get-tuple-element.47), channel_id=1, source_target_pairs={{0,1},{1,2},{2,3},{3,0},{4,5},{5,6},{6,7},{7,4},{8,9},{9,10},{10,1... | collective-permute-start | bytes 442376 | tf_op jit(solution)/shard_map/ppermute | solution.py:244
  104.9 5.6 %collective-permute-start.14 = (bf16[2,8,112,512]{3,2,1,0:T(8,128)(2,1)S(1)}, bf16[2,8,112,512]{3,2,1,0:T(8,128)(2,1)S(1)}, u32[]{:S(2)}, u32[]{:S(2)}) collective-permute-start(bf16[2,8,112,512]{3,2,1,0:T(8,128)(2,1)S(1)} %collective-permute-done.13.refs_4_), channel_id=1, source_target_pairs={{0,4},{8,12},{16,20},{24,28},{1,5},{9,13},{17,21},{25,29},{2,6},{1... | collective-permute-start | bytes 5505032 | tf_op jit(solution)/shard_map/ppermute | solution.py:235
  106.3 9.2 %collective-permute-start.12 = (f32[3,96,128]{2,1,0:T(8,128)S(1)}, f32[3,96,128]{2,1,0:T(8,128)S(1)}, u32[]{:S(2)}, u32[]{:S(2)}) collective-permute-start(f32[3,96,128]{2,1,0:T(8,128)S(1)} %get-tuple-element.51), channel_id=1, source_target_pairs={{0,3},{1,0},{2,1},{3,2},{4,7},{5,4},{6,5},{7,6},{8,11},{9,8},{10,9... | collective-permute-start | bytes 442376 | tf_op jit(solution)/shard_map/ppermute | solution.py:244
  110.4 6.7 %collective-permute-start.11 = (f32[3,96,128]{2,1,0:T(8,128)S(1)}, f32[3,96,128]{2,1,0:T(8,128)S(1)}, u32[]{:S(2)}, u32[]{:S(2)}) collective-permute-start(f32[3,96,128]{2,1,0:T(8,128)S(1)} %get-tuple-element.49), channel_id=1, source_target_pairs={{0,2},{1,3},{2,0},{3,1},{4,6},{5,7},{6,4},{7,5},{8,10},{9,11},{10,... | collective-permute-start | bytes 442376 | tf_op jit(solution)/shard_map/ppermute | solution.py:244
  117.2 7.8 %collective-permute-start.17 = (f32[3,112,128]{2,1,0:T(8,128)S(1)}, f32[3,112,128]{2,1,0:T(8,128)S(1)}, u32[]{:S(2)}, u32[]{:S(2)}) collective-permute-start(f32[3,112,128]{2,1,0:T(8,128)S(1)} %get-tuple-element.60), channel_id=1, source_target_pairs={{0,3},{1,0},{2,1},{3,2},{4,7},{5,4},{6,5},{7,6},{8,11},{9,8},{10,9... | collective-permute-start | bytes 516104 | tf_op jit(solution)/shard_map/ppermute | solution.py:244
  120.1 13.1 %collective-permute-start.16 = (f32[3,112,128]{2,1,0:T(8,128)S(1)}, f32[3,112,128]{2,1,0:T(8,128)S(1)}, u32[]{:S(2)}, u32[]{:S(2)}) collective-permute-start(f32[3,112,128]{2,1,0:T(8,128)S(1)} %get-tuple-element.58), channel_id=1, source_target_pairs={{0,2},{1,3},{2,0},{3,1},{4,6},{5,7},{6,4},{7,5},{8,10},{9,11},{10,... | collective-permute-start | bytes 516104 | tf_op jit(solution)/shard_map/ppermute | solution.py:244
  120.1 13.1 %collective-permute-start.15 = (f32[3,112,128]{2,1,0:T(8,128)S(1)}, f32[3,112,128]{2,1,0:T(8,128)S(1)}, u32[]{:S(2)}, u32[]{:S(2)}) collective-permute-start(f32[3,112,128]{2,1,0:T(8,128)S(1)} %get-tuple-element.56), channel_id=1, source_target_pairs={{0,1},{1,2},{2,3},{3,0},{4,5},{5,6},{6,7},{7,4},{8,9},{9,10},{10,1... | collective-permute-start | bytes 516104 | tf_op jit(solution)/shard_map/ppermute | solution.py:244
